TPU v7x, 512 devices: a whole 4x4x16 slice. The times are simulated.
512 devices in a mesh: row: 32 (over y, x, core), col: 16 (over z).
Axes of the slice: x: 4, y: 4, z: 16, core: 2. Of those that a mesh axis runs over, the one named last changes fastest.
Arguments:
- tokens: float32 [512, 6144], P('row', 'col'), may hold values from -6 to 6
- weight_in: float32 [6144, 12288], P('col', 'row'), may hold values from -0.078125 to 0.078125
- weight_out: float32 [12288, 6144], P('row', 'col'), may hold values from -0.0546875 to 0.0546875
- cotangent: float32 [512, 6144], P('row', 'col'), may hold values from -1.5 to 1.5
Outputs:
- output: float32 [512, 6144], P('row', 'col')
- input_grad: float32 [512, 6144], P('row', 'col')
- weight_in_grad: float32 [6144, 12288], P('col', 'row')
- weight_out_grad: float32 [12288, 6144], P('row', 'col')
All inputs are finite; a program needn't handle non-finite values.
Results may differ from a plain program's by a relative error of at most 0.00012.
Values sent between devices are 32-bit elements; how exact they have to be, the bound alone decides.
No kernel may reach another device: no remote copies, remote signals or barrier semaphores. Data moves between devices by JAX's collectives and lax.ppermute only.
A program may use at most 64 MiB of HBM per device.

v0:
```python
import math

import jax
import jax.numpy as jnp
from jax import lax
from jax.sharding import PartitionSpec as P


def product(left, right):
    return jnp.dot(left, right, precision=lax.Precision.HIGHEST, preferred_element_type=jnp.float32)


def contract_rows(left, right):
    return lax.dot_general(
        left,
        right,
        (((0,), (0,)), ((), ())),
        precision=lax.Precision.HIGHEST,
        preferred_element_type=jnp.float32,
    )


def contract_cols(left, right):
    return lax.dot_general(
        left,
        right,
        (((1,), (1,)), ((), ())),
        precision=lax.Precision.HIGHEST,
        preferred_element_type=jnp.float32,
    )


def gelu_value(pre):
    return pre * 0.5 * (1.0 + jax.scipy.special.erf(pre / math.sqrt(2.0)))


def gelu_slope(pre):
    cumulative = 0.5 * (1.0 + jax.scipy.special.erf(pre / math.sqrt(2.0)))
    density = jnp.exp(-0.5 * pre * pre) / math.sqrt(2.0 * math.pi)
    return cumulative + pre * density


def local(tokens, weight_in, weight_out, cotangent):
    token_all = lax.all_gather(tokens, "row", axis=0, tiled=True)
    cotangent_all = lax.all_gather(cotangent, "row", axis=0, tiled=True)
    pre_share = lax.psum_scatter(
        product(token_all, weight_in), "col", scatter_dimension=0, tiled=True
    )
    act_all = lax.all_gather(gelu_value(pre_share), "col", axis=0, tiled=True)
    grad_share = lax.psum_scatter(
        contract_cols(cotangent_all, weight_out), "col", scatter_dimension=0, tiled=True
    )
    pre_grad_all = lax.all_gather(grad_share * gelu_slope(pre_share), "col", axis=0, tiled=True)
    output = lax.psum_scatter(product(act_all, weight_out), "row", scatter_dimension=0, tiled=True)
    weight_out_grad = contract_rows(act_all, cotangent_all)
    input_grad = lax.psum_scatter(
        contract_cols(pre_grad_all, weight_in), "row", scatter_dimension=0, tiled=True
    )
    weight_in_grad = contract_rows(token_all, pre_grad_all)
    return (output, input_grad, weight_in_grad, weight_out_grad)


def solution(mesh):
    placed = (P("row", "col"), P("col", "row"), P("row", "col"), P("row", "col"))
    return jax.shard_map(
        local,
        mesh=mesh,
        in_specs=placed,
        out_specs=(P("row", "col"), P("row", "col"), P("col", "row"), P("row", "col")),
        check_vma=False,
    )
```

profile of v0, /device:TPU:6, one launch (start us, length us, event | category | flops | bytes accessed | tf_op | source)
XLA Modules:
  0.0 424.9 jit_solution(13108197438664471)
XLA Ops:
  7.2 0.0 copy-start
  7.2 0.0 copy-start.3
  7.2 0.0 reduce-scatter.9.cloned.1.call-start
  7.2 27.8 %all_gather.14 = f32[512,384]{1,0:T(8,128)S(1)} all-gather(f32[16,384]{1,0:T(8,128)} %param.7), channel_id=1, replica_groups=mesh['row'=32,'col'=16] {'row'}, dimensions={0}, use_global_device_ids=true | all-gather | bytes 811008 | tf_op jit(solution)/shard_map/all_gather | solution.py:45
  35.0 0.0 copy-done.3
  35.0 2.5 fusion.7
  37.5 0.0 copy-start.4
  37.5 0.0 reduce-scatter.9.cloned.1.call-update
  37.6 0.0 reduce-scatter.5.cloned.1.call-start
  37.6 0.7 copy-done.4
  38.3 22.5 %all_gather.12 = f32[512,384]{1,0:T(8,128)S(1)} all-gather(f32[16,384]{1,0:T(8,128)S(1)} %copy-done.4), channel_id=1, replica_groups=mesh['row'=32,'col'=16] {'row'}, dimensions={0}, use_global_device_ids=true | all-gather | bytes 811008 | tf_op jit(solution)/shard_map/all_gather | solution.py:44
  60.8 0.0 copy-done
  60.8 2.5 fusion.5
  63.3 0.0 reduce-scatter.5.cloned.1.call-update
  63.3 0.0 reduce-scatter.11.cloned.1.call-start
  63.4 43.9 %reduce-scatter.9.cloned.1.call-done = f32[32,384]{1,0:T(8,128)} async-done(((f32[512,384]{1,0:T(8,128)}), f32[32,384]{1,0:T(8,128)}) %reduce-scatter.9.cloned.1.call-update) | async-done | bytes 49168 | tf_op jit(solution)/shard_map/reduce_scatter | solution.py:50
  107.3 70.8 %reduce-scatter.5.cloned.1.call-done = f32[32,384]{1,0:T(8,128)} async-done(((f32[512,384]{1,0:T(8,128)}), f32[32,384]{1,0:T(8,128)}) %reduce-scatter.5.cloned.1.call-update) | async-done | bytes 49168 | tf_op jit(solution)/shard_map/reduce_scatter | solution.py:46
  178.1 1.5 fusion.4
  179.5 32.2 %all_gather.15 = f32[512,384]{1,0:T(8,128)S(1)} all-gather(f32[32,384]{1,0:T(8,128)S(1)} %get-tuple-element.8), channel_id=1, replica_groups=mesh['row'=32,'col'=16] {'col'}, dimensions={0}, use_global_device_ids=true | all-gather | bytes 835584 | tf_op jit(solution)/shard_map/all_gather | solution.py:53
  211.7 2.5 fusion.8
  214.2 0.0 reduce-scatter.11.cloned.1.call-update
  214.3 0.0 reduce-scatter.7.cloned.1.call-start
  214.3 32.0 %all_gather.13 = f32[512,384]{1,0:T(8,128)S(1)} all-gather(f32[32,384]{1,0:T(8,128)} %get-tuple-element.9), channel_id=1, replica_groups=mesh['row'=32,'col'=16] {'col'}, dimensions={0}, use_global_device_ids=true | all-gather | bytes 835584 | tf_op jit(solution)/shard_map/all_gather | solution.py:49
  246.4 0.0 copy-start.1
  246.4 0.9 copy-done.1
  247.2 2.5 fusion.6
  249.8 0.0 reduce-scatter.7.cloned.1.call-update
  249.8 1.4 convolution_bitcast_fusion
  251.2 0.0 copy-start.2
  251.2 1.1 copy.8
  252.3 0.1 copy-done.2
  252.4 2.3 fusion.9
  254.6 59.0 %reduce-scatter.11.cloned.1.call-done = f32[16,384]{1,0:T(8,128)} async-done(((f32[512,384]{1,0:T(8,128)}), f32[16,384]{1,0:T(8,128)}) %reduce-scatter.11.cloned.1.call-update) | async-done | bytes 24592 | tf_op jit(solution)/shard_map/reduce_scatter | solution.py:56
  313.6 104.7 %reduce-scatter.7.cloned.1.call-done = f32[16,384]{1,0:T(8,128)} async-done(((f32[512,384]{1,0:T(8,128)}), f32[16,384]{1,0:T(8,128)}) %reduce-scatter.7.cloned.1.call-update) | async-done | bytes 24592 | tf_op jit(solution)/shard_map/reduce_scatter | solution.py:54
Async XLA Ops:
  7.2 53.6 %copy-start = (f32[384,384]{1,0:T(8,128)S(1)}, f32[384,384]{1,0:T(8,128)}, u32[]{:S(2)}) copy-start(f32[384,384]{1,0:T(8,128)} %param.5) | copy-start | bytes 1769476
  7.2 27.9 %copy-start.3 = (f32[384,384]{1,0:T(8,128)S(1)}, f32[384,384]{1,0:T(8,128)}, u32[]{:S(2)}) copy-start(f32[384,384]{1,0:T(8,128)} %param.6) | copy-start | bytes 1769476
  7.2 100.1 %reduce-scatter.9.cloned.1.call-start = ((), (), s32[]{:S(2)}) async-start(), calls=%async_computation.6 | async-start | bytes 835584 | tf_op jit(solution)/shard_map/reduce_scatter | solution.py:50
  37.5 0.7 copy-start.4
  37.6 140.5 %reduce-scatter.5.cloned.1.call-start = ((), (), s32[]{:S(2)}) async-start(), calls=%async_computation.4 | async-start | bytes 835584 | tf_op jit(solution)/shard_map/reduce_scatter | solution.py:46
  63.3 250.3 %reduce-scatter.11.cloned.1.call-start = ((), (), s32[]{:S(2)}) async-start(), calls=%async_computation.7 | async-start | bytes 811008 | tf_op jit(solution)/shard_map/reduce_scatter | solution.py:56
  214.3 204.1 %reduce-scatter.7.cloned.1.call-start = ((), (), s32[]{:S(2)}) async-start(), calls=%async_computation.5 | async-start | bytes 811008 | tf_op jit(solution)/shard_map/reduce_scatter | solution.py:54
  246.4 0.9 copy-start.1
  251.2 1.1 copy-start.2
Sparse Core Ops, SparseCore 0:
  37.7 69.5 reduce-scatter.8
  110.3 67.6 reduce-scatter.4
  214.4 99.1 reduce-scatter.10
  318.4 99.9 reduce-scatter.6
where the time goes:
time: 425 us
  waiting for transfers between devices  278 us (65%)
  blocking collectives  115 us (27%)
  between operations  13.8 us (3%)
  matrix products  13.7 us (3%)
    reduce_scatter x1, waiting for transfers between devices, local(): lax.psum_scatter(product(act_all, weight_out), 'row', scatter_dimension=0...  105 us
    reduce_scatter x1, waiting for transfers between devices, local(): lax.psum_scatter(product(token_all, weight_in), 'col', scatter_dimension=...  70.8 us
    reduce_scatter x1, waiting for transfers between devices, local(): lax.psum_scatter(contract_cols(pre_grad_all, weight_in), 'row', scatter_d...  59 us
    reduce_scatter x1, waiting for transfers between devices, local(): lax.psum_scatter(contract_cols(cotangent_all, weight_out), 'col', scatter...  43.9 us
    all_gather x1, blocking collectives, local(): lax.all_gather(grad_share * gelu_slope(pre_share), 'col', axis=0, tiled=T...  32.2 us
    all_gather x1, blocking collectives, local(): act_all = lax.all_gather(gelu_value(pre_share), 'col', axis=0, tiled=True)  32 us
    all_gather x1, blocking collectives, local(): cotangent_all = lax.all_gather(cotangent, 'row', axis=0, tiled=True)  27.8 us
    all_gather x1, blocking collectives, local(): token_all = lax.all_gather(tokens, 'row', axis=0, tiled=True)  22.5 us
  transfers between devices with their start and end apart: 4, of which 4 were waited for; matrix products, arithmetic and copies ran while one was open for 2% of the time, Pallas kernels for 0%

commit v1 on v0

v1 whole, which is shorter than its diff:
```python
import math

import jax
import jax.numpy as jnp
from jax import lax
from jax.sharding import PartitionSpec as P

BOTH = ("row", "col")
HIGH = lax.Precision.HIGH


def dot(left, right, dims):
    return lax.dot_general(left, right, (dims, ((), ())), precision=HIGH, preferred_element_type=jnp.float32)


def gelu_value(pre):
    return pre * 0.5 * (1.0 + jax.scipy.special.erf(pre / math.sqrt(2.0)))


def gelu_slope(pre):
    cumulative = 0.5 * (1.0 + jax.scipy.special.erf(pre / math.sqrt(2.0)))
    density = jnp.exp(-0.5 * pre * pre) / math.sqrt(2.0 * math.pi)
    return cumulative + pre * density


class Plan:
    def __init__(self, rows, cols):
        self.rows, self.cols = rows, cols
        self.ring = cols // 2
        self.steps = self.ring // 2

    def flat(self, row, col):
        return row * self.cols + col

    def partner(self, core, col):
        return (col + (1 if (col + core) % 2 == 0 else -1)) % self.cols

    def peer(self, step, core, place):
        if (step + core) % 2 == 0:
            return place ^ 1
        return (place + 1) % self.ring if place % 2 else (place - 1) % self.ring

    def received(self, step, core, place):
        peer = self.peer(step, core, place)
        if step == 0:
            return [peer]
        if step == 1:
            return self.received(0, core, peer) + [peer]
        return self.received(step - 1, core, peer)

    def own_order(self, core, col):
        place = col // 2
        order = []
        for step in reversed(range(self.steps)):
            order += self.received(step, core, place)
        return [2 * k + col % 2 for k in order + [place]]

    def order(self, core, col):
        return self.own_order(core, self.partner(core, col)) + self.own_order(core, col)

    def chip_groups(self):
        return [
            [self.flat(2 * k + core, col) for k in self.order(core, col)]
            for col in range(self.cols)
            for core in range(2)
        ]

    def neighbour_perm(self):
        return [
            (self.flat(row, col), self.flat(row, self.partner(row % 2, col)))
            for row in range(self.rows)
            for col in range(self.cols)
        ]

    def ring_groups(self, step):
        groups = []
        for row in range(self.rows):
            core = row % 2
            for col in range(self.cols):
                place = col // 2
                if place % 2 == (step + core) % 2:
                    peer = self.peer(step, core, place)
                    groups.append([self.flat(row, col), self.flat(row, 2 * peer + col % 2)])
        return groups


def solution(mesh):
    rows, cols = mesh.shape["row"], mesh.shape["col"]
    plan = Plan(rows, cols)
    half = cols // 2
    chip_groups = plan.chip_groups()
    neighbour_perm = plan.neighbour_perm()
    core_perm = [(row, row ^ 1) for row in range(rows)]

    def local(tokens, weight_in, weight_out, cotangent):
        n, d = tokens.shape
        h = weight_in.shape[1]
        turn = lax.axis_index("row") + (lax.axis_index("col") >> 1)

        def ring_swap(block, step):
            pair = lax.all_gather(block, BOTH, axis=0, axis_index_groups=plan.ring_groups(step))
            return jnp.where((turn + step) & 1 == 0, pair[1], pair[0])

        weight_in_other = lax.ppermute(weight_in, "row", core_perm)
        weight_out_other = lax.ppermute(weight_out, "row", core_perm)

        both = jnp.concatenate([tokens, cotangent], axis=0)
        sent = jnp.broadcast_to(both[None], (cols, 2 * n, d))
        gathered = lax.all_to_all(sent, BOTH, 0, 0, tiled=True, axis_index_groups=chip_groups)
        token_all = gathered[:, :n].reshape(cols * n, d)
        cotangent_all = gathered[:, n:].reshape(cols * n, d)
        cut = half * n

        w_in = jnp.concatenate([weight_in, weight_in_other], axis=1)
        w_out = jnp.concatenate([weight_out, weight_out_other], axis=0)

        pre_away = lax.ppermute(dot(token_all[:cut], w_in, ((1,), (0,))), BOTH, neighbour_perm)
        grad_away = lax.ppermute(dot(cotangent_all[:cut], w_out, ((1,), (1,))), BOTH, neighbour_perm)
        pre_sum = dot(token_all[cut:], w_in, ((1,), (0,))) + pre_away
        grad_sum = dot(cotangent_all[cut:], w_out, ((1,), (1,))) + grad_away
        sums = jnp.stack([pre_sum, grad_sum]).reshape(2, half, n, 2 * h)

        arrived = None
        at = 0
        for step in reversed(range(1, plan.steps)):
            part = sums[:, at : at + 2]
            at += 2
            arrived = ring_swap(part if arrived is None else part + arrived, step)
        last = sums[:, at : at + 1] + arrived[:, :1]
        mine = sums[:, at + 1 :] + arrived[:, 1:] + ring_swap(last, 0)

        pre, grad = mine[0], mine[1]
        own = jnp.stack([gelu_value(pre), grad * gelu_slope(pre)])
        blocks = [own]
        got = ring_swap(own, 0)
        blocks.insert(0, got)
        block = jnp.concatenate([got, own], axis=1)
        for step in range(1, plan.steps):
            block = ring_swap(block, step)
            blocks.insert(0, block)
        hidden = jnp.concatenate(blocks, axis=1).reshape(2, cut, 2 * h)
        act_here, slope_here = hidden[0], hidden[1]
        act_away = lax.ppermute(act_here, BOTH, neighbour_perm)
        slope_away = lax.ppermute(slope_here, BOTH, neighbour_perm)
        act_all = jnp.concatenate([act_away, act_here], axis=0)
        slope_all = jnp.concatenate([slope_away, slope_here], axis=0)

        out_part = dot(act_all, w_out, ((1,), (0,))).reshape(cols, n, d)
        in_part = dot(slope_all, w_in, ((1,), (1,))).reshape(cols, n, d)

        out_other = dot(act_all[:, h:], cotangent_all, ((0,), (0,)))
        in_other = dot(token_all, slope_all[:, h:], ((0,), (0,)))
        out_other = lax.ppermute(out_other, "row", core_perm)
        in_other = lax.ppermute(in_other, "row", core_perm)
        weight_out_grad = dot(act_all[:, :h], cotangent_all, ((0,), (0,))) + out_other
        weight_in_grad = dot(token_all, slope_all[:, :h], ((0,), (0,))) + in_other

        parts = jnp.concatenate([out_part, in_part], axis=1)
        parts = lax.all_to_all(parts, BOTH, 0, 0, tiled=True, axis_index_groups=chip_groups)
        total = jnp.sum(parts, axis=0)
        return (total[:n], total[n:], weight_in_grad, weight_out_grad)

    placed = (P("row", "col"), P("col", "row"), P("row", "col"), P("row", "col"))
    return jax.shard_map(
        local,
        mesh=mesh,
        in_specs=placed,
        out_specs=(P("row", "col"), P("row", "col"), P("col", "row"), P("row", "col")),
        check_vma=False,
    )
```

time: 425 us -> 169 us (0.40)
  waiting for transfers between devices: 278 us -> 17.8 us
  starting transfers between devices: 0.16 us -> 44 us
  blocking collectives: 115 us -> 81.8 us
  between operations: 13.8 us -> 1 us
    reduce_scatter x4 -> x0, waiting for transfers between devices: 278 us -> none  [the longest x1 105 us: local(): lax.psum_scatter(product(act_all, weight_out), 'row', scatter_dimension=0...]
    all_gather x4 -> x8, blocking collectives: 115 us -> 81.8 us  [ring_swap(): lax.all_gather(block, BOTH, axis=0, axis_index_groups=plan.ring_groups(st...]
    all_to_all x0 -> x2, starting transfers between devices: none -> 24.2 us  [the longest x1 13.2 us: local(): lax.all_to_all(parts, BOTH, 0, 0, tiled=True, axis_index_groups=chip_groups)]
    ppermute x0 -> x8, starting transfers between devices: none -> 19.8 us  [the longest x1 3.92 us: local(): act_away = lax.ppermute(act_here, BOTH, neighbour_perm)]
    ppermute x0 -> x8, waiting for transfers between devices: none -> 9.22 us  [the longest x1 3.73 us: local(): slope_away = lax.ppermute(slope_here, BOTH, neighbour_perm)]
    all_to_all x0 -> x2, waiting for transfers between devices: none -> 8.58 us  [the longest x1 5.74 us: local(): lax.all_to_all(parts, BOTH, 0, 0, tiled=True, axis_index_groups=chip_groups)]
    dot_general x6 -> x10, matrix products: 13.7 us -> 14.9 us  [dot(): lax.dot_general(left, right, (dims, ((), ())), precision=HIGH, preferred_...]
  transfers between devices with their start and end apart: 4 -> 10, of which waited for: 4 -> 6; matrix products, arithmetic and copies ran while one was open for 2% -> 11% of each run, Pallas kernels for 0% -> 0%
where the time goes in v1:
time: 169 us; the launch traced here: 167 us
  blocking collectives  81.8 us (48%)
  starting transfers between devices  44 us (26%)
  waiting for transfers between devices  17.8 us (11%)
  matrix products  14.9 us (9%)
  local copies, waits for them, and re-layouts  5.14 us (3%)
  other arithmetic  2.16 us (1%)
    all_gather x8, blocking collectives, ring_swap(): lax.all_gather(block, BOTH, axis=0, axis_index_groups=plan.ring_groups(st...  81.8 us
    dot_general x10, matrix products, dot(): lax.dot_general(left, right, (dims, ((), ())), precision=HIGH, preferred_...  14.9 us
    all_to_all x1, starting transfers between devices, local(): lax.all_to_all(parts, BOTH, 0, 0, tiled=True, axis_index_groups=chip_groups)  13.2 us
    all_to_all x1, starting transfers between devices, local(): lax.all_to_all(sent, BOTH, 0, 0, tiled=True, axis_index_groups=chip_groups)  11 us
    all_to_all x1, waiting for transfers between devices, local(): lax.all_to_all(parts, BOTH, 0, 0, tiled=True, axis_index_groups=chip_groups)  5.74 us
    ppermute x1, starting transfers between devices, local(): act_away = lax.ppermute(act_here, BOTH, neighbour_perm)  3.92 us
    ppermute x1, starting transfers between devices, local(): lax.ppermute(dot(cotangent_all[:cut], w_out, ((1,), (1,))), BOTH, neighbo...  3.91 us
    ppermute x1, waiting for transfers between devices, local(): slope_away = lax.ppermute(slope_here, BOTH, neighbour_perm)  3.73 us
  transfers between devices with their start and end apart: 10, of which 6 were waited for; matrix products, arithmetic and copies ran while one was open for 11% of the time, Pallas kernels for 0%

profile of v1, /device:TPU:6, one launch (start us, length us, event | category | flops | bytes accessed | tf_op | source)
XLA Modules:
  0.0 166.8 jit_solution(3303348439112382232)
XLA Ops:
  0.6 0.8 pad_maximum_fusion.7
  1.4 1.0 broadcast_in_dim.2
  2.4 11.0 %all-to-all-start = ((f32[16,32,384]{2,1,0:T(8,128)}), f32[16,32,384]{2,1,0:T(8,128)S(1)}, u32[]{:S(2)}, u32[]{:S(2)}) async-start(f32[16,32,384]{2,1,0:T(8,128)} %broadcast_in_dim.2), calls=%async_computation | async-start | bytes 1572864 | tf_op jit(solution)/shard_map/all_to_all | solution.py:109
  13.4 1.9 %collective-permute-start = (f32[384,384]{1,0:T(8,128)}, f32[384,384]{1,0:T(8,128)S(1)}, u32[]{:S(2)}, u32[]{:S(2)}) collective-permute-start(f32[384,384]{1,0:T(8,128)} %param.5), channel_id=1, source_target_pairs={{0,16},{16,0},{32,48},{48,32},{64,80},{80,64},{96,112},{112,96},{1... | collective-permute-start | bytes 1769480 | tf_op jit(solution)/shard_map/ppermute | solution.py:104
  15.3 2.4 %collective-permute-start.2 = (f32[384,384]{1,0:T(8,128)}, f32[384,384]{1,0:T(8,128)}, u32[]{:S(2)}, u32[]{:S(2)}) collective-permute-start(f32[384,384]{1,0:T(8,128)} %param.6), channel_id=1, source_target_pairs={{0,16},{16,0},{32,48},{48,32},{64,80},{80,64},{96,112},{112,96},{1... | collective-permute-start | bytes 1769480 | tf_op jit(solution)/shard_map/ppermute | solution.py:105
  17.7 1.1 constant_dynamic-update-slice_fusion.1
  18.8 1.1 constant_dynamic-update-slice_fusion.3
  19.9 0.0 collective-permute-done
  20.0 2.8 %all-to-all-done = f32[16,32,384]{2,1,0:T(8,128)S(1)} async-done(((f32[16,32,384]{2,1,0:T(8,128)}), f32[16,32,384]{2,1,0:T(8,128)S(1)}, u32[]{:S(2)}, u32[]{:S(2)}) %all-to-all-start) | async-done | bytes 786464 | tf_op jit(solution)/shard_map/all_to_all | solution.py:109
  22.8 0.1 fusion.35
  22.9 1.3 fusion.37
  24.1 1.9 %collective-permute-start.1 = (f32[128,768]{1,0:T(8,128)}, f32[128,768]{1,0:T(8,128)}, u32[]{:S(2)}, u32[]{:S(2)}) collective-permute-start(f32[128,768]{1,0:T(8,128)} %fusion.37), channel_id=1, source_target_pairs={{0,1},{1,0},{2,3},{3,2},{4,5},{5,4},{6,7},{7,6},{8,9},{9,8},{10,11... | collective-permute-start | bytes 1179656 | tf_op jit(solution)/shard_map/ppermute | solution.py:117
  26.0 0.0 collective-permute-done.2
  26.1 1.1 constant_dynamic-update-slice_fusion.2
  27.2 1.4 fusion.38
  28.5 3.9 %collective-permute-start.3 = (f32[128,768]{1,0:T(8,128)}, f32[128,768]{1,0:T(8,128)}, u32[]{:S(2)}, u32[]{:S(2)}) collective-permute-start(f32[128,768]{1,0:T(8,128)} %fusion.38), channel_id=1, source_target_pairs={{0,1},{1,0},{2,3},{3,2},{4,5},{5,4},{6,7},{7,6},{8,9},{9,8},{10,11... | collective-permute-start | bytes 1179656 | tf_op jit(solution)/shard_map/ppermute | solution.py:118
  32.5 1.6 collective-permute-done.1
  34.1 1.5 convolution_add_fusion.3
  35.6 2.9 %collective-permute-done.3 = f32[128,768]{1,0:T(8,128)} collective-permute-done((f32[128,768]{1,0:T(8,128)}, f32[128,768]{1,0:T(8,128)}, u32[]{:S(2)}, u32[]{:S(2)}) %collective-permute-start.3) | collective-permute-done | bytes 393248 | tf_op jit(solution)/shard_map/ppermute | solution.py:118
  38.5 1.6 convolution_add_fusion.2
  40.2 17.0 %all-gather = f32[4,2,16,768]{3,2,1,0:T(8,128)S(1)} all-gather(f32[2,2,16,768]{3,2,1,0:T(8,128)S(1)} %fusion.12), channel_id=2, replica_groups={{2,4},{3,5},{6,8},{7,9},{10,12},{11,13},{14,0},{15,1},{16,18},{17,19},{..., dimensions={0}, use_global_device_ids=true | all-gather | bytes 589824 | tf_op jit(solution)/shard_map/all_gather | solution.py:101
  57.2 13.4 %all-gather.1 = f32[4,2,16,768]{3,2,1,0:T(8,128)S(1)} all-gather(f32[2,2,16,768]{3,2,1,0:T(8,128)S(1)} %fusion.16), channel_id=3, replica_groups={{0,2},{1,3},{4,6},{5,7},{8,10},{9,11},{12,14},{13,15},{18,20},{19,21},{..., dimensions={0}, use_global_device_ids=true | all-gather | bytes 589824 | tf_op jit(solution)/shard_map/all_gather | solution.py:101
  70.7 8.6 %all-gather.2 = f32[4,2,16,768]{3,2,1,0:T(8,128)S(1)} all-gather(f32[2,2,16,768]{3,2,1,0:T(8,128)S(1)} %fusion.14), channel_id=4, replica_groups={{2,4},{3,5},{6,8},{7,9},{10,12},{11,13},{14,0},{15,1},{16,18},{17,19},{..., dimensions={0}, use_global_device_ids=true | all-gather | bytes 589824 | tf_op jit(solution)/shard_map/all_gather | solution.py:101
  79.4 6.2 %all-gather.3 = f32[4,1,16,768]{3,2,1,0:T(8,128)S(1)} all-gather(f32[2,1,16,768]{3,2,1,0:T(8,128)S(1)} %slice_add_fusion), channel_id=5, replica_groups={{0,2},{1,3},{4,6},{5,7},{8,10},{9,11},{12,14},{13,15},{18,20},{19,21},{..., dimensions={0}, use_global_device_ids=true | all-gather | bytes 294912 | tf_op jit(solution)/shard_map/all_gather | solution.py:101
  85.7 7.2 %all-gather.4 = f32[4,1,16,768]{3,2,1,0:T(8,128)S(1)} all-gather(f32[2,1,16,768]{3,2,1,0:T(8,128)S(1)} %pad_maximum_fusion.6), channel_id=6, replica_groups={{0,2},{1,3},{4,6},{5,7},{8,10},{9,11},{12,14},{13,15},{18,20},{19,21},{..., dimensions={0}, use_global_device_ids=true | all-gather | bytes 294912 | tf_op jit(solution)/shard_map/all_gather | solution.py:101
  92.9 11.5 %all-gather.5 = f32[4,2,16,768]{3,2,1,0:T(8,128)S(1)} all-gather(f32[2,2,16,768]{3,2,1,0:T(8,128)S(1)} %maximum_maximum_fusion), channel_id=7, replica_groups={{2,4},{3,5},{6,8},{7,9},{10,12},{11,13},{14,0},{15,1},{16,18},{17,19},{..., dimensions={0}, use_global_device_ids=true | all-gather | bytes 589824 | tf_op jit(solution)/shard_map/all_gather | solution.py:101
  104.4 7.4 %all-gather.6 = f32[4,2,16,768]{3,2,1,0:T(8,128)S(1)} all-gather(f32[2,2,16,768]{3,2,1,0:T(8,128)S(1)} %slice_select_fusion.2), channel_id=8, replica_groups={{0,2},{1,3},{4,6},{5,7},{8,10},{9,11},{12,14},{13,15},{18,20},{19,21},{..., dimensions={0}, use_global_device_ids=true | all-gather | bytes 589824 | tf_op jit(solution)/shard_map/all_gather | solution.py:101
  111.8 10.5 %all_gather.57 = f32[2,2,2,16,768]{4,3,2,1,0:T(8,128)S(1)} all-gather(f32[1,2,2,16,768]{4,3,2,1,0:T(8,128)S(1)} %fusion.21), channel_id=1, replica_groups={{2,4},{3,5},{6,8},{7,9},{10,12},{11,13},{14,0},{15,1},{16,18},{17,19},{..., dimensions={0}, use_global_device_ids=true | all-gather | bytes 589824 | tf_op jit(solution)/shard_map/all_gather | solution.py:101
  122.4 0.1 fusion.34
  122.5 1.9 %collective-permute-start.5 = (f32[128,768]{1,0:T(8,128)S(1)}, f32[128,768]{1,0:T(8,128)S(1)}, u32[]{:S(2)}, u32[]{:S(2)}) collective-permute-start(f32[128,768]{1,0:T(8,128)S(1)} %bitcast.46), channel_id=1, source_target_pairs={{0,1},{1,0},{2,3},{3,2},{4,5},{5,4},{6,7},{7,6},{8,9},{9,8},{10,11... | collective-permute-start | bytes 1179656 | tf_op jit(solution)/shard_map/ppermute | solution.py:144
  124.4 3.9 %collective-permute-start.4 = (f32[128,768]{1,0:T(8,128)S(1)}, f32[128,768]{1,0:T(8,128)S(1)}, u32[]{:S(2)}, u32[]{:S(2)}) collective-permute-start(f32[128,768]{1,0:T(8,128)S(1)} %bitcast.42), channel_id=1, source_target_pairs={{0,1},{1,0},{2,3},{3,2},{4,5},{5,4},{6,7},{7,6},{8,9},{9,8},{10,11... | collective-permute-start | bytes 1179656 | tf_op jit(solution)/shard_map/ppermute | solution.py:143
  128.4 0.1 fusion.33
  128.4 0.0 copy-start.8
  128.5 3.7 %collective-permute-done.5 = f32[128,768]{1,0:T(8,128)S(1)} collective-permute-done((f32[128,768]{1,0:T(8,128)S(1)}, f32[128,768]{1,0:T(8,128)S(1)}, u32[]{:S(2)}, u32[]{:S(2)}) %collective-permute-start.5) | collective-permute-done | bytes 393248 | tf_op jit(solution)/shard_map/ppermute | solution.py:144
  132.2 1.3 fusion.5
  133.5 1.9 %collective-permute-start.6 = (f32[384,384]{1,0:T(8,128)}, f32[384,384]{1,0:T(8,128)}, u32[]{:S(2)}, u32[]{:S(2)}) collective-permute-start(f32[384,384]{1,0:T(8,128)} %fusion.5), channel_id=1, source_target_pairs={{0,16},{16,0},{32,48},{48,32},{64,80},{80,64},{96,112},{112,96},{1... | collective-permute-start | bytes 1769480 | tf_op jit(solution)/shard_map/ppermute | solution.py:154
  135.4 0.9 collective-permute-done.4
  136.4 1.3 fusion.10
  137.7 1.9 %collective-permute-start.7 = (f32[384,384]{1,0:T(8,128)}, f32[384,384]{1,0:T(8,128)}, u32[]{:S(2)}, u32[]{:S(2)}) collective-permute-start(f32[384,384]{1,0:T(8,128)} %fusion.10), channel_id=1, source_target_pairs={{0,16},{16,0},{32,48},{48,32},{64,80},{80,64},{96,112},{112,96},{1... | collective-permute-start | bytes 1769480 | tf_op jit(solution)/shard_map/ppermute | solution.py:153
  139.7 0.8 fusion
  140.5 0.8 fusion.1
  141.3 1.0 pad_maximum_fusion.4
  142.3 13.2 %all-to-all-start.1 = ((f32[16,32,384]{2,1,0:T(8,128)}), f32[16,32,384]{2,1,0:T(8,128)S(1)}, u32[]{:S(2)}, u32[]{:S(2)}) async-start(f32[16,32,384]{2,1,0:T(8,128)} %pad_maximum_fusion.4), calls=%async_computation.1 | async-start | bytes 1572864 | tf_op jit(solution)/shard_map/all_to_all | solution.py:159
  155.5 0.0 collective-permute-done.6
  155.5 2.5 %convolution_add_fusion.1 = f32[384,384]{1,0:T(8,128)} fusion(f32[384,384]{1,0:T(8,128)} %collective-permute-done.6, f32[256,384]{1,0:T(8,128)S(1)} %bitcast.53, f32[128,768]{1,0:T(8,128)S(1)} %copy-done.5, f32[128,768]{1,0:T(8,128)S(1)} %bitcast.49), kind=kOutput, calls=%fused_computation.1 | convolution fusion | flops 226738176 | bytes 2359296 | tf_op jit(solution)/shard_map/dot_general | solution.py:13
  158.0 2.4 %convolution_add_fusion = f32[384,384]{1,0:T(8,128)} fusion(f32[384,384]{1,0:T(8,128)} %collective-permute-done.7, f32[256,384]{1,0:T(8,128)S(1)} %bitcast.51, f32[128,768]{1,0:T(8,128)S(1)} %copy-done.3, f32[128,768]{1,0:T(8,128)S(1)} %bitcast.45), kind=kOutput, calls=%fused_computation | convolution fusion | flops 226738176 | bytes 2359296 | tf_op jit(solution)/shard_map/dot_general | solution.py:13
  160.4 5.7 %all-to-all-done.1 = f32[16,32,384]{2,1,0:T(8,128)S(1)} async-done(((f32[16,32,384]{2,1,0:T(8,128)}), f32[16,32,384]{2,1,0:T(8,128)S(1)}, u32[]{:S(2)}, u32[]{:S(2)}) %all-to-all-start.1) | async-done | bytes 786464 | tf_op jit(solution)/shard_map/all_to_all | solution.py:159
  166.2 0.6 fusion.36
  (39 shorter events, 0.5 us)
Async XLA Ops:
  2.4 20.5 %all-to-all-start = ((f32[16,32,384]{2,1,0:T(8,128)}), f32[16,32,384]{2,1,0:T(8,128)S(1)}, u32[]{:S(2)}, u32[]{:S(2)}) async-start(f32[16,32,384]{2,1,0:T(8,128)} %broadcast_in_dim.2), calls=%async_computation | async-start | bytes 1572864 | tf_op jit(solution)/shard_map/all_to_all | solution.py:109
  13.4 6.6 %collective-permute-start = (f32[384,384]{1,0:T(8,128)}, f32[384,384]{1,0:T(8,128)S(1)}, u32[]{:S(2)}, u32[]{:S(2)}) collective-permute-start(f32[384,384]{1,0:T(8,128)} %param.5), channel_id=1, source_target_pairs={{0,16},{16,0},{32,48},{48,32},{64,80},{80,64},{96,112},{112,96},{1... | collective-permute-start | bytes 1769480 | tf_op jit(solution)/shard_map/ppermute | solution.py:104
  15.3 10.8 %collective-permute-start.2 = (f32[384,384]{1,0:T(8,128)}, f32[384,384]{1,0:T(8,128)}, u32[]{:S(2)}, u32[]{:S(2)}) collective-permute-start(f32[384,384]{1,0:T(8,128)} %param.6), channel_id=1, source_target_pairs={{0,16},{16,0},{32,48},{48,32},{64,80},{80,64},{96,112},{112,96},{1... | collective-permute-start | bytes 1769480 | tf_op jit(solution)/shard_map/ppermute | solution.py:105
  24.1 10.0 %collective-permute-start.1 = (f32[128,768]{1,0:T(8,128)}, f32[128,768]{1,0:T(8,128)}, u32[]{:S(2)}, u32[]{:S(2)}) collective-permute-start(f32[128,768]{1,0:T(8,128)} %fusion.37), channel_id=1, source_target_pairs={{0,1},{1,0},{2,3},{3,2},{4,5},{5,4},{6,7},{7,6},{8,9},{9,8},{10,11... | collective-permute-start | bytes 1179656 | tf_op jit(solution)/shard_map/ppermute | solution.py:117
  28.5 10.0 %collective-permute-start.3 = (f32[128,768]{1,0:T(8,128)}, f32[128,768]{1,0:T(8,128)}, u32[]{:S(2)}, u32[]{:S(2)}) collective-permute-start(f32[128,768]{1,0:T(8,128)} %fusion.38), channel_id=1, source_target_pairs={{0,1},{1,0},{2,3},{3,2},{4,5},{5,4},{6,7},{7,6},{8,9},{9,8},{10,11... | collective-permute-start | bytes 1179656 | tf_op jit(solution)/shard_map/ppermute | solution.py:118
  122.5 17.2 %copy-start = (f32[1,8,16,768]{3,2,1,0:T(8,128)}, f32[1,8,16,768]{3,2,1,0:T(8,128)S(1)}, u32[]{:S(2)}) copy-start(f32[1,8,16,768]{3,2,1,0:T(8,128)S(1)} %get-tuple-element.7) | copy-start | bytes 1179652
  122.5 9.7 %collective-permute-start.5 = (f32[128,768]{1,0:T(8,128)S(1)}, f32[128,768]{1,0:T(8,128)S(1)}, u32[]{:S(2)}, u32[]{:S(2)}) collective-permute-start(f32[128,768]{1,0:T(8,128)S(1)} %bitcast.46), channel_id=1, source_target_pairs={{0,1},{1,0},{2,3},{3,2},{4,5},{5,4},{6,7},{7,6},{8,9},{9,8},{10,11... | collective-permute-start | bytes 1179656 | tf_op jit(solution)/shard_map/ppermute | solution.py:144
  124.4 12.0 %collective-permute-start.4 = (f32[128,768]{1,0:T(8,128)S(1)}, f32[128,768]{1,0:T(8,128)S(1)}, u32[]{:S(2)}, u32[]{:S(2)}) collective-permute-start(f32[128,768]{1,0:T(8,128)S(1)} %bitcast.42), channel_id=1, source_target_pairs={{0,1},{1,0},{2,3},{3,2},{4,5},{5,4},{6,7},{7,6},{8,9},{9,8},{10,11... | collective-permute-start | bytes 1179656 | tf_op jit(solution)/shard_map/ppermute | solution.py:143
  128.4 9.3 %copy-start.6 = (f32[16,16,384]{2,1,0:T(8,128)}, f32[16,16,384]{2,1,0:T(8,128)S(1)}, u32[]{:S(2)}) copy-start(f32[16,16,384]{2,1,0:T(8,128)S(1)} %get-tuple-element.4) | copy-start | bytes 1179652
  128.4 9.3 %copy-start.8 = (f32[16,16,384]{2,1,0:T(8,128)}, f32[16,16,384]{2,1,0:T(8,128)S(1)}, u32[]{:S(2)}) copy-start(f32[16,16,384]{2,1,0:T(8,128)S(1)} %get-tuple-element.5) | copy-start | bytes 1179652
  132.2 7.5 %copy-start.4 = (f32[128,768]{1,0:T(8,128)}, f32[128,768]{1,0:T(8,128)S(1)}, u32[]{:S(2)}) copy-start(f32[128,768]{1,0:T(8,128)S(1)} %collective-permute-done.5) | copy-start | bytes 1179652
  133.5 22.0 %collective-permute-start.6 = (f32[384,384]{1,0:T(8,128)}, f32[384,384]{1,0:T(8,128)}, u32[]{:S(2)}, u32[]{:S(2)}) collective-permute-start(f32[384,384]{1,0:T(8,128)} %fusion.5), channel_id=1, source_target_pairs={{0,16},{16,0},{32,48},{48,32},{64,80},{80,64},{96,112},{112,96},{1... | collective-permute-start | bytes 1769480 | tf_op jit(solution)/shard_map/ppermute | solution.py:154
  136.4 4.1 %copy-start.2 = (f32[128,768]{1,0:T(8,128)}, f32[128,768]{1,0:T(8,128)S(1)}, u32[]{:S(2)}) copy-start(f32[128,768]{1,0:T(8,128)S(1)} %collective-permute-done.4) | copy-start | bytes 1179652
  137.7 20.3 %collective-permute-start.7 = (f32[384,384]{1,0:T(8,128)}, f32[384,384]{1,0:T(8,128)}, u32[]{:S(2)}, u32[]{:S(2)}) collective-permute-start(f32[384,384]{1,0:T(8,128)} %fusion.10), channel_id=1, source_target_pairs={{0,16},{16,0},{32,48},{48,32},{64,80},{80,64},{96,112},{112,96},{1... | collective-permute-start | bytes 1769480 | tf_op jit(solution)/shard_map/ppermute | solution.py:153
  142.3 13.2 %copy-start.1 = (f32[1,8,16,768]{3,2,1,0:T(8,128)S(1)}, f32[1,8,16,768]{3,2,1,0:T(8,128)}, u32[]{:S(2)}) copy-start(f32[1,8,16,768]{3,2,1,0:T(8,128)} %copy-done) | copy-start | bytes 1179652
  142.3 13.3 %copy-start.5 = (f32[128,768]{1,0:T(8,128)S(1)}, f32[128,768]{1,0:T(8,128)}, u32[]{:S(2)}) copy-start(f32[128,768]{1,0:T(8,128)} %copy-done.4) | copy-start | bytes 1179652
  142.3 13.3 %copy-start.9 = (f32[16,16,384]{2,1,0:T(8,128)S(1)}, f32[16,16,384]{2,1,0:T(8,128)}, u32[]{:S(2)}) copy-start(f32[16,16,384]{2,1,0:T(8,128)} %copy-done.8) | copy-start | bytes 1179652
  142.3 23.9 %all-to-all-start.1 = ((f32[16,32,384]{2,1,0:T(8,128)}), f32[16,32,384]{2,1,0:T(8,128)S(1)}, u32[]{:S(2)}, u32[]{:S(2)}) async-start(f32[16,32,384]{2,1,0:T(8,128)} %pad_maximum_fusion.4), calls=%async_computation.1 | async-start | bytes 1572864 | tf_op jit(solution)/shard_map/all_to_all | solution.py:159
  155.5 2.5 %copy-start.3 = (f32[128,768]{1,0:T(8,128)S(1)}, f32[128,768]{1,0:T(8,128)}, u32[]{:S(2)}) copy-start(f32[128,768]{1,0:T(8,128)} %copy-done.2) | copy-start | bytes 1179652
  155.5 2.5 %copy-start.7 = (f32[16,16,384]{2,1,0:T(8,128)S(1)}, f32[16,16,384]{2,1,0:T(8,128)}, u32[]{:S(2)}) copy-start(f32[16,16,384]{2,1,0:T(8,128)} %copy-done.6) | copy-start | bytes 1179652

commit v2 on v0

v2 whole, which is shorter than its diff:
```python
import math

import jax
import jax.numpy as jnp
from jax import lax
from jax.experimental import pallas as pl
from jax.experimental.pallas import tpu as pltpu
from jax.sharding import PartitionSpec as P

BOTH = ("row", "col")
HIGH = lax.Precision.HIGH


def dot(left, right, dims):
    return lax.dot_general(left, right, (dims, ((), ())), precision=HIGH, preferred_element_type=jnp.float32)


def gelu_value(pre):
    return pre * 0.5 * (1.0 + jax.scipy.special.erf(pre / math.sqrt(2.0)))


def gelu_slope(pre):
    cumulative = 0.5 * (1.0 + jax.scipy.special.erf(pre / math.sqrt(2.0)))
    density = jnp.exp(-0.5 * pre * pre) / math.sqrt(2.0 * math.pi)
    return cumulative + pre * density


def split(value):
    high = value.astype(jnp.bfloat16)
    return high, (value - high.astype(jnp.float32)).astype(jnp.bfloat16)


def over_tokens(left, right):
    def one(a, b):
        return lax.dot_general(a, b, (((0,), (0,)), ((), ())), preferred_element_type=jnp.float32)

    (lh, ll), (rh, rl) = split(left), split(right)
    return one(lh, rh) + (one(lh, rl) + one(ll, rh))


def join_kernel(w_in, w_in_other, w_out, w_out_other, in_joined, out_joined):
    size = w_in.shape[1]
    in_joined[:, :size] = w_in[...]
    in_joined[:, size:] = w_in_other[...]
    out_joined[:size] = w_out[...]
    out_joined[size:] = w_out_other[...]


def join(w_in, w_in_other, w_out, w_out_other):
    d, h = w_in.shape
    return pl.pallas_call(
        join_kernel,
        out_shape=[jax.ShapeDtypeStruct((d, 2 * h), jnp.float32), jax.ShapeDtypeStruct((2 * h, d), jnp.float32)],
        in_specs=[pl.BlockSpec(memory_space=pltpu.VMEM)] * 4,
        out_specs=[pl.BlockSpec(memory_space=pltpu.VMEM)] * 2,
        compiler_params=pltpu.CompilerParams(vmem_limit_bytes=16 * 2**20),
        cost_estimate=pl.CostEstimate(flops=1000, bytes_accessed=1000, transcendentals=0),
    )(w_in, w_in_other, w_out, w_out_other)


def weight_grads_kernel(act_away, act_here, slope_away, slope_here, tokens, cotangent, *rest):
    cut = act_away.shape[0]
    size = cotangent.shape[1]
    outs = rest[-2:]
    at = pl.ds(0, size) if len(rest) == 4 else pl.ds(act_away.shape[1] - size, size)
    grad = over_tokens(act_away[:, at], cotangent[:cut]) + over_tokens(act_here[:, at], cotangent[cut:])
    outs[0][...] = grad + rest[0][...] if len(rest) == 4 else grad
    grad = over_tokens(tokens[:cut], slope_away[:, at]) + over_tokens(tokens[cut:], slope_here[:, at])
    outs[1][...] = grad + rest[1][...] if len(rest) == 4 else grad


def weight_grads(act_away, act_here, slope_away, slope_here, tokens, cotangent, *other):
    size = cotangent.shape[1]
    args = (act_away, act_here, slope_away, slope_here, tokens, cotangent, *other)
    return pl.pallas_call(
        weight_grads_kernel,
        out_shape=[jax.ShapeDtypeStruct((size, size), jnp.float32)] * 2,
        in_specs=[pl.BlockSpec(memory_space=pltpu.VMEM)] * len(args),
        out_specs=[pl.BlockSpec(memory_space=pltpu.VMEM)] * 2,
        compiler_params=pltpu.CompilerParams(vmem_limit_bytes=24 * 2**20),
        cost_estimate=pl.CostEstimate(flops=1000, bytes_accessed=1000, transcendentals=0),
    )(*args)


class Plan:
    def __init__(self, rows, cols):
        self.rows, self.cols = rows, cols
        self.ring = cols // 2

    def flat(self, row, col):
        return row * self.cols + col

    def members(self, core, parity):
        return [2 * ((core + i) % self.ring) + parity for i in range(self.ring)]

    def chip_groups(self):
        groups = []
        for col in range(self.cols):
            for core in range(2):
                order = self.members(core, 1 - col % 2) + self.members(core, col % 2)
                groups.append([self.flat(2 * k + core, col) for k in order])
        return groups

    def neighbour_perm(self, way):
        return [
            (self.flat(row, col), self.flat(row, (col + (way if row % 2 == 0 else -way)) % self.cols))
            for row in range(self.rows)
            for col in range(self.cols)
        ]

    def ring_groups(self):
        return [
            [self.flat(row, col) for col in self.members(row % 2, parity)]
            for row in range(self.rows)
            for parity in range(2)
        ]

    def pair_groups(self, step):
        groups = []
        for ring in self.ring_groups():
            for i in range(step % 2, self.ring, 2):
                groups.append([ring[i], ring[(i + 1) % self.ring]])
        return groups


def solution(mesh):
    rows, cols = mesh.shape["row"], mesh.shape["col"]
    plan = Plan(rows, cols)
    half = cols // 2
    chip_groups = plan.chip_groups()
    ring_groups = plan.ring_groups()
    one_way, other_way = plan.neighbour_perm(1), plan.neighbour_perm(-1)
    core_perm = [(row, row ^ 1) for row in range(rows)]

    def local(tokens, weight_in, weight_out, cotangent):
        n, d = tokens.shape
        h = weight_in.shape[1]
        core = lax.axis_index("row") & 1
        place = ((lax.axis_index("col") >> 1) - core) & (half - 1)
        odd = place & 1
        pair_at = place >> 1
        turn = 2 * odd - 1
        pairs = half // 2

        def pair_swap(block, step):
            got = lax.all_gather(block, BOTH, axis=0, axis_index_groups=plan.pair_groups(step))
            return jnp.where((odd + step) & 1 == 0, got[1], got[0])

        sent = jnp.broadcast_to(jnp.concatenate([tokens, cotangent], axis=0)[None], (cols, 2 * n, d))
        sent, weight_in, weight_out = lax.optimization_barrier((sent, weight_in, weight_out))
        weight_in_other = lax.ppermute(weight_in, "row", core_perm)
        weight_out_other = lax.ppermute(weight_out, "row", core_perm)
        gathered = lax.all_to_all(sent, BOTH, 0, 0, tiled=True, axis_index_groups=chip_groups)
        w_in, w_out = join(weight_in, weight_in_other, weight_out, weight_out_other)
        gathered, w_in, w_out = lax.optimization_barrier((gathered, w_in, w_out))
        token_all = gathered[:, :n].reshape(cols * n, d)
        cotangent_all = gathered[:, n:].reshape(cols * n, d)
        cut = half * n

        pre_away = lax.ppermute(dot(token_all[:cut], w_in, ((1,), (0,))), BOTH, one_way)
        grad_away = lax.ppermute(dot(cotangent_all[:cut], w_out, ((1,), (1,))), BOTH, other_way)
        pre_sum = dot(token_all[cut:], w_in, ((1,), (0,))) + pre_away
        grad_sum = dot(cotangent_all[cut:], w_out, ((1,), (1,))) + grad_away
        sums = jnp.stack([pre_sum, grad_sum]).reshape(2, pairs, 2 * n, 2 * h)

        def pair_sum(at):
            return lax.dynamic_slice_in_dim(sums, at & (pairs - 1), 1, axis=1)

        arrived = pair_swap(pair_sum(pair_at + 2), 3)
        arrived = pair_swap(pair_sum(pair_at - turn) + arrived, 2)
        arrived = pair_swap(pair_sum(pair_at + turn) + arrived, 1)
        last = (pair_sum(pair_at) + arrived).reshape(2, 2, n, 2 * h)
        theirs = jnp.where(odd == 0, last[:, 1], last[:, 0])
        mine = jnp.where(odd == 0, last[:, 0], last[:, 1]) + pair_swap(theirs, 0)

        pre, grad = mine[0], mine[1]
        own = jnp.stack([gelu_value(pre), grad * gelu_slope(pre)])
        ring = lax.all_gather(own, BOTH, axis=0, axis_index_groups=ring_groups)
        act_here = ring[:, 0].reshape(cut, 2 * h)
        slope_here = ring[:, 1].reshape(cut, 2 * h)
        act_away = lax.ppermute(act_here, BOTH, one_way)
        slope_away = lax.ppermute(slope_here, BOTH, other_way)

        def out_rows(act):
            return dot(act, w_out, ((1,), (0,))).reshape(half, n, d)

        def in_rows(slope):
            return dot(slope, w_in, ((1,), (1,))).reshape(half, n, d)

        here = jnp.concatenate([out_rows(act_here), in_rows(slope_here)], axis=1)
        away = jnp.concatenate([out_rows(act_away), in_rows(slope_away)], axis=1)
        parts = jnp.concatenate([away, here], axis=0)
        parts, act_away, slope_away = lax.optimization_barrier((parts, act_away, slope_away))
        parts = lax.all_to_all(parts, BOTH, 0, 0, tiled=True, axis_index_groups=chip_groups)

        hidden = (act_away, act_here, slope_away, slope_here, token_all, cotangent_all)
        out_other, in_other = weight_grads(*hidden)
        out_other = lax.ppermute(out_other, "row", core_perm)
        in_other = lax.ppermute(in_other, "row", core_perm)
        weight_out_grad, weight_in_grad = weight_grads(*hidden, out_other, in_other)

        total = jnp.sum(parts, axis=0)
        return (total[:n], total[n:], weight_in_grad, weight_out_grad)

    placed = (P("row", "col"), P("col", "row"), P("row", "col"), P("row", "col"))
    return jax.shard_map(
        local,
        mesh=mesh,
        in_specs=placed,
        out_specs=(P("row", "col"), P("row", "col"), P("col", "row"), P("row", "col")),
        check_vma=False,
    )
```

time: 425 us -> 152 us (0.36)
  waiting for transfers between devices: 278 us -> 20.2 us
  blocking collectives: 115 us -> 71.9 us
  starting transfers between devices: 0.16 us -> 41 us
  between operations: 13.8 us -> 0.93 us
  matrix products: 13.7 us -> 6.64 us
    reduce_scatter x4 -> x0, waiting for transfers between devices: 278 us -> none  [the longest x1 105 us: local(): lax.psum_scatter(product(act_all, weight_out), 'row', scatter_dimension=0...]
    all_gather x4 -> x5, blocking collectives: 115 us -> 71.9 us  [the longest x4 36.3 us: pair_swap(): lax.all_gather(block, BOTH, axis=0, axis_index_groups=plan.pair_groups(st...]
    ppermute x0 -> x8, starting transfers between devices: none -> 26.6 us  [the longest x1 9.5 us: local(): lax.ppermute(dot(cotangent_all[:cut], w_out, ((1,), (1,))), BOTH, other_way)]
    ppermute x0 -> x8, waiting for transfers between devices: none -> 14.9 us  [the longest x1 4.78 us: local(): lax.ppermute(dot(token_all[:cut], w_in, ((1,), (0,))), BOTH, one_way)]
    all_to_all x0 -> x2, starting transfers between devices: none -> 14.4 us  [the longest x1 8.6 us: local(): lax.all_to_all(sent, BOTH, 0, 0, tiled=True, axis_index_groups=chip_groups)]
    dot_general x6 -> x8, matrix products: 13.7 us -> 6.64 us  [dot(): lax.dot_general(left, right, (dims, ((), ())), precision=HIGH, preferred_...]
    all_to_all x0 -> x2, waiting for transfers between devices: none -> 5.28 us  [the longest x1 5.28 us: local(): lax.all_to_all(sent, BOTH, 0, 0, tiled=True, axis_index_groups=chip_groups)]
  transfers between devices with their start and end apart: 4 -> 10, of which waited for: 4 -> 6; matrix products, arithmetic and copies ran while one was open for 2% -> 3% of each run, Pallas kernels for 0% -> 2%
where the time goes in v2:
time: 152 us; the launch traced here: 150 us
  blocking collectives  71.9 us (47%)
  starting transfers between devices  41 us (27%)
  waiting for transfers between devices  20.2 us (13%)
  matrix products  6.64 us (4%)
  local copies, waits for them, and re-layouts  4.18 us (3%)
  Pallas kernels  3.21 us (2%)
  other arithmetic  2.03 us (1%)
    all_gather x4, blocking collectives, pair_swap(): lax.all_gather(block, BOTH, axis=0, axis_index_groups=plan.pair_groups(st...  36.3 us
    all_gather x1, blocking collectives, local(): ring = lax.all_gather(own, BOTH, axis=0, axis_index_groups=ring_groups)  35.6 us
    ppermute x1, starting transfers between devices, local(): lax.ppermute(dot(cotangent_all[:cut], w_out, ((1,), (1,))), BOTH, other_way)  9.5 us
    all_to_all x1, starting transfers between devices, local(): lax.all_to_all(sent, BOTH, 0, 0, tiled=True, axis_index_groups=chip_groups)  8.6 us
    dot_general x8, matrix products, dot(): lax.dot_general(left, right, (dims, ((), ())), precision=HIGH, preferred_...  6.64 us
    all_to_all x1, starting transfers between devices, local(): lax.all_to_all(parts, BOTH, 0, 0, tiled=True, axis_index_groups=chip_groups)  5.75 us
    all_to_all x1, waiting for transfers between devices, local(): lax.all_to_all(sent, BOTH, 0, 0, tiled=True, axis_index_groups=chip_groups)  5.28 us
    ppermute x1, waiting for transfers between devices, local(): lax.ppermute(dot(token_all[:cut], w_in, ((1,), (0,))), BOTH, one_way)  4.78 us
  transfers between devices with their start and end apart: 10, of which 6 were waited for; matrix products, arithmetic and copies ran while one was open for 3% of the time, Pallas kernels for 2%

profile of v2, /device:TPU:6, one launch (start us, length us, event | category | flops | bytes accessed | tf_op | source)
XLA Modules:
  0.0 150.0 jit_solution(18109499235709312805)
XLA Ops:
  0.6 0.8 pad_maximum_fusion.1
  1.4 1.0 broadcast_in_dim.2
  2.4 8.6 %all-to-all-start = ((f32[16,32,384]{2,1,0:T(8,128)}), f32[16,32,384]{2,1,0:T(8,128)}, u32[]{:S(2)}, u32[]{:S(2)}) async-start(f32[16,32,384]{2,1,0:T(8,128)} %broadcast_in_dim.2), calls=%async_computation | async-start | bytes 1572864 | tf_op jit(solution)/shard_map/all_to_all | solution.py:153
  11.0 0.0 copy-done.2
  11.0 1.9 %collective-permute-start = (f32[384,384]{1,0:T(8,128)S(1)}, f32[384,384]{1,0:T(8,128)S(1)}, u32[]{:S(2)}, u32[]{:S(2)}) collective-permute-start(f32[384,384]{1,0:T(8,128)S(1)} %copy-done.2), channel_id=1, source_target_pairs={{0,16},{16,0},{32,48},{48,32},{64,80},{80,64},{96,112},{112,96},{1... | collective-permute-start | bytes 1769480 | tf_op jit(solution)/shard_map/ppermute | solution.py:151
  12.9 0.0 copy-done.3
  12.9 2.4 %collective-permute-start.1 = (f32[384,384]{1,0:T(8,128)S(1)}, f32[384,384]{1,0:T(8,128)S(1)}, u32[]{:S(2)}, u32[]{:S(2)}) collective-permute-start(f32[384,384]{1,0:T(8,128)S(1)} %copy-done.3), channel_id=1, source_target_pairs={{0,16},{16,0},{32,48},{48,32},{64,80},{80,64},{96,112},{112,96},{1... | collective-permute-start | bytes 1769480 | tf_op jit(solution)/shard_map/ppermute | solution.py:152
  15.4 0.0 collective-permute-done.w_in_other
  15.4 1.6 %collective-permute-done.1.w_out_other = f32[384,384]{1,0:T(8,128)S(1)} collective-permute-done((f32[384,384]{1,0:T(8,128)S(1)}, f32[384,384]{1,0:T(8,128)S(1)}, u32[]{:S(2)}, u32[]{:S(2)}) %collective-permute-start.1) | collective-permute-done | bytes 589856 | tf_op jit(solution)/shard_map/ppermute | solution.py:152
  17.0 0.2 shard_map.75
  17.1 5.3 %all-to-all-done = f32[16,32,384]{2,1,0:T(8,128)} async-done(((f32[16,32,384]{2,1,0:T(8,128)}), f32[16,32,384]{2,1,0:T(8,128)}, u32[]{:S(2)}, u32[]{:S(2)}) %all-to-all-start) | async-done | bytes 786464 | tf_op jit(solution)/shard_map/all_to_all | solution.py:153
  22.4 1.3 fusion.23
  23.7 0.5 fusion.25
  24.2 2.6 %collective-permute-start.2 = (f32[128,768]{1,0:T(8,128)S(1)}, f32[128,768]{1,0:T(8,128)}, u32[]{:S(2)}, u32[]{:S(2)}) collective-permute-start(f32[128,768]{1,0:T(8,128)S(1)} %fusion.25), channel_id=1, source_target_pairs={{0,1},{1,2},{2,3},{3,4},{4,5},{5,6},{6,7},{7,8},{8,9},{9,10},{10,1... | collective-permute-start | bytes 1179656 | tf_op jit(solution)/shard_map/ppermute | solution.py:160
  26.8 0.6 fusion.26
  27.5 9.5 %collective-permute-start.3 = (f32[128,768]{1,0:T(8,128)S(1)}, f32[128,768]{1,0:T(8,128)}, u32[]{:S(2)}, u32[]{:S(2)}) collective-permute-start(f32[128,768]{1,0:T(8,128)S(1)} %fusion.26), channel_id=1, source_target_pairs={{0,15},{1,0},{2,1},{3,2},{4,3},{5,4},{6,5},{7,6},{8,7},{9,8},{10,9... | collective-permute-start | bytes 1179656 | tf_op jit(solution)/shard_map/ppermute | solution.py:161
  37.0 4.8 %collective-permute-done.2 = f32[128,768]{1,0:T(8,128)} collective-permute-done((f32[128,768]{1,0:T(8,128)S(1)}, f32[128,768]{1,0:T(8,128)}, u32[]{:S(2)}, u32[]{:S(2)}) %collective-permute-start.2) | collective-permute-done | bytes 393248 | tf_op jit(solution)/shard_map/ppermute | solution.py:160
  41.8 1.5 convolution_add_fusion.1
  43.3 0.0 collective-permute-done.3
  43.3 1.6 %convolution_add_fusion = f32[128,768]{1,0:T(8,128)S(1)} fusion(f32[128,768]{1,0:T(8,128)} %collective-permute-done.3, f32[128,384]{1,0:T(8,128)S(1)} %bitcast.83, f32[768,384]{1,0:T(8,128)S(1)} %get-tuple-element.26), kind=kOutput, calls=%fused_computation.8 | convolution fusion | flops 226590720 | bytes 2162688 | tf_op jit(solution)/shard_map/dot_general | solution.py:15
  45.0 10.4 %all-gather = f32[4,1,32,768]{3,2,1,0:T(8,128)S(1)} all-gather(f32[2,1,32,768]{3,2,1,0:T(8,128)S(1)} %fusion.6), channel_id=2, replica_groups={{2,4},{6,8},{10,12},{14,0},{3,5},{7,9},{11,13},{15,1},{20,22},{24,26},{..., dimensions={0}, use_global_device_ids=true | all-gather | bytes 589824 | tf_op jit(solution)/shard_map/all_gather | solution.py:146
  55.5 8.1 %all-gather.1 = f32[4,1,32,768]{3,2,1,0:T(8,128)S(1)} all-gather(f32[2,1,32,768]{3,2,1,0:T(8,128)S(1)} %fusion.12), channel_id=3, replica_groups={{0,2},{4,6},{8,10},{12,14},{1,3},{5,7},{9,11},{13,15},{18,20},{22,24},{..., dimensions={0}, use_global_device_ids=true | all-gather | bytes 589824 | tf_op jit(solution)/shard_map/all_gather | solution.py:146
  63.7 11.5 %all-gather.2 = f32[4,1,32,768]{3,2,1,0:T(8,128)S(1)} all-gather(f32[2,1,32,768]{3,2,1,0:T(8,128)S(1)} %fusion.10), channel_id=4, replica_groups={{2,4},{6,8},{10,12},{14,0},{3,5},{7,9},{11,13},{15,1},{20,22},{24,26},{..., dimensions={0}, use_global_device_ids=true | all-gather | bytes 589824 | tf_op jit(solution)/shard_map/all_gather | solution.py:146
  75.2 6.2 %all-gather.3 = f32[4,1,16,768]{3,2,1,0:T(8,128)S(1)} all-gather(f32[2,1,16,768]{3,2,1,0:T(8,128)S(1)} %slice_select_fusion.4), channel_id=5, replica_groups={{0,2},{4,6},{8,10},{12,14},{1,3},{5,7},{9,11},{13,15},{18,20},{22,24},{..., dimensions={0}, use_global_device_ids=true | all-gather | bytes 294912 | tf_op jit(solution)/shard_map/all_gather | solution.py:146
  81.5 35.6 %all-gather.4 = f32[16,16,768]{2,1,0:T(8,128)S(1)} all-gather(f32[2,16,768]{2,1,0:T(8,128)S(1)} %pad_maximum_fusion), channel_id=6, replica_groups={{0,2,4,6,8,10,12,14},{1,3,5,7,9,11,13,15},{18,20,22,24,26,28,30,16},{19..., dimensions={0}, use_global_device_ids=true | all-gather | bytes 884736 | tf_op jit(solution)/shard_map/all_gather | solution.py:178
  117.1 0.1 fusion.22
  117.1 0.0 copy-start
  117.2 1.9 %collective-permute-start.5 = (f32[128,768]{1,0:T(8,128)S(1)}, f32[128,768]{1,0:T(8,128)S(1)}, u32[]{:S(2)}, u32[]{:S(2)}) collective-permute-start(f32[128,768]{1,0:T(8,128)S(1)} %bitcast.63), channel_id=1, source_target_pairs={{0,15},{1,0},{2,1},{3,2},{4,3},{5,4},{6,5},{7,6},{8,7},{9,8},{10,9... | collective-permute-start | bytes 1179656 | tf_op jit(solution)/shard_map/ppermute | solution.py:182
  119.1 0.7 fusion
  119.8 3.9 %collective-permute-start.4 = (f32[128,768]{1,0:T(8,128)S(1)}, f32[128,768]{1,0:T(8,128)S(1)}, u32[]{:S(2)}, u32[]{:S(2)}) collective-permute-start(f32[128,768]{1,0:T(8,128)S(1)} %bitcast.60), channel_id=1, source_target_pairs={{0,1},{1,2},{2,3},{3,4},{4,5},{5,6},{6,7},{7,8},{8,9},{9,10},{10,1... | collective-permute-start | bytes 1179656 | tf_op jit(solution)/shard_map/ppermute | solution.py:181
  123.7 0.5 fusion.2
  124.2 0.0 copy-done
  124.2 2.6 %collective-permute-done.5.slope_away = f32[128,768]{1,0:T(8,128)S(1)} collective-permute-done((f32[128,768]{1,0:T(8,128)S(1)}, f32[128,768]{1,0:T(8,128)S(1)}, u32[]{:S(2)}, u32[]{:S(2)}) %collective-permute-start.5) | collective-permute-done | bytes 393248 | tf_op jit(solution)/shard_map/ppermute | solution.py:182
  126.8 0.7 fusion.28
  127.5 4.3 %collective-permute-done.4.act_away = f32[128,768]{1,0:T(8,128)S(1)} collective-permute-done((f32[128,768]{1,0:T(8,128)S(1)}, f32[128,768]{1,0:T(8,128)S(1)}, u32[]{:S(2)}, u32[]{:S(2)}) %collective-permute-start.4) | collective-permute-done | bytes 393248 | tf_op jit(solution)/shard_map/ppermute | solution.py:181
  131.8 0.5 fusion.27
  132.3 1.0 maximum_maximum_fusion
  133.4 5.8 %all-to-all-start.1 = ((f32[16,32,384]{2,1,0:T(8,128)}), f32[16,32,384]{2,1,0:T(8,128)S(1)}, u32[]{:S(2)}, u32[]{:S(2)}) async-start(f32[16,32,384]{2,1,0:T(8,128)} %maximum_maximum_fusion), calls=%async_computation.1 | async-start | bytes 1572864 | tf_op jit(solution)/shard_map/all_to_all | solution.py:194
  139.1 1.2 fusion.21
  140.3 0.0 copy-done.1
  140.4 1.1 shard_map.76
  141.5 1.9 %collective-permute-start.6 = (f32[384,384]{1,0:T(8,128)S(1)}, f32[384,384]{1,0:T(8,128)S(1)}, u32[]{:S(2)}, u32[]{:S(2)}) collective-permute-start(f32[384,384]{1,0:T(8,128)S(1)} %get-tuple-element.30), channel_id=1, source_target_pairs={{0,16},{16,0},{32,48},{48,32},{64,80},{80,64},{96,112},{112,96},{1... | collective-permute-start | bytes 1769480 | tf_op jit(solution)/shard_map/ppermute | solution.py:198
  143.4 2.4 %collective-permute-start.7 = (f32[384,384]{1,0:T(8,128)S(1)}, f32[384,384]{1,0:T(8,128)S(1)}, u32[]{:S(2)}, u32[]{:S(2)}) collective-permute-start(f32[384,384]{1,0:T(8,128)S(1)} %get-tuple-element.31), channel_id=1, source_target_pairs={{0,16},{16,0},{32,48},{48,32},{64,80},{80,64},{96,112},{112,96},{1... | collective-permute-start | bytes 1769480 | tf_op jit(solution)/shard_map/ppermute | solution.py:199
  145.8 0.0 collective-permute-done.6.rest_0_
  145.8 1.6 %collective-permute-done.7.rest_1_ = f32[384,384]{1,0:T(8,128)S(1)} collective-permute-done((f32[384,384]{1,0:T(8,128)S(1)}, f32[384,384]{1,0:T(8,128)S(1)}, u32[]{:S(2)}, u32[]{:S(2)}) %collective-permute-start.7) | collective-permute-done | bytes 589856 | tf_op jit(solution)/shard_map/ppermute | solution.py:199
  147.4 1.9 %shard_map.77 = (f32[384,384]{1,0:T(8,128)}, f32[384,384]{1,0:T(8,128)}) custom-call(f32[128,768]{1,0:T(8,128)S(1)} %collective-permute-done.4.act_away, f32[128,768]{1,0:T(8,128)S(1)} %bitcast.62, f32[128,768]{1,0:T(8,128)S(1)} %collective-permute-done.5.slope_away, f32[128,768]{1,0:T(8,128)S(1)} %bitcast.65, f32[256,384]{1,0:T(8,128)S(1)} %bitcast.69, ...), custom_call_target="tpu_custom_call" | custom-call | flops 1000 | bytes 1000 | tf_op jit(solution)/shard_map/pallas_call | solution.py:75
  149.4 0.0 all-to-all-done.1
  149.4 0.6 fusion.24
  (12 shorter events, 0.3 us)
Async XLA Ops:
  1.4 9.6 %copy-start.2 = (f32[384,384]{1,0:T(8,128)S(1)}, f32[384,384]{1,0:T(8,128)}, u32[]{:S(2)}) copy-start(f32[384,384]{1,0:T(8,128)} %w_in) | copy-start | bytes 1769476
  1.4 11.5 %copy-start.3 = (f32[384,384]{1,0:T(8,128)S(1)}, f32[384,384]{1,0:T(8,128)}, u32[]{:S(2)}) copy-start(f32[384,384]{1,0:T(8,128)} %w_out) | copy-start | bytes 1769476
  2.4 20.0 %all-to-all-start = ((f32[16,32,384]{2,1,0:T(8,128)}), f32[16,32,384]{2,1,0:T(8,128)}, u32[]{:S(2)}, u32[]{:S(2)}) async-start(f32[16,32,384]{2,1,0:T(8,128)} %broadcast_in_dim.2), calls=%async_computation | async-start | bytes 1572864 | tf_op jit(solution)/shard_map/all_to_all | solution.py:153
  11.0 4.4 %collective-permute-start = (f32[384,384]{1,0:T(8,128)S(1)}, f32[384,384]{1,0:T(8,128)S(1)}, u32[]{:S(2)}, u32[]{:S(2)}) collective-permute-start(f32[384,384]{1,0:T(8,128)S(1)} %copy-done.2), channel_id=1, source_target_pairs={{0,16},{16,0},{32,48},{48,32},{64,80},{80,64},{96,112},{112,96},{1... | collective-permute-start | bytes 1769480 | tf_op jit(solution)/shard_map/ppermute | solution.py:151
  12.9 4.0 %collective-permute-start.1 = (f32[384,384]{1,0:T(8,128)S(1)}, f32[384,384]{1,0:T(8,128)S(1)}, u32[]{:S(2)}, u32[]{:S(2)}) collective-permute-start(f32[384,384]{1,0:T(8,128)S(1)} %copy-done.3), channel_id=1, source_target_pairs={{0,16},{16,0},{32,48},{48,32},{64,80},{80,64},{96,112},{112,96},{1... | collective-permute-start | bytes 1769480 | tf_op jit(solution)/shard_map/ppermute | solution.py:152
  24.2 17.6 %collective-permute-start.2 = (f32[128,768]{1,0:T(8,128)S(1)}, f32[128,768]{1,0:T(8,128)}, u32[]{:S(2)}, u32[]{:S(2)}) collective-permute-start(f32[128,768]{1,0:T(8,128)S(1)} %fusion.25), channel_id=1, source_target_pairs={{0,1},{1,2},{2,3},{3,4},{4,5},{5,6},{6,7},{7,8},{8,9},{9,10},{10,1... | collective-permute-start | bytes 1179656 | tf_op jit(solution)/shard_map/ppermute | solution.py:160
  27.5 15.8 %collective-permute-start.3 = (f32[128,768]{1,0:T(8,128)S(1)}, f32[128,768]{1,0:T(8,128)}, u32[]{:S(2)}, u32[]{:S(2)}) collective-permute-start(f32[128,768]{1,0:T(8,128)S(1)} %fusion.26), channel_id=1, source_target_pairs={{0,15},{1,0},{2,1},{3,2},{4,3},{5,4},{6,5},{7,6},{8,7},{9,8},{10,9... | collective-permute-start | bytes 1179656 | tf_op jit(solution)/shard_map/ppermute | solution.py:161
  117.1 7.1 %copy-start = (f32[8,1,16,768]{3,2,1,0:T(8,128)}, f32[8,1,16,768]{3,2,1,0:T(8,128)S(1)}, u32[]{:S(2)}) copy-start(f32[8,1,16,768]{3,2,1,0:T(8,128)S(1)} %get-tuple-element.37) | copy-start | bytes 1179652
  117.2 9.7 %collective-permute-start.5 = (f32[128,768]{1,0:T(8,128)S(1)}, f32[128,768]{1,0:T(8,128)S(1)}, u32[]{:S(2)}, u32[]{:S(2)}) collective-permute-start(f32[128,768]{1,0:T(8,128)S(1)} %bitcast.63), channel_id=1, source_target_pairs={{0,15},{1,0},{2,1},{3,2},{4,3},{5,4},{6,5},{7,6},{8,7},{9,8},{10,9... | collective-permute-start | bytes 1179656 | tf_op jit(solution)/shard_map/ppermute | solution.py:182
  119.8 12.1 %collective-permute-start.4 = (f32[128,768]{1,0:T(8,128)S(1)}, f32[128,768]{1,0:T(8,128)S(1)}, u32[]{:S(2)}, u32[]{:S(2)}) collective-permute-start(f32[128,768]{1,0:T(8,128)S(1)} %bitcast.60), channel_id=1, source_target_pairs={{0,1},{1,2},{2,3},{3,4},{4,5},{5,6},{6,7},{7,8},{8,9},{9,10},{10,1... | collective-permute-start | bytes 1179656 | tf_op jit(solution)/shard_map/ppermute | solution.py:181
  133.4 16.0 %all-to-all-start.1 = ((f32[16,32,384]{2,1,0:T(8,128)}), f32[16,32,384]{2,1,0:T(8,128)S(1)}, u32[]{:S(2)}, u32[]{:S(2)}) async-start(f32[16,32,384]{2,1,0:T(8,128)} %maximum_maximum_fusion), calls=%async_computation.1 | async-start | bytes 1572864 | tf_op jit(solution)/shard_map/all_to_all | solution.py:194
  139.1 1.2 copy-start.1
  141.5 4.3 %collective-permute-start.6 = (f32[384,384]{1,0:T(8,128)S(1)}, f32[384,384]{1,0:T(8,128)S(1)}, u32[]{:S(2)}, u32[]{:S(2)}) collective-permute-start(f32[384,384]{1,0:T(8,128)S(1)} %get-tuple-element.30), channel_id=1, source_target_pairs={{0,16},{16,0},{32,48},{48,32},{64,80},{80,64},{96,112},{112,96},{1... | collective-permute-start | bytes 1769480 | tf_op jit(solution)/shard_map/ppermute | solution.py:198
  143.4 4.0 %collective-permute-start.7 = (f32[384,384]{1,0:T(8,128)S(1)}, f32[384,384]{1,0:T(8,128)S(1)}, u32[]{:S(2)}, u32[]{:S(2)}) collective-permute-start(f32[384,384]{1,0:T(8,128)S(1)} %get-tuple-element.31), channel_id=1, source_target_pairs={{0,16},{16,0},{32,48},{48,32},{64,80},{80,64},{96,112},{112,96},{1... | collective-permute-start | bytes 1769480 | tf_op jit(solution)/shard_map/ppermute | solution.py:199

commit v3 on v0

v3 whole, which is shorter than its diff:
```python
import math

import jax
import jax.numpy as jnp
from jax import lax
from jax.experimental import pallas as pl
from jax.experimental.pallas import tpu as pltpu
from jax.sharding import PartitionSpec as P

BOTH = ("row", "col")
VMEM = pl.BlockSpec(memory_space=pltpu.VMEM)


def gelu_value(pre):
    return pre * 0.5 * (1.0 + jax.scipy.special.erf(pre / math.sqrt(2.0)))


def gelu_slope(pre):
    cumulative = 0.5 * (1.0 + jax.scipy.special.erf(pre / math.sqrt(2.0)))
    density = jnp.exp(-0.5 * pre * pre) / math.sqrt(2.0 * math.pi)
    return cumulative + pre * density


def split(value):
    high = value.astype(jnp.bfloat16)
    return high, (value - high.astype(jnp.float32)).astype(jnp.bfloat16)


def three(left, right, dims):
    def one(a, b):
        return lax.dot_general(a, b, (dims, ((), ())), preferred_element_type=jnp.float32)

    (lh, ll), (rh, rl) = split(left), split(right)
    return one(lh, rh) + (one(lh, rl) + one(ll, rh))


PLAIN, RIGHT_T, LEFT_T = ((1,), (0,)), ((1,), (1,)), ((0,), (0,))


def kernel_call(body, out_shapes, args, far=False):
    out = [pltpu.HBM(shape, jnp.float32) if far else jax.ShapeDtypeStruct(shape, jnp.float32) for shape in out_shapes]
    return pl.pallas_call(
        body,
        out_shape=out,
        in_specs=[VMEM] * len(args),
        out_specs=[VMEM] * len(out),
        compiler_params=pltpu.CompilerParams(vmem_limit_bytes=16 * 2**20),
        cost_estimate=pl.CostEstimate(flops=1000, bytes_accessed=1000, transcendentals=0),
    )(*args)


def token_rows(gathered, first, last, which):
    n, d = gathered.shape[1] // 2, gathered.shape[2]
    return gathered[first:last, which * n : (which + 1) * n, :].reshape((last - first) * n, d)


def sums_kernel(first, gathered, w_in, w_in_other, w_out, w_out_other, *outs):
    chips = gathered.shape[0] // 4
    size = w_in.shape[1]
    at = slice(first * chips, (first + len(outs)) * chips)
    for which, (weights, dims) in enumerate((((w_in, w_in_other), PLAIN), ((w_out, w_out_other), RIGHT_T))):
        rows = token_rows(gathered, at.start, at.stop, which)
        for k in range(2):
            term = three(rows, weights[k][...], dims)
            block = term.shape[0] // len(outs) // 2
            for i, out in enumerate(outs):
                for part in range(2):
                    start = (2 * i + part) * block
                    out[part, which, :, k * size : (k + 1) * size] = term[start : start + block]


def hidden_rows(blocks, which, at):
    return jnp.concatenate([block[part, which, :, at] for block in blocks for part in range(2)], axis=0)


def back_kernel(first, count, gathered, w_in, w_in_other, w_out, w_out_other, *refs):
    blocks, refs = refs[:count], refs[count:]
    before, (rows, *grads) = refs[: len(refs) - 5], refs[len(refs) - 5 :]
    size = w_in.shape[1]
    chips = count * (gathered.shape[0] // 4)
    n = rows.shape[1] // 2
    units = (slice(0, size), slice(size, 2 * size))
    act = [hidden_rows(blocks, 0, at) for at in units]
    slope = [hidden_rows(blocks, 1, at) for at in units]
    begin = first * (gathered.shape[0] // 4)
    out_rows = three(act[0], w_out[...], PLAIN) + three(act[1], w_out_other[...], PLAIN)
    in_rows = three(slope[0], w_in[...], RIGHT_T) + three(slope[1], w_in_other[...], RIGHT_T)
    rows[:chips, :n, :] = out_rows.reshape(chips, n, size)
    rows[:chips, n:, :] = in_rows.reshape(chips, n, size)
    if before:
        rows[chips:] = before[0][...]
    tokens, cotangent = (token_rows(gathered, begin, begin + chips, which) for which in range(2))
    for k in range(2):
        out_grad = three(act[1 - k], cotangent, LEFT_T)
        in_grad = three(tokens, slope[1 - k], LEFT_T)
        grads[2 * k][...] = out_grad + before[1 + 2 * k][...] if before else out_grad
        grads[2 * k + 1][...] = in_grad + before[2 + 2 * k][...] if before else in_grad


def send_kernel(tokens, cotangent, sent):
    n = tokens.shape[0]
    for k in range(sent.shape[0]):
        sent[k, :n] = tokens[...]
        sent[k, n:] = cotangent[...]


def collect_kernel(parts, output, input_grad):
    n = output.shape[0]
    output[...] = jnp.sum(parts[:, :n], axis=0)
    input_grad[...] = jnp.sum(parts[:, n:], axis=0)


class Plan:
    def __init__(self, rows, cols):
        self.rows, self.cols = rows, cols

    def flat(self, row, col):
        return row * self.cols + col

    def steps(self, core, col):
        near = 1 if (col + core) % 2 == 0 else -1
        far = 2 if (col // 2 + core) % 2 == 0 else -2
        return near, -near, far

    def planes(self):
        return [
            [
                self.flat(2 * chip + core, col)
                for step in (*self.steps(core, col), 0)
                for chip in range((col + step) % 4, self.rows // 2, 4)
            ]
            for core in range(2)
            for col in range(self.cols)
        ]

    def swap(self, k):
        return [
            (self.flat(row, col), self.flat(row, (col + self.steps(row % 2, col)[k]) % self.cols))
            for row in range(self.rows)
            for col in range(self.cols)
        ]

    def quarter(self, core, col):
        return (col // 4 - core) % 4

    def pairs(self, mates):
        groups = []
        for row in range(self.rows):
            for col in range(self.cols):
                at = self.quarter(row % 2, col)
                if mates and at % 2 == 0:
                    groups.append([self.flat(row, col), self.flat(row, (col + 4) % self.cols)])
                if not mates and at < 2:
                    step = 4 if at == 1 else -4
                    groups.append([self.flat(row, col), self.flat(row, (col + step) % self.cols)])
        return groups


def solution(mesh):
    rows, cols = mesh.shape["row"], mesh.shape["col"]
    plan = Plan(rows, cols)
    planes = plan.planes()
    swaps = [plan.swap(k) for k in range(3)]
    core_perm = [(row, row ^ 1) for row in range(rows)]
    across, mates = plan.pairs(False), plan.pairs(True)

    def local(tokens, weight_in, weight_out, cotangent):
        n, d = tokens.shape
        h = weight_in.shape[1]
        chips = rows // 2
        block = (2, 2, chips // 8 * n, 2 * h)
        at = ((lax.axis_index("col") >> 2) - (lax.axis_index("row") & 1)) & 3
        keep = at >> 1

        sent = kernel_call(send_kernel, [(chips, 2 * n, d)], (tokens, cotangent))[0]
        sent, weight_in, weight_out = lax.optimization_barrier((sent, weight_in, weight_out))
        weight_in_other = lax.ppermute(weight_in, "row", core_perm)
        weight_out_other = lax.ppermute(weight_out, "row", core_perm)
        gathered = lax.all_to_all(sent, BOTH, 0, 0, tiled=True, axis_index_groups=planes)
        weights = (weight_in, weight_in_other, weight_out, weight_out_other)

        away = kernel_call(lambda *refs: sums_kernel(0, *refs), [block] * 3, (gathered, *weights))
        away = [lax.ppermute(value, BOTH, perm) for value, perm in zip(away, swaps)]
        own = kernel_call(lambda *refs: sums_kernel(3, *refs), [block], (gathered, *weights))[0]
        total = own + away[0] + away[1] + away[2]

        def swap(value, groups, first):
            got = lax.all_gather(value, BOTH, axis=0, axis_index_groups=groups)
            return jnp.where(first == 0, got[1], got[0])

        kept = lax.dynamic_index_in_dim(total, keep, 0, keepdims=False)
        given = lax.dynamic_index_in_dim(total, 1 - keep, 0, keepdims=False)
        kept = kept + swap(given, across, keep)
        kept = kept + swap(kept, mates, at & 1)

        pre, grad = kept[0], kept[1]
        hidden = jnp.stack([gelu_value(pre), grad * gelu_slope(pre)])
        own = lax.all_gather(hidden, BOTH, axis=0, axis_index_groups=across)
        blocks = [lax.ppermute(own, BOTH, perm) for perm in swaps] + [own]

        square = [(d, h)] * 4
        early = kernel_call(
            lambda *refs: back_kernel(2, 2, *refs), [(chips // 2, 2 * n, d)] + square, (gathered, *weights, *blocks[2:])
        )
        parts, *grads = kernel_call(
            lambda *refs: back_kernel(0, 2, *refs),
            [(chips, 2 * n, d)] + square,
            (gathered, *weights, *blocks[:2], *early),
            far=True,
        )
        parts = lax.all_to_all(parts, BOTH, 0, 0, tiled=True, axis_index_groups=planes)
        weight_out_grad = grads[2] + lax.ppermute(grads[0], "row", core_perm)
        weight_in_grad = grads[3] + lax.ppermute(grads[1], "row", core_perm)
        output, input_grad = kernel_call(collect_kernel, [(n, d)] * 2, (parts,))
        return (output, input_grad, weight_in_grad, weight_out_grad)

    placed = (P("row", "col"), P("col", "row"), P("row", "col"), P("row", "col"))
    return jax.shard_map(
        local,
        mesh=mesh,
        in_specs=placed,
        out_specs=(P("row", "col"), P("row", "col"), P("col", "row"), P("row", "col")),
        check_vma=False,
    )
```

time: 425 us -> 144 us (0.34)
  waiting for transfers between devices: 278 us -> 31.2 us
  blocking collectives: 115 us -> 43.1 us
  starting transfers between devices: 0.16 us -> 51.4 us
  matrix products: 13.7 us -> 0 us
  between operations: 13.8 us -> 0.85 us
  Pallas kernels: 0 us -> 10.1 us
    reduce_scatter x4 -> x0, waiting for transfers between devices: 278 us -> none  [the longest x1 105 us: local(): lax.psum_scatter(product(act_all, weight_out), 'row', scatter_dimension=0...]
    all_gather x4 -> x3, blocking collectives: 115 us -> 43.1 us  [the longest x2 30.4 us: swap(): got = lax.all_gather(value, BOTH, axis=0, axis_index_groups=groups)]
    ppermute x0 -> x10, starting transfers between devices: none -> 36.9 us  [the longest x3 15.2 us: local(): away = [lax.ppermute(value, BOTH, perm) for value, perm in zip(away, swaps)]]
    ppermute x0 -> x10, waiting for transfers between devices: none -> 21.3 us  [the longest x3 11.1 us: local(): away = [lax.ppermute(value, BOTH, perm) for value, perm in zip(away, swaps)]]
    all_to_all x0 -> x2, starting transfers between devices: none -> 14.5 us  [the longest x1 8.73 us: local(): lax.all_to_all(sent, BOTH, 0, 0, tiled=True, axis_index_groups=planes)]
    dot_general x6 -> x0, matrix products: 13.7 us -> none  [the longest x2 5.02 us: product(): jnp.dot(left, right, precision=lax.Precision.HIGHEST, preferred_element_t...]
    pallas_call x0 -> x6, Pallas kernels: none -> 10.1 us  [kernel_call(): pl.pallas_call(body, out_shape=out, in_specs=[VMEM] * len(args), out_spec...]
    all_to_all x0 -> x2, waiting for transfers between devices: none -> 9.81 us  [the longest x1 5.53 us: local(): lax.all_to_all(sent, BOTH, 0, 0, tiled=True, axis_index_groups=planes)]
  transfers between devices with their start and end apart: 4 -> 12, of which waited for: 4 -> 7; matrix products, arithmetic and copies ran while one was open for 2% -> 1% of each run, Pallas kernels for 0% -> 2%
where the time goes in v3:
time: 144 us; the launch traced here: 141 us
  starting transfers between devices  51.4 us (36%)
  blocking collectives  43.1 us (30%)
  waiting for transfers between devices  31.2 us (22%)
  Pallas kernels  10.1 us (7%)
  other arithmetic  3.21 us (2%)
  local copies, waits for them, and re-layouts  1.51 us (1%)
    all_gather x2, blocking collectives, swap(): got = lax.all_gather(value, BOTH, axis=0, axis_index_groups=groups)  30.4 us
    ppermute x3, starting transfers between devices, local(): away = [lax.ppermute(value, BOTH, perm) for value, perm in zip(away, swaps)]  15.2 us
    ppermute x3, starting transfers between devices, local(): blocks = [lax.ppermute(own, BOTH, perm) for perm in swaps] + [own]  13 us
    all_gather x1, blocking collectives, local(): own = lax.all_gather(hidden, BOTH, axis=0, axis_index_groups=across)  12.8 us
    ppermute x3, waiting for transfers between devices, local(): away = [lax.ppermute(value, BOTH, perm) for value, perm in zip(away, swaps)]  11.1 us
    pallas_call x6, Pallas kernels, kernel_call(): pl.pallas_call(body, out_shape=out, in_specs=[VMEM] * len(args), out_spec...  10.1 us
    all_to_all x1, starting transfers between devices, local(): lax.all_to_all(sent, BOTH, 0, 0, tiled=True, axis_index_groups=planes)  8.73 us
    ppermute x3, waiting for transfers between devices, local(): blocks = [lax.ppermute(own, BOTH, perm) for perm in swaps] + [own]  7.77 us
  transfers between devices with their start and end apart: 12, of which 7 were waited for; matrix products, arithmetic and copies ran while one was open for 1% of the time, Pallas kernels for 2%

profile of v3, /device:TPU:6, one launch (start us, length us, event | category | flops | bytes accessed | tf_op | source)
XLA Modules:
  0.0 141.3 jit_solution(3076906460999949778)
XLA Ops:
  0.6 0.0 copy-start.2
  0.6 0.7 copy-done.2
  1.4 0.0 copy-start.3
  1.4 0.7 copy-done.3
  2.1 0.9 shard_map.75
  3.0 0.0 copy-start
  3.0 8.7 %all-to-all-start = ((f32[16,32,384]{2,1,0:T(8,128)}), f32[16,32,384]{2,1,0:T(8,128)S(1)}, u32[]{:S(2)}, u32[]{:S(2)}) async-start(f32[16,32,384]{2,1,0:T(8,128)} %shard_map.75), calls=%async_computation | async-start | bytes 1572864 | tf_op jit(solution)/shard_map/all_to_all | solution.py:179
  11.8 0.0 copy-done
  11.8 1.9 %collective-permute-start = (f32[384,384]{1,0:T(8,128)S(1)}, f32[384,384]{1,0:T(8,128)S(1)}, u32[]{:S(2)}, u32[]{:S(2)}) collective-permute-start(f32[384,384]{1,0:T(8,128)S(1)} %copy-done), channel_id=1, source_target_pairs={{0,16},{16,0},{32,48},{48,32},{64,80},{80,64},{96,112},{112,96},{1... | collective-permute-start | bytes 1769480 | tf_op jit(solution)/shard_map/ppermute | solution.py:177
  13.7 0.0 copy-done.1
  13.7 2.4 %collective-permute-start.1 = (f32[384,384]{1,0:T(8,128)S(1)}, f32[384,384]{1,0:T(8,128)S(1)}, u32[]{:S(2)}, u32[]{:S(2)}) collective-permute-start(f32[384,384]{1,0:T(8,128)S(1)} %copy-done.1), channel_id=1, source_target_pairs={{0,16},{16,0},{32,48},{48,32},{64,80},{80,64},{96,112},{112,96},{1... | collective-permute-start | bytes 1769480 | tf_op jit(solution)/shard_map/ppermute | solution.py:178
  16.1 0.0 collective-permute-done.refs_2_
  16.1 1.6 %collective-permute-done.1.refs_4_ = f32[384,384]{1,0:T(8,128)S(1)} collective-permute-done((f32[384,384]{1,0:T(8,128)S(1)}, f32[384,384]{1,0:T(8,128)S(1)}, u32[]{:S(2)}, u32[]{:S(2)}) %collective-permute-start.1) | collective-permute-done | bytes 589856 | tf_op jit(solution)/shard_map/ppermute | solution.py:178
  17.7 5.5 %all-to-all-done.refs_0_ = f32[16,32,384]{2,1,0:T(8,128)S(1)} async-done(((f32[16,32,384]{2,1,0:T(8,128)}), f32[16,32,384]{2,1,0:T(8,128)S(1)}, u32[]{:S(2)}, u32[]{:S(2)}) %all-to-all-start) | async-done | bytes 786464 | tf_op jit(solution)/shard_map/all_to_all | solution.py:179
  23.3 2.2 %shard_map.77 = (f32[2,2,32,768]{3,2,1,0:T(8,128)}, f32[2,2,32,768]{3,2,1,0:T(8,128)}, f32[2,2,32,768]{3,2,1,0:T(8,128)S(1)}) custom-call(f32[16,32,384]{2,1,0:T(8,128)S(1)} %all-to-all-done.refs_0_, f32[384,384]{1,0:T(8,128)S(1)} %copy-done, f32[384,384]{1,0:T(8,128)S(1)} %collective-permute-done.refs_2_, f32[384,384]{1,0:T(8,128)S(1)} %copy-done.1, ...), custom_call_target="tpu_custom_call" | custom-call | flops 1000 | bytes 1000 | tf_op jit(solution)/shard_map/pallas_call | solution.py:42
  25.5 2.7 %collective-permute-start.2 = (f32[2,2,32,768]{3,2,1,0:T(8,128)}, f32[2,2,32,768]{3,2,1,0:T(8,128)}, u32[]{:S(2)}, u32[]{:S(2)}) collective-permute-start(f32[2,2,32,768]{3,2,1,0:T(8,128)} %get-tuple-element.25), channel_id=1, source_target_pairs={{0,1},{1,0},{2,3},{3,2},{4,5},{5,4},{6,7},{7,6},{8,9},{9,8},{10,11... | collective-permute-start | bytes 1179656 | tf_op jit(solution)/shard_map/ppermute | solution.py:183
  28.2 10.6 %collective-permute-start.3 = (f32[2,2,32,768]{3,2,1,0:T(8,128)}, f32[2,2,32,768]{3,2,1,0:T(8,128)}, u32[]{:S(2)}, u32[]{:S(2)}) collective-permute-start(f32[2,2,32,768]{3,2,1,0:T(8,128)} %get-tuple-element.26), channel_id=1, source_target_pairs={{0,15},{1,2},{2,1},{3,4},{4,3},{5,6},{6,5},{7,8},{8,7},{9,10},{10,... | collective-permute-start | bytes 1179656 | tf_op jit(solution)/shard_map/ppermute | solution.py:183
  38.8 1.9 %collective-permute-start.4 = (f32[2,2,32,768]{3,2,1,0:T(8,128)S(1)}, f32[2,2,32,768]{3,2,1,0:T(8,128)}, u32[]{:S(2)}, u32[]{:S(2)}) collective-permute-start(f32[2,2,32,768]{3,2,1,0:T(8,128)S(1)} %get-tuple-element.27), channel_id=1, source_target_pairs={{0,2},{1,3},{2,0},{3,1},{4,6},{5,7},{6,4},{7,5},{8,10},{9,11},{10,... | collective-permute-start | bytes 1179656 | tf_op jit(solution)/shard_map/ppermute | solution.py:183
  40.8 1.0 shard_map.76
  41.8 0.0 collective-permute-done.2
  41.8 10.2 %collective-permute-done.3 = f32[2,2,32,768]{3,2,1,0:T(8,128)} collective-permute-done((f32[2,2,32,768]{3,2,1,0:T(8,128)}, f32[2,2,32,768]{3,2,1,0:T(8,128)}, u32[]{:S(2)}, u32[]{:S(2)}) %collective-permute-start.3) | collective-permute-done | bytes 393248 | tf_op jit(solution)/shard_map/ppermute | solution.py:183
  52.0 0.8 collective-permute-done.4
  52.8 1.3 add_add_fusion
  54.2 16.6 %all_gather.14 = f32[2,2,32,768]{3,2,1,0:T(8,128)S(1)} all-gather(f32[1,2,32,768]{3,2,1,0:T(8,128)S(1)} %constant_dynamic-slice_fusion), channel_id=1, replica_groups={{0,12},{1,13},{2,14},{3,15},{4,8},{5,9},{6,10},{7,11},{20,16},{21,17},{..., dimensions={0}, use_global_device_ids=true | all-gather | bytes 589824 | tf_op jit(solution)/shard_map/all_gather | solution.py:188
  70.8 13.8 %all_gather.15 = f32[2,2,32,768]{3,2,1,0:T(8,128)S(1)} all-gather(f32[1,2,32,768]{3,2,1,0:T(8,128)S(1)} %fusion.1), channel_id=1, replica_groups={{0,4},{1,5},{2,6},{3,7},{8,12},{9,13},{10,14},{11,15},{20,24},{21,25},{..., dimensions={0}, use_global_device_ids=true | all-gather | bytes 589824 | tf_op jit(solution)/shard_map/all_gather | solution.py:188
  84.7 0.1 multiply_multiply_fusion.1
  84.7 12.8 %all-gather = f32[4,32,768]{2,1,0:T(8,128)S(1)} all-gather(f32[2,32,768]{2,1,0:T(8,128)S(1)} %pad_maximum_fusion), channel_id=2, replica_groups={{0,12},{1,13},{2,14},{3,15},{4,8},{5,9},{6,10},{7,11},{20,16},{21,17},{..., dimensions={0}, use_global_device_ids=true | all-gather | bytes 589824 | tf_op jit(solution)/shard_map/all_gather | solution.py:198
  97.5 7.0 %collective-permute-start.7 = (f32[2,2,32,768]{3,2,1,0:T(8,128)S(1)}, f32[2,2,32,768]{3,2,1,0:T(8,128)S(1)}, u32[]{:S(2)}, u32[]{:S(2)}) collective-permute-start(f32[2,2,32,768]{3,2,1,0:T(8,128)S(1)} %bitcast.17), channel_id=1, source_target_pairs={{0,2},{1,3},{2,0},{3,1},{4,6},{5,7},{6,4},{7,5},{8,10},{9,11},{10,... | collective-permute-start | bytes 1179656 | tf_op jit(solution)/shard_map/ppermute | solution.py:199
  104.5 4.1 %collective-permute-start.6 = (f32[2,2,32,768]{3,2,1,0:T(8,128)S(1)}, f32[2,2,32,768]{3,2,1,0:T(8,128)S(1)}, u32[]{:S(2)}, u32[]{:S(2)}) collective-permute-start(f32[2,2,32,768]{3,2,1,0:T(8,128)S(1)} %bitcast.18), channel_id=1, source_target_pairs={{0,15},{1,2},{2,1},{3,4},{4,3},{5,6},{6,5},{7,8},{8,7},{9,10},{10,... | collective-permute-start | bytes 1179656 | tf_op jit(solution)/shard_map/ppermute | solution.py:199
  108.6 1.9 %collective-permute-start.5 = (f32[2,2,32,768]{3,2,1,0:T(8,128)S(1)}, f32[2,2,32,768]{3,2,1,0:T(8,128)S(1)}, u32[]{:S(2)}, u32[]{:S(2)}) collective-permute-start(f32[2,2,32,768]{3,2,1,0:T(8,128)S(1)} %bitcast.19), channel_id=1, source_target_pairs={{0,1},{1,0},{2,3},{3,2},{4,5},{5,4},{6,7},{7,6},{8,9},{9,8},{10,11... | collective-permute-start | bytes 1179656 | tf_op jit(solution)/shard_map/ppermute | solution.py:199
  110.6 7.8 %collective-permute-done.7.refs_5_ = f32[2,2,32,768]{3,2,1,0:T(8,128)S(1)} collective-permute-done((f32[2,2,32,768]{3,2,1,0:T(8,128)S(1)}, f32[2,2,32,768]{3,2,1,0:T(8,128)S(1)}, u32[]{:S(2)}, u32[]{:S(2)}) %collective-permute-start.7) | collective-permute-done | bytes 393248 | tf_op jit(solution)/shard_map/ppermute | solution.py:199
  118.3 2.0 %shard_map.78 = (f32[8,32,384]{2,1,0:T(8,128)S(1)}, f32[384,384]{1,0:T(8,128)S(1)}, f32[384,384]{1,0:T(8,128)S(1)}, f32[384,384]{1,0:T(8,128)S(1)}, f32[384,384]{1,0:T(8,128)S(1)}) custom-call(f32[16,32,384]{2,1,0:T(8,128)S(1)} %all-to-all-done.refs_0_, f32[384,384]{1,0:T(8,128)S(1)} %copy-done, f32[384,384]{1,0:T(8,128)S(1)} %collective-permute-done.refs_2_, ...), custom_call_target="tpu_custom_call" | custom-call | flops 1000 | bytes 1000 | tf_op jit(solution)/shard_map/pallas_call | solution.py:42
  120.3 0.0 collective-permute-done.6.refs_6_
  120.3 0.0 collective-permute-done.5.refs_5_
  120.3 3.3 %shard_map.79 = (f32[16,32,384]{2,1,0:T(8,128)}, f32[384,384]{1,0:T(8,128)}, f32[384,384]{1,0:T(8,128)}, f32[384,384]{1,0:T(8,128)}, f32[384,384]{1,0:T(8,128)}) custom-call(f32[16,32,384]{2,1,0:T(8,128)S(1)} %all-to-all-done.refs_0_, f32[384,384]{1,0:T(8,128)S(1)} %copy-done, f32[384,384]{1,0:T(8,128)S(1)} %collective-permute-done.refs_2_, ...), custom_call_target="tpu_custom_call" | custom-call | flops 1000 | bytes 1000 | tf_op jit(solution)/shard_map/pallas_call | solution.py:42
  123.6 5.8 %all-to-all-start.1 = ((f32[16,32,384]{2,1,0:T(8,128)}), f32[16,32,384]{2,1,0:T(8,128)S(1)}, u32[]{:S(2)}, u32[]{:S(2)}) async-start(f32[16,32,384]{2,1,0:T(8,128)} %get-tuple-element.33), calls=%async_computation.1 | async-start | bytes 1572864 | tf_op jit(solution)/shard_map/all_to_all | solution.py:211
  129.4 0.0 copy-done.6
  129.4 1.9 %collective-permute-start.8 = (f32[384,384]{1,0:T(8,128)S(1)}, f32[384,384]{1,0:T(8,128)S(1)}, u32[]{:S(2)}, u32[]{:S(2)}) collective-permute-start(f32[384,384]{1,0:T(8,128)S(1)} %copy-done.6), channel_id=1, source_target_pairs={{0,16},{16,0},{32,48},{48,32},{64,80},{80,64},{96,112},{112,96},{1... | collective-permute-start | bytes 1769480 | tf_op jit(solution)/shard_map/ppermute | solution.py:213
  131.3 2.4 %collective-permute-start.9 = (f32[384,384]{1,0:T(8,128)}, f32[384,384]{1,0:T(8,128)S(1)}, u32[]{:S(2)}, u32[]{:S(2)}) collective-permute-start(f32[384,384]{1,0:T(8,128)} %get-tuple-element.39), channel_id=1, source_target_pairs={{0,16},{16,0},{32,48},{48,32},{64,80},{80,64},{96,112},{112,96},{1... | collective-permute-start | bytes 1769480 | tf_op jit(solution)/shard_map/ppermute | solution.py:212
  133.7 0.0 collective-permute-done.8
  133.7 0.0 copy-done.5
  133.7 0.0 copy-start.4
  133.7 0.9 add.51
  134.6 0.9 collective-permute-done.9
  135.5 0.0 copy-done.4
  135.5 0.9 add.52
  136.4 4.3 %all-to-all-done.1.parts = f32[16,32,384]{2,1,0:T(8,128)S(1)} async-done(((f32[16,32,384]{2,1,0:T(8,128)}), f32[16,32,384]{2,1,0:T(8,128)S(1)}, u32[]{:S(2)}, u32[]{:S(2)}) %all-to-all-start.1) | async-done | bytes 786464 | tf_op jit(solution)/shard_map/all_to_all | solution.py:211
  140.7 0.7 shard_map.80
  (7 shorter events, 0.1 us)
Async XLA Ops:
  0.6 0.7 copy-start.2
  1.4 0.7 copy-start.3
  3.0 8.7 %copy-start = (f32[384,384]{1,0:T(8,128)S(1)}, f32[384,384]{1,0:T(8,128)}, u32[]{:S(2)}) copy-start(f32[384,384]{1,0:T(8,128)} %refs_1_.3) | copy-start | bytes 1769476
  3.0 10.7 %copy-start.1 = (f32[384,384]{1,0:T(8,128)S(1)}, f32[384,384]{1,0:T(8,128)}, u32[]{:S(2)}) copy-start(f32[384,384]{1,0:T(8,128)} %refs_3_.3) | copy-start | bytes 1769476
  3.0 20.2 %all-to-all-start = ((f32[16,32,384]{2,1,0:T(8,128)}), f32[16,32,384]{2,1,0:T(8,128)S(1)}, u32[]{:S(2)}, u32[]{:S(2)}) async-start(f32[16,32,384]{2,1,0:T(8,128)} %shard_map.75), calls=%async_computation | async-start | bytes 1572864 | tf_op jit(solution)/shard_map/all_to_all | solution.py:179
  11.8 4.4 %collective-permute-start = (f32[384,384]{1,0:T(8,128)S(1)}, f32[384,384]{1,0:T(8,128)S(1)}, u32[]{:S(2)}, u32[]{:S(2)}) collective-permute-start(f32[384,384]{1,0:T(8,128)S(1)} %copy-done), channel_id=1, source_target_pairs={{0,16},{16,0},{32,48},{48,32},{64,80},{80,64},{96,112},{112,96},{1... | collective-permute-start | bytes 1769480 | tf_op jit(solution)/shard_map/ppermute | solution.py:177
  13.7 4.0 %collective-permute-start.1 = (f32[384,384]{1,0:T(8,128)S(1)}, f32[384,384]{1,0:T(8,128)S(1)}, u32[]{:S(2)}, u32[]{:S(2)}) collective-permute-start(f32[384,384]{1,0:T(8,128)S(1)} %copy-done.1), channel_id=1, source_target_pairs={{0,16},{16,0},{32,48},{48,32},{64,80},{80,64},{96,112},{112,96},{1... | collective-permute-start | bytes 1769480 | tf_op jit(solution)/shard_map/ppermute | solution.py:178
  25.5 16.3 %collective-permute-start.2 = (f32[2,2,32,768]{3,2,1,0:T(8,128)}, f32[2,2,32,768]{3,2,1,0:T(8,128)}, u32[]{:S(2)}, u32[]{:S(2)}) collective-permute-start(f32[2,2,32,768]{3,2,1,0:T(8,128)} %get-tuple-element.25), channel_id=1, source_target_pairs={{0,1},{1,0},{2,3},{3,2},{4,5},{5,4},{6,7},{7,6},{8,9},{9,8},{10,11... | collective-permute-start | bytes 1179656 | tf_op jit(solution)/shard_map/ppermute | solution.py:183
  28.2 23.9 %collective-permute-start.3 = (f32[2,2,32,768]{3,2,1,0:T(8,128)}, f32[2,2,32,768]{3,2,1,0:T(8,128)}, u32[]{:S(2)}, u32[]{:S(2)}) collective-permute-start(f32[2,2,32,768]{3,2,1,0:T(8,128)} %get-tuple-element.26), channel_id=1, source_target_pairs={{0,15},{1,2},{2,1},{3,4},{4,3},{5,6},{6,5},{7,8},{8,7},{9,10},{10,... | collective-permute-start | bytes 1179656 | tf_op jit(solution)/shard_map/ppermute | solution.py:183
  38.8 14.0 %collective-permute-start.4 = (f32[2,2,32,768]{3,2,1,0:T(8,128)S(1)}, f32[2,2,32,768]{3,2,1,0:T(8,128)}, u32[]{:S(2)}, u32[]{:S(2)}) collective-permute-start(f32[2,2,32,768]{3,2,1,0:T(8,128)S(1)} %get-tuple-element.27), channel_id=1, source_target_pairs={{0,2},{1,3},{2,0},{3,1},{4,6},{5,7},{6,4},{7,5},{8,10},{9,11},{10,... | collective-permute-start | bytes 1179656 | tf_op jit(solution)/shard_map/ppermute | solution.py:183
  97.5 20.8 %collective-permute-start.7 = (f32[2,2,32,768]{3,2,1,0:T(8,128)S(1)}, f32[2,2,32,768]{3,2,1,0:T(8,128)S(1)}, u32[]{:S(2)}, u32[]{:S(2)}) collective-permute-start(f32[2,2,32,768]{3,2,1,0:T(8,128)S(1)} %bitcast.17), channel_id=1, source_target_pairs={{0,2},{1,3},{2,0},{3,1},{4,6},{5,7},{6,4},{7,5},{8,10},{9,11},{10,... | collective-permute-start | bytes 1179656 | tf_op jit(solution)/shard_map/ppermute | solution.py:199
  104.5 15.8 %collective-permute-start.6 = (f32[2,2,32,768]{3,2,1,0:T(8,128)S(1)}, f32[2,2,32,768]{3,2,1,0:T(8,128)S(1)}, u32[]{:S(2)}, u32[]{:S(2)}) collective-permute-start(f32[2,2,32,768]{3,2,1,0:T(8,128)S(1)} %bitcast.18), channel_id=1, source_target_pairs={{0,15},{1,2},{2,1},{3,4},{4,3},{5,6},{6,5},{7,8},{8,7},{9,10},{10,... | collective-permute-start | bytes 1179656 | tf_op jit(solution)/shard_map/ppermute | solution.py:199
  108.6 11.7 %collective-permute-start.5 = (f32[2,2,32,768]{3,2,1,0:T(8,128)S(1)}, f32[2,2,32,768]{3,2,1,0:T(8,128)S(1)}, u32[]{:S(2)}, u32[]{:S(2)}) collective-permute-start(f32[2,2,32,768]{3,2,1,0:T(8,128)S(1)} %bitcast.19), channel_id=1, source_target_pairs={{0,1},{1,0},{2,3},{3,2},{4,5},{5,4},{6,7},{7,6},{8,9},{9,8},{10,11... | collective-permute-start | bytes 1179656 | tf_op jit(solution)/shard_map/ppermute | solution.py:199
  123.6 5.8 %copy-start.6 = (f32[384,384]{1,0:T(8,128)S(1)}, f32[384,384]{1,0:T(8,128)}, u32[]{:S(2)}) copy-start(f32[384,384]{1,0:T(8,128)} %get-tuple-element.37) | copy-start | bytes 1769476
  123.6 10.1 %copy-start.5 = (f32[384,384]{1,0:T(8,128)S(1)}, f32[384,384]{1,0:T(8,128)}, u32[]{:S(2)}) copy-start(f32[384,384]{1,0:T(8,128)} %get-tuple-element.36) | copy-start | bytes 1769476
  123.6 17.1 %all-to-all-start.1 = ((f32[16,32,384]{2,1,0:T(8,128)}), f32[16,32,384]{2,1,0:T(8,128)S(1)}, u32[]{:S(2)}, u32[]{:S(2)}) async-start(f32[16,32,384]{2,1,0:T(8,128)} %get-tuple-element.33), calls=%async_computation.1 | async-start | bytes 1572864 | tf_op jit(solution)/shard_map/all_to_all | solution.py:211
  129.4 4.3 %collective-permute-start.8 = (f32[384,384]{1,0:T(8,128)S(1)}, f32[384,384]{1,0:T(8,128)S(1)}, u32[]{:S(2)}, u32[]{:S(2)}) collective-permute-start(f32[384,384]{1,0:T(8,128)S(1)} %copy-done.6), channel_id=1, source_target_pairs={{0,16},{16,0},{32,48},{48,32},{64,80},{80,64},{96,112},{112,96},{1... | collective-permute-start | bytes 1769480 | tf_op jit(solution)/shard_map/ppermute | solution.py:213
  131.3 4.2 %collective-permute-start.9 = (f32[384,384]{1,0:T(8,128)}, f32[384,384]{1,0:T(8,128)S(1)}, u32[]{:S(2)}, u32[]{:S(2)}) collective-permute-start(f32[384,384]{1,0:T(8,128)} %get-tuple-element.39), channel_id=1, source_target_pairs={{0,16},{16,0},{32,48},{48,32},{64,80},{80,64},{96,112},{112,96},{1... | collective-permute-start | bytes 1769480 | tf_op jit(solution)/shard_map/ppermute | solution.py:212
  133.7 1.8 %copy-start.4 = (f32[384,384]{1,0:T(8,128)S(1)}, f32[384,384]{1,0:T(8,128)}, u32[]{:S(2)}) copy-start(f32[384,384]{1,0:T(8,128)} %get-tuple-element.38) | copy-start | bytes 1769476

commit v4 on v3

v4 whole, which is shorter than its diff:
```python
import math

import jax
import jax.numpy as jnp
from jax import lax
from jax.experimental import pallas as pl
from jax.experimental.pallas import tpu as pltpu
from jax.sharding import PartitionSpec as P

BOTH = ("row", "col")
VMEM = pl.BlockSpec(memory_space=pltpu.VMEM)
SMEM = pl.BlockSpec(memory_space=pltpu.SMEM)
FAR = pl.BlockSpec(memory_space=pltpu.HBM)


def gelu_value(pre):
    return pre * 0.5 * (1.0 + jax.scipy.special.erf(pre / math.sqrt(2.0)))


def gelu_slope(pre):
    cumulative = 0.5 * (1.0 + jax.scipy.special.erf(pre / math.sqrt(2.0)))
    density = jnp.exp(-0.5 * pre * pre) / math.sqrt(2.0 * math.pi)
    return cumulative + pre * density


def split(value):
    high = value.astype(jnp.bfloat16)
    return high, (value - high.astype(jnp.float32)).astype(jnp.bfloat16)


def three(left, right, dims):
    def one(a, b):
        return lax.dot_general(a, b, (dims, ((), ())), preferred_element_type=jnp.float32)

    (lh, ll), (rh, rl) = left, right
    return one(lh, rh) + (one(lh, rl) + one(ll, rh))


def join_kernel(w_in, w_in_other, w_out, w_out_other, in_parts, out_parts):
    size = w_in.shape[1]
    for k, (v, w) in enumerate(((w_in, w_out), (w_in_other, w_out_other))):
        at = slice(k * size, (k + 1) * size)
        in_parts[0, :, at], in_parts[1, :, at] = split(v[...])
        out_parts[0, at, :], out_parts[1, at, :] = split(w[...])


PLAIN, RIGHT_T, LEFT_T = ((1,), (0,)), ((1,), (1,)), ((0,), (0,))


def kernel_call(body, out_shapes, args, kept_as=jnp.float32):
    out = [jax.ShapeDtypeStruct(shape, kept_as) for shape in out_shapes]
    return pl.pallas_call(
        body,
        out_shape=out,
        in_specs=[VMEM] * len(args),
        out_specs=[VMEM] * len(out),
        compiler_params=pltpu.CompilerParams(vmem_limit_bytes=9 * 2**20),
        cost_estimate=pl.CostEstimate(flops=1000, bytes_accessed=1000, transcendentals=0),
    )(*args)


def token_rows(gathered, first, last, which):
    n, d = gathered.shape[1] // 2, gathered.shape[2]
    return gathered[first:last, which * n : (which + 1) * n, :].reshape((last - first) * n, d)


def sums_kernel(first, gathered, w_in, w_out, *outs):
    chips = gathered.shape[0] // 4
    for which, (weight, dims) in enumerate(((w_in, PLAIN), (w_out, RIGHT_T))):
        rows = split(token_rows(gathered, first * chips, (first + len(outs)) * chips, which))
        term = three(rows, (weight[0], weight[1]), dims)
        block = term.shape[0] // len(outs) // 2
        for i, out in enumerate(outs):
            for part in range(2):
                start = (2 * i + part) * block
                out[part, which] = term[start : start + block]


def halves_kernel(keep, *refs):
    terms, (kept, given) = refs[:-2], refs[-2:]
    for out, half in ((kept, keep[0]), (given, 1 - keep[0])):
        total = terms[0][half]
        for term in terms[1:]:
            total = total + term[half]
        out[...] = total


def hidden_rows(blocks, which):
    return jnp.concatenate([block[part, which] for block in blocks for part in range(2)], axis=0)


def back_terms(first, count, gathered, w_in, w_out, blocks):
    size = gathered.shape[2]
    quarter = gathered.shape[0] // 4
    begin, end = first * quarter, (first + count) * quarter
    act, slope = split(hidden_rows(blocks, 0)), split(hidden_rows(blocks, 1))
    tokens, cotangent = (split(token_rows(gathered, begin, end, which)) for which in range(2))
    for k in range(2):
        at = slice((1 - k) * size, (2 - k) * size)
        yield three([v[:, at] for v in act], cotangent, LEFT_T)
        yield three(tokens, [v[:, at] for v in slope], LEFT_T)
    shape = (count * quarter, gathered.shape[1] // 2, size)
    yield three(act, (w_out[0], w_out[1]), PLAIN).reshape(shape)
    yield three(slope, (w_in[0], w_in[1]), RIGHT_T).reshape(shape)


def early_kernel(gathered, w_in, w_out, *refs):
    rows, *grads = refs[2:]
    n = rows.shape[1] // 2
    for k, term in enumerate(back_terms(2, 2, gathered, w_in, w_out, refs[:2])):
        if k < 4:
            grads[k][...] = term
        else:
            rows[:, (k - 4) * n : (k - 3) * n, :] = term


def late_kernel(gathered, w_in, w_out, *refs):
    blocks, (early_rows, *early), refs = refs[:2], refs[2:7], refs[7:]
    parts, grads, rows, scratch, done = refs[0], refs[1:5], refs[5], refs[6], refs[7]
    n = rows.shape[1] // 2
    chips = rows.shape[0] // 2
    copies = [pltpu.make_async_copy(scratch.at[k], grads[k], done.at[k]) for k in range(4)]
    copies.append(pltpu.make_async_copy(rows, parts, done.at[4]))
    rows[chips:] = early_rows[...]
    for k, term in enumerate(back_terms(0, 2, gathered, w_in, w_out, blocks)):
        if k < 4:
            scratch[k] = term + early[k][...]
            copies[k].start()
        else:
            rows[:chips, (k - 4) * n : (k - 3) * n, :] = term
    copies[4].start()
    for copy in copies:
        copy.wait()


def collect_kernel(parts, output, input_grad):
    n = output.shape[0]
    output[...] = jnp.sum(parts[:, :n], axis=0)
    input_grad[...] = jnp.sum(parts[:, n:], axis=0)


class Plan:
    def __init__(self, rows, cols):
        self.rows, self.cols = rows, cols

    def flat(self, row, col):
        return row * self.cols + col

    def steps(self, core, col):
        near = 1 if (col + core) % 2 == 0 else -1
        far = 2 if (col // 2 + core) % 2 == 0 else -2
        return near, -near, far

    def planes(self):
        return [
            [
                self.flat(2 * chip + core, col)
                for step in (*self.steps(core, col), 0)
                for chip in range((col + step) % 4, self.rows // 2, 4)
            ]
            for core in range(2)
            for col in range(self.cols)
        ]

    def swap(self, k):
        return [
            (self.flat(row, col), self.flat(row, (col + self.steps(row % 2, col)[k]) % self.cols))
            for row in range(self.rows)
            for col in range(self.cols)
        ]

    def quarter(self, core, col):
        return (col // 4 - core) % 4

    def pairs(self, mates):
        groups = []
        for row in range(self.rows):
            for col in range(self.cols):
                at = self.quarter(row % 2, col)
                if mates and at % 2 == 0:
                    groups.append([self.flat(row, col), self.flat(row, (col + 4) % self.cols)])
                if not mates and at < 2:
                    step = 4 if at == 1 else -4
                    groups.append([self.flat(row, col), self.flat(row, (col + step) % self.cols)])
        return groups


def solution(mesh):
    rows, cols = mesh.shape["row"], mesh.shape["col"]
    plan = Plan(rows, cols)
    planes = plan.planes()
    swaps = [plan.swap(k) for k in range(3)]
    core_perm = [(row, row ^ 1) for row in range(rows)]
    across, mates = plan.pairs(False), plan.pairs(True)

    def local(tokens, weight_in, weight_out, cotangent):
        n, d = tokens.shape
        h = weight_in.shape[1]
        chips = rows // 2
        block = (2, 2, chips // 8 * n, 2 * h)
        at = ((lax.axis_index("col") >> 2) - (lax.axis_index("row") & 1)) & 3
        keep = at >> 1

        sent = jnp.broadcast_to(jnp.concatenate([tokens, cotangent], axis=0)[None], (chips, 2 * n, d))
        sent, weight_in, weight_out = lax.optimization_barrier((sent, weight_in, weight_out))
        weight_in_other = lax.ppermute(weight_in, "row", core_perm)
        weight_out_other = lax.ppermute(weight_out, "row", core_perm)
        gathered = lax.all_to_all(sent, BOTH, 0, 0, tiled=True, axis_index_groups=planes)
        weights = kernel_call(
            join_kernel,
            [(2, d, 2 * h), (2, 2 * h, d)],
            (weight_in, weight_in_other, weight_out, weight_out_other),
            kept_as=jnp.bfloat16,
        )
        gathered, *weights = lax.optimization_barrier((gathered, *weights))

        away = kernel_call(lambda *refs: sums_kernel(0, *refs), [block] * 3, (gathered, *weights))
        away = [lax.ppermute(value, BOTH, perm) for value, perm in zip(away, swaps)]
        own = kernel_call(lambda *refs: sums_kernel(3, *refs), [block], (gathered, *weights))[0]
        kept, given = pl.pallas_call(
            halves_kernel,
            out_shape=[jax.ShapeDtypeStruct(block[1:], jnp.float32)] * 2,
            in_specs=[SMEM] + [VMEM] * 4,
            out_specs=[VMEM] * 2,
            compiler_params=pltpu.CompilerParams(vmem_limit_bytes=9 * 2**20),
            cost_estimate=pl.CostEstimate(flops=1000, bytes_accessed=1000, transcendentals=0),
        )(keep.astype(jnp.int32).reshape(1), own, *away)

        def swap(value, groups, first):
            got = lax.all_gather(value, BOTH, axis=0, axis_index_groups=groups)
            return jnp.where(first == 0, got[1], got[0])

        kept = kept + swap(given, across, keep)
        kept = kept + swap(kept, mates, at & 1)

        pre, grad = kept[0], kept[1]
        hidden = jnp.stack([gelu_value(pre), grad * gelu_slope(pre)])
        own = lax.all_gather(hidden, BOTH, axis=0, axis_index_groups=across)
        blocks = [lax.ppermute(own, BOTH, perm) for perm in swaps] + [own]

        square = [(d, h)] * 4
        early = kernel_call(early_kernel, [(chips // 2, 2 * n, d)] + square, (gathered, *weights, *blocks[2:]))
        parts, *grads = pl.pallas_call(
            late_kernel,
            out_shape=[pltpu.HBM(shape, jnp.float32) for shape in [(chips, 2 * n, d)] + square],
            in_specs=[VMEM] * 10,
            out_specs=[FAR] * 5,
            scratch_shapes=[
                pltpu.VMEM((chips, 2 * n, d), jnp.float32),
                pltpu.VMEM((4, d, h), jnp.float32),
                pltpu.SemaphoreType.DMA((5,)),
            ],
            compiler_params=pltpu.CompilerParams(vmem_limit_bytes=9 * 2**20),
            cost_estimate=pl.CostEstimate(flops=1000, bytes_accessed=1000, transcendentals=0),
        )(gathered, *weights, *blocks[:2], *early)
        parts = lax.all_to_all(parts, BOTH, 0, 0, tiled=True, axis_index_groups=planes)
        weight_out_grad = grads[2] + lax.ppermute(grads[0], "row", core_perm)
        weight_in_grad = grads[3] + lax.ppermute(grads[1], "row", core_perm)
        output, input_grad = kernel_call(collect_kernel, [(n, d)] * 2, (parts,))
        return (output, input_grad, weight_in_grad, weight_out_grad)

    placed = (P("row", "col"), P("col", "row"), P("row", "col"), P("row", "col"))
    return jax.shard_map(
        local,
        mesh=mesh,
        in_specs=placed,
        out_specs=(P("row", "col"), P("row", "col"), P("col", "row"), P("row", "col")),
        check_vma=False,
    )
```

time: 144 us -> 142 us (0.986); the launches traced: 141 us -> 141 us
  waiting for transfers between devices: 31.2 us -> 27.7 us
  starting transfers between devices: 51.4 us -> 53.4 us
  local copies, waits for them, and re-layouts: 1.51 us -> 3.11 us
    pallas_call x0 -> x2, Pallas kernels: none -> 4.14 us  [the longest x1 2.95 us: local(): pl.pallas_call(late_kernel, out_shape=[pltpu.HBM(shape, jnp.float32) for...]
    all_to_all x1, starting transfers between devices: 5.75 us -> 9.82 us  [local(): lax.all_to_all(parts, BOTH, 0, 0, tiled=True, axis_index_groups=planes)]
    pallas_call x6 -> x5, Pallas kernels: 10.1 us -> 6.07 us  [kernel_call(): pl.pallas_call(body, out_shape=out, in_specs=[VMEM] * len(args), out_spec...]
    all_to_all x1, waiting for transfers between devices: 5.53 us -> 2.94 us  [local(): lax.all_to_all(sent, BOTH, 0, 0, tiled=True, axis_index_groups=planes)]
    ppermute x3, starting transfers between devices: 13 us -> 11 us  [local(): blocks = [lax.ppermute(own, BOTH, perm) for perm in swaps] + [own]]
    ppermute x3, waiting for transfers between devices: 7.77 us -> 5.99 us  [local(): blocks = [lax.ppermute(own, BOTH, perm) for perm in swaps] + [own]]
  transfers between devices with their start and end apart: 12 -> 12, of which waited for: 7 -> 8; matrix products, arithmetic and copies ran while one was open for 1% -> 1% of each run, Pallas kernels for 2% -> 2%
where the time goes in v4:
time: 142 us; the launch traced here: 141 us
  starting transfers between devices  53.4 us (38%)
  blocking collectives  43 us (30%)
  waiting for transfers between devices  27.7 us (20%)
  Pallas kernels  10.2 us (7%)
  local copies, waits for them, and re-layouts  3.11 us (2%)
  other arithmetic  2.65 us (2%)
    all_gather x2, blocking collectives, swap(): got = lax.all_gather(value, BOTH, axis=0, axis_index_groups=groups)  29.7 us
    ppermute x3, starting transfers between devices, local(): away = [lax.ppermute(value, BOTH, perm) for value, perm in zip(away, swaps)]  15.2 us
    all_gather x1, blocking collectives, local(): own = lax.all_gather(hidden, BOTH, axis=0, axis_index_groups=across)  13.3 us
    ppermute x3, waiting for transfers between devices, local(): away = [lax.ppermute(value, BOTH, perm) for value, perm in zip(away, swaps)]  11.2 us
    ppermute x3, starting transfers between devices, local(): blocks = [lax.ppermute(own, BOTH, perm) for perm in swaps] + [own]  11 us
    all_to_all x1, starting transfers between devices, local(): lax.all_to_all(parts, BOTH, 0, 0, tiled=True, axis_index_groups=planes)  9.82 us
    all_to_all x1, starting transfers between devices, local(): lax.all_to_all(sent, BOTH, 0, 0, tiled=True, axis_index_groups=planes)  8.6 us
    pallas_call x5, Pallas kernels, kernel_call(): pl.pallas_call(body, out_shape=out, in_specs=[VMEM] * len(args), out_spec...  6.07 us
  transfers between devices with their start and end apart: 12, of which 8 were waited for; matrix products, arithmetic and copies ran while one was open for 1% of the time, Pallas kernels for 2%

profile of v4, /device:TPU:6, one launch (start us, length us, event | category | flops | bytes accessed | tf_op | source)
XLA Modules:
  0.0 140.9 jit_solution(2518232910693599293)
XLA Ops:
  0.6 0.8 pad_maximum_fusion.1
  1.4 0.0 copy-start
  1.4 0.0 copy-start.2
  1.4 1.0 broadcast_in_dim.2
  2.4 8.6 %all-to-all-start = ((f32[16,32,384]{2,1,0:T(8,128)}), f32[16,32,384]{2,1,0:T(8,128)S(1)}, u32[]{:S(2)}, u32[]{:S(2)}) async-start(f32[16,32,384]{2,1,0:T(8,128)} %broadcast_in_dim.2), calls=%async_computation | async-start | bytes 1572864 | tf_op jit(solution)/shard_map/all_to_all | solution.py:208
  11.0 0.0 copy-done
  11.0 1.9 %collective-permute-start = (f32[384,384]{1,0:T(8,128)S(1)}, f32[384,384]{1,0:T(8,128)S(1)}, u32[]{:S(2)}, u32[]{:S(2)}) collective-permute-start(f32[384,384]{1,0:T(8,128)S(1)} %copy-done), channel_id=1, source_target_pairs={{0,16},{16,0},{32,48},{48,32},{64,80},{80,64},{96,112},{112,96},{1... | collective-permute-start | bytes 1769480 | tf_op jit(solution)/shard_map/ppermute | solution.py:206
  12.9 0.0 copy-done.2
  12.9 2.4 %collective-permute-start.1 = (f32[384,384]{1,0:T(8,128)S(1)}, f32[384,384]{1,0:T(8,128)S(1)}, u32[]{:S(2)}, u32[]{:S(2)}) collective-permute-start(f32[384,384]{1,0:T(8,128)S(1)} %copy-done.2), channel_id=1, source_target_pairs={{0,16},{16,0},{32,48},{48,32},{64,80},{80,64},{96,112},{112,96},{1... | collective-permute-start | bytes 1769480 | tf_op jit(solution)/shard_map/ppermute | solution.py:207
  15.3 0.0 collective-permute-done.w_in_other
  15.3 1.6 %collective-permute-done.1.w_out_other = f32[384,384]{1,0:T(8,128)S(1)} collective-permute-done((f32[384,384]{1,0:T(8,128)S(1)}, f32[384,384]{1,0:T(8,128)S(1)}, u32[]{:S(2)}, u32[]{:S(2)}) %collective-permute-start.1) | collective-permute-done | bytes 589856 | tf_op jit(solution)/shard_map/ppermute | solution.py:207
  16.9 1.1 copy-done.1
  18.0 1.1 copy-done.3
  19.1 0.5 shard_map.75
  19.5 2.9 %all-to-all-done.refs_0_.gathered = f32[16,32,384]{2,1,0:T(8,128)S(1)} async-done(((f32[16,32,384]{2,1,0:T(8,128)}), f32[16,32,384]{2,1,0:T(8,128)S(1)}, u32[]{:S(2)}, u32[]{:S(2)}) %all-to-all-start) | async-done | bytes 786464 | tf_op jit(solution)/shard_map/all_to_all | solution.py:208
  22.5 2.2 %shard_map.77 = (f32[2,2,32,768]{3,2,1,0:T(8,128)}, f32[2,2,32,768]{3,2,1,0:T(8,128)}, f32[2,2,32,768]{3,2,1,0:T(8,128)}) custom-call(f32[16,32,384]{2,1,0:T(8,128)S(1)} %all-to-all-done.refs_0_.gathered, bf16[2,384,768]{2,1,0:T(8,128)(2,1)S(1)} %get-tuple-element.35.refs_1_.w_in, bf16[2,768,384]{2,1,0:T(8,128)(2,1)S(1)} %get-tuple-element.36.refs_2_.w_out), custom_call_target="tpu_custom_call" | custom-call | flops 1000 | bytes 1000 | tf_op jit(solution)/shard_map/pallas_call | solution.py:52
  24.6 2.7 %collective-permute-start.2 = (f32[2,2,32,768]{3,2,1,0:T(8,128)}, f32[2,2,32,768]{3,2,1,0:T(8,128)S(1)}, u32[]{:S(2)}, u32[]{:S(2)}) collective-permute-start(f32[2,2,32,768]{3,2,1,0:T(8,128)} %get-tuple-element.37), channel_id=1, source_target_pairs={{0,1},{1,0},{2,3},{3,2},{4,5},{5,4},{6,7},{7,6},{8,9},{9,8},{10,11... | collective-permute-start | bytes 1179656 | tf_op jit(solution)/shard_map/ppermute | solution.py:218
  27.3 10.6 %collective-permute-start.3 = (f32[2,2,32,768]{3,2,1,0:T(8,128)}, f32[2,2,32,768]{3,2,1,0:T(8,128)}, u32[]{:S(2)}, u32[]{:S(2)}) collective-permute-start(f32[2,2,32,768]{3,2,1,0:T(8,128)} %get-tuple-element.38), channel_id=1, source_target_pairs={{0,15},{1,2},{2,1},{3,4},{4,3},{5,6},{6,5},{7,8},{8,7},{9,10},{10,... | collective-permute-start | bytes 1179656 | tf_op jit(solution)/shard_map/ppermute | solution.py:218
  37.9 1.9 %collective-permute-start.4 = (f32[2,2,32,768]{3,2,1,0:T(8,128)}, f32[2,2,32,768]{3,2,1,0:T(8,128)}, u32[]{:S(2)}, u32[]{:S(2)}) collective-permute-start(f32[2,2,32,768]{3,2,1,0:T(8,128)} %get-tuple-element.39), channel_id=1, source_target_pairs={{0,2},{1,3},{2,0},{3,1},{4,6},{5,7},{6,4},{7,5},{8,10},{9,11},{10,... | collective-permute-start | bytes 1179656 | tf_op jit(solution)/shard_map/ppermute | solution.py:218
  39.9 0.9 shard_map.76.refs_0_
  40.8 0.0 collective-permute-done.2.refs_1_
  40.8 10.4 %collective-permute-done.3.refs_2_ = f32[2,2,32,768]{3,2,1,0:T(8,128)} collective-permute-done((f32[2,2,32,768]{3,2,1,0:T(8,128)}, f32[2,2,32,768]{3,2,1,0:T(8,128)}, u32[]{:S(2)}, u32[]{:S(2)}) %collective-permute-start.3) | collective-permute-done | bytes 393248 | tf_op jit(solution)/shard_map/ppermute | solution.py:218
  51.2 0.8 collective-permute-done.4.refs_3_
  52.0 1.2 shard_map.78
  53.2 14.5 %all-gather = f32[4,32,768]{2,1,0:T(8,128)S(1)} all-gather(f32[2,32,768]{2,1,0:T(8,128)S(1)} %get-tuple-element.41), channel_id=2, replica_groups={{0,12},{1,13},{2,14},{3,15},{4,8},{5,9},{6,10},{7,11},{20,16},{21,17},{..., dimensions={0}, use_global_device_ids=true | all-gather | bytes 589824 | tf_op jit(solution)/shard_map/all_gather | solution.py:230
  67.7 15.2 %all-gather.1 = f32[4,32,768]{2,1,0:T(8,128)S(1)} all-gather(f32[2,32,768]{2,1,0:T(8,128)S(1)} %fusion.1), channel_id=3, replica_groups={{0,4},{1,5},{2,6},{3,7},{8,12},{9,13},{10,14},{11,15},{20,24},{21,25},{..., dimensions={0}, use_global_device_ids=true | all-gather | bytes 589824 | tf_op jit(solution)/shard_map/all_gather | solution.py:230
  82.9 0.1 multiply_multiply_fusion.1
  83.0 13.3 %all-gather.2 = f32[4,32,768]{2,1,0:T(8,128)S(1)} all-gather(f32[2,32,768]{2,1,0:T(8,128)S(1)} %pad_maximum_fusion), channel_id=4, replica_groups={{0,12},{1,13},{2,14},{3,15},{4,8},{5,9},{6,10},{7,11},{20,16},{21,17},{..., dimensions={0}, use_global_device_ids=true | all-gather | bytes 589824 | tf_op jit(solution)/shard_map/all_gather | solution.py:238
  96.3 1.9 %collective-permute-start.7 = (f32[2,2,32,768]{3,2,1,0:T(8,128)S(1)}, f32[2,2,32,768]{3,2,1,0:T(8,128)S(1)}, u32[]{:S(2)}, u32[]{:S(2)}) collective-permute-start(f32[2,2,32,768]{3,2,1,0:T(8,128)S(1)} %bitcast.2), channel_id=1, source_target_pairs={{0,2},{1,3},{2,0},{3,1},{4,6},{5,7},{6,4},{7,5},{8,10},{9,11},{10,... | collective-permute-start | bytes 1179656 | tf_op jit(solution)/shard_map/ppermute | solution.py:239
  98.2 7.2 %collective-permute-start.6 = (f32[2,2,32,768]{3,2,1,0:T(8,128)S(1)}, f32[2,2,32,768]{3,2,1,0:T(8,128)S(1)}, u32[]{:S(2)}, u32[]{:S(2)}) collective-permute-start(f32[2,2,32,768]{3,2,1,0:T(8,128)S(1)} %bitcast.3), channel_id=1, source_target_pairs={{0,15},{1,2},{2,1},{3,4},{4,3},{5,6},{6,5},{7,8},{8,7},{9,10},{10,... | collective-permute-start | bytes 1179656 | tf_op jit(solution)/shard_map/ppermute | solution.py:239
  105.4 1.9 %collective-permute-start.5 = (f32[2,2,32,768]{3,2,1,0:T(8,128)S(1)}, f32[2,2,32,768]{3,2,1,0:T(8,128)S(1)}, u32[]{:S(2)}, u32[]{:S(2)}) collective-permute-start(f32[2,2,32,768]{3,2,1,0:T(8,128)S(1)} %bitcast.4), channel_id=1, source_target_pairs={{0,1},{1,0},{2,3},{3,2},{4,5},{5,4},{6,7},{7,6},{8,9},{9,8},{10,11... | collective-permute-start | bytes 1179656 | tf_op jit(solution)/shard_map/ppermute | solution.py:239
  107.3 3.5 %collective-permute-done.7.refs_0_ = f32[2,2,32,768]{3,2,1,0:T(8,128)S(1)} collective-permute-done((f32[2,2,32,768]{3,2,1,0:T(8,128)S(1)}, f32[2,2,32,768]{3,2,1,0:T(8,128)S(1)}, u32[]{:S(2)}, u32[]{:S(2)}) %collective-permute-start.7) | collective-permute-done | bytes 393248 | tf_op jit(solution)/shard_map/ppermute | solution.py:239
  110.8 1.9 %shard_map.79 = (f32[8,32,384]{2,1,0:T(8,128)S(1)}, f32[384,384]{1,0:T(8,128)S(1)}, f32[384,384]{1,0:T(8,128)S(1)}, f32[384,384]{1,0:T(8,128)S(1)}, f32[384,384]{1,0:T(8,128)S(1)}) custom-call(f32[16,32,384]{2,1,0:T(8,128)S(1)} %all-to-all-done.refs_0_.gathered, bf16[2,384,768]{2,1,0:T(8,128)(2,1)S(1)} %get-tuple-element.35.refs_1_.w_in, ...), custom_call_target="tpu_custom_call" | custom-call | flops 1000 | bytes 1000 | tf_op jit(solution)/shard_map/pallas_call | solution.py:52
  112.7 2.5 %collective-permute-done.6.refs_1_ = f32[2,2,32,768]{3,2,1,0:T(8,128)S(1)} collective-permute-done((f32[2,2,32,768]{3,2,1,0:T(8,128)S(1)}, f32[2,2,32,768]{3,2,1,0:T(8,128)S(1)}, u32[]{:S(2)}, u32[]{:S(2)}) %collective-permute-start.6) | collective-permute-done | bytes 393248 | tf_op jit(solution)/shard_map/ppermute | solution.py:239
  115.2 0.0 collective-permute-done.5.refs_0_
  115.2 3.0 %shard_map.80 = (f32[16,32,384]{2,1,0:T(8,128)}, f32[384,384]{1,0:T(8,128)}, f32[384,384]{1,0:T(8,128)}, f32[384,384]{1,0:T(8,128)}, f32[384,384]{1,0:T(8,128)}) custom-call(f32[16,32,384]{2,1,0:T(8,128)S(1)} %all-to-all-done.refs_0_.gathered, bf16[2,384,768]{2,1,0:T(8,128)(2,1)S(1)} %get-tuple-element.35.refs_1_.w_in, ...), custom_call_target="tpu_custom_call" | custom-call | flops 1000 | bytes 1000 | tf_op jit(solution)/shard_map/pallas_call | solution.py:243
  118.2 0.0 copy-start.5
  118.2 9.8 %all-to-all-start.1 = ((f32[16,32,384]{2,1,0:T(8,128)}), f32[16,32,384]{2,1,0:T(8,128)S(1)}, u32[]{:S(2)}, u32[]{:S(2)}) async-start(f32[16,32,384]{2,1,0:T(8,128)} %get-tuple-element.47), calls=%async_computation.1 | async-start | bytes 1572864 | tf_op jit(solution)/shard_map/all_to_all | solution.py:256
  128.0 2.1 %collective-permute-start.8 = (f32[384,384]{1,0:T(8,128)}, f32[384,384]{1,0:T(8,128)S(1)}, u32[]{:S(2)}, u32[]{:S(2)}) collective-permute-start(f32[384,384]{1,0:T(8,128)} %get-tuple-element.51), channel_id=1, source_target_pairs={{0,16},{16,0},{32,48},{48,32},{64,80},{80,64},{96,112},{112,96},{1... | collective-permute-start | bytes 1769480 | tf_op jit(solution)/shard_map/ppermute | solution.py:258
  130.1 2.4 %collective-permute-start.9 = (f32[384,384]{1,0:T(8,128)}, f32[384,384]{1,0:T(8,128)S(1)}, u32[]{:S(2)}, u32[]{:S(2)}) collective-permute-start(f32[384,384]{1,0:T(8,128)} %get-tuple-element.53), channel_id=1, source_target_pairs={{0,16},{16,0},{32,48},{48,32},{64,80},{80,64},{96,112},{112,96},{1... | collective-permute-start | bytes 1769480 | tf_op jit(solution)/shard_map/ppermute | solution.py:257
  132.5 0.0 collective-permute-done.8
  132.5 0.0 copy-done.5
  132.5 0.9 add.26
  133.4 0.9 collective-permute-done.9
  134.3 0.0 copy-done.4
  134.3 0.9 add.27
  135.2 5.1 %all-to-all-done.1.parts = f32[16,32,384]{2,1,0:T(8,128)S(1)} async-done(((f32[16,32,384]{2,1,0:T(8,128)}), f32[16,32,384]{2,1,0:T(8,128)S(1)}, u32[]{:S(2)}, u32[]{:S(2)}) %all-to-all-start.1) | async-done | bytes 786464 | tf_op jit(solution)/shard_map/all_to_all | solution.py:256
  140.3 0.7 shard_map.81
  (6 shorter events, 0.1 us)
Async XLA Ops:
  1.4 9.6 %copy-start = (f32[384,384]{1,0:T(8,128)S(1)}, f32[384,384]{1,0:T(8,128)}, u32[]{:S(2)}) copy-start(f32[384,384]{1,0:T(8,128)} %w_in) | copy-start | bytes 1769476
  1.4 11.5 %copy-start.2 = (f32[384,384]{1,0:T(8,128)S(1)}, f32[384,384]{1,0:T(8,128)}, u32[]{:S(2)}) copy-start(f32[384,384]{1,0:T(8,128)} %w_out) | copy-start | bytes 1769476
  2.4 20.1 %all-to-all-start = ((f32[16,32,384]{2,1,0:T(8,128)}), f32[16,32,384]{2,1,0:T(8,128)S(1)}, u32[]{:S(2)}, u32[]{:S(2)}) async-start(f32[16,32,384]{2,1,0:T(8,128)} %broadcast_in_dim.2), calls=%async_computation | async-start | bytes 1572864 | tf_op jit(solution)/shard_map/all_to_all | solution.py:208
  11.0 4.4 %collective-permute-start = (f32[384,384]{1,0:T(8,128)S(1)}, f32[384,384]{1,0:T(8,128)S(1)}, u32[]{:S(2)}, u32[]{:S(2)}) collective-permute-start(f32[384,384]{1,0:T(8,128)S(1)} %copy-done), channel_id=1, source_target_pairs={{0,16},{16,0},{32,48},{48,32},{64,80},{80,64},{96,112},{112,96},{1... | collective-permute-start | bytes 1769480 | tf_op jit(solution)/shard_map/ppermute | solution.py:206
  12.9 4.0 %collective-permute-start.1 = (f32[384,384]{1,0:T(8,128)S(1)}, f32[384,384]{1,0:T(8,128)S(1)}, u32[]{:S(2)}, u32[]{:S(2)}) collective-permute-start(f32[384,384]{1,0:T(8,128)S(1)} %copy-done.2), channel_id=1, source_target_pairs={{0,16},{16,0},{32,48},{48,32},{64,80},{80,64},{96,112},{112,96},{1... | collective-permute-start | bytes 1769480 | tf_op jit(solution)/shard_map/ppermute | solution.py:207
  16.9 1.1 copy-start.1
  18.0 1.1 copy-start.3
  24.6 16.2 %collective-permute-start.2 = (f32[2,2,32,768]{3,2,1,0:T(8,128)}, f32[2,2,32,768]{3,2,1,0:T(8,128)S(1)}, u32[]{:S(2)}, u32[]{:S(2)}) collective-permute-start(f32[2,2,32,768]{3,2,1,0:T(8,128)} %get-tuple-element.37), channel_id=1, source_target_pairs={{0,1},{1,0},{2,3},{3,2},{4,5},{5,4},{6,7},{7,6},{8,9},{9,8},{10,11... | collective-permute-start | bytes 1179656 | tf_op jit(solution)/shard_map/ppermute | solution.py:218
  27.3 23.9 %collective-permute-start.3 = (f32[2,2,32,768]{3,2,1,0:T(8,128)}, f32[2,2,32,768]{3,2,1,0:T(8,128)}, u32[]{:S(2)}, u32[]{:S(2)}) collective-permute-start(f32[2,2,32,768]{3,2,1,0:T(8,128)} %get-tuple-element.38), channel_id=1, source_target_pairs={{0,15},{1,2},{2,1},{3,4},{4,3},{5,6},{6,5},{7,8},{8,7},{9,10},{10,... | collective-permute-start | bytes 1179656 | tf_op jit(solution)/shard_map/ppermute | solution.py:218
  37.9 14.0 %collective-permute-start.4 = (f32[2,2,32,768]{3,2,1,0:T(8,128)}, f32[2,2,32,768]{3,2,1,0:T(8,128)}, u32[]{:S(2)}, u32[]{:S(2)}) collective-permute-start(f32[2,2,32,768]{3,2,1,0:T(8,128)} %get-tuple-element.39), channel_id=1, source_target_pairs={{0,2},{1,3},{2,0},{3,1},{4,6},{5,7},{6,4},{7,5},{8,10},{9,11},{10,... | collective-permute-start | bytes 1179656 | tf_op jit(solution)/shard_map/ppermute | solution.py:218
  96.3 14.5 %collective-permute-start.7 = (f32[2,2,32,768]{3,2,1,0:T(8,128)S(1)}, f32[2,2,32,768]{3,2,1,0:T(8,128)S(1)}, u32[]{:S(2)}, u32[]{:S(2)}) collective-permute-start(f32[2,2,32,768]{3,2,1,0:T(8,128)S(1)} %bitcast.2), channel_id=1, source_target_pairs={{0,2},{1,3},{2,0},{3,1},{4,6},{5,7},{6,4},{7,5},{8,10},{9,11},{10,... | collective-permute-start | bytes 1179656 | tf_op jit(solution)/shard_map/ppermute | solution.py:239
  98.2 17.0 %collective-permute-start.6 = (f32[2,2,32,768]{3,2,1,0:T(8,128)S(1)}, f32[2,2,32,768]{3,2,1,0:T(8,128)S(1)}, u32[]{:S(2)}, u32[]{:S(2)}) collective-permute-start(f32[2,2,32,768]{3,2,1,0:T(8,128)S(1)} %bitcast.3), channel_id=1, source_target_pairs={{0,15},{1,2},{2,1},{3,4},{4,3},{5,6},{6,5},{7,8},{8,7},{9,10},{10,... | collective-permute-start | bytes 1179656 | tf_op jit(solution)/shard_map/ppermute | solution.py:239
  105.4 9.8 %collective-permute-start.5 = (f32[2,2,32,768]{3,2,1,0:T(8,128)S(1)}, f32[2,2,32,768]{3,2,1,0:T(8,128)S(1)}, u32[]{:S(2)}, u32[]{:S(2)}) collective-permute-start(f32[2,2,32,768]{3,2,1,0:T(8,128)S(1)} %bitcast.4), channel_id=1, source_target_pairs={{0,1},{1,0},{2,3},{3,2},{4,5},{5,4},{6,7},{7,6},{8,9},{9,8},{10,11... | collective-permute-start | bytes 1179656 | tf_op jit(solution)/shard_map/ppermute | solution.py:239
  118.2 14.3 %copy-start.5 = (f32[384,384]{1,0:T(8,128)S(1)}, f32[384,384]{1,0:T(8,128)}, u32[]{:S(2)}) copy-start(f32[384,384]{1,0:T(8,128)} %get-tuple-element.50) | copy-start | bytes 1769476
  118.2 22.1 %all-to-all-start.1 = ((f32[16,32,384]{2,1,0:T(8,128)}), f32[16,32,384]{2,1,0:T(8,128)S(1)}, u32[]{:S(2)}, u32[]{:S(2)}) async-start(f32[16,32,384]{2,1,0:T(8,128)} %get-tuple-element.47), calls=%async_computation.1 | async-start | bytes 1572864 | tf_op jit(solution)/shard_map/all_to_all | solution.py:256
  128.0 6.3 %copy-start.4 = (f32[384,384]{1,0:T(8,128)S(1)}, f32[384,384]{1,0:T(8,128)}, u32[]{:S(2)}) copy-start(f32[384,384]{1,0:T(8,128)} %get-tuple-element.52) | copy-start | bytes 1769476
  128.0 4.5 %collective-permute-start.8 = (f32[384,384]{1,0:T(8,128)}, f32[384,384]{1,0:T(8,128)S(1)}, u32[]{:S(2)}, u32[]{:S(2)}) collective-permute-start(f32[384,384]{1,0:T(8,128)} %get-tuple-element.51), channel_id=1, source_target_pairs={{0,16},{16,0},{32,48},{48,32},{64,80},{80,64},{96,112},{112,96},{1... | collective-permute-start | bytes 1769480 | tf_op jit(solution)/shard_map/ppermute | solution.py:258
  130.1 4.2 %collective-permute-start.9 = (f32[384,384]{1,0:T(8,128)}, f32[384,384]{1,0:T(8,128)S(1)}, u32[]{:S(2)}, u32[]{:S(2)}) collective-permute-start(f32[384,384]{1,0:T(8,128)} %get-tuple-element.53), channel_id=1, source_target_pairs={{0,16},{16,0},{32,48},{48,32},{64,80},{80,64},{96,112},{112,96},{1... | collective-permute-start | bytes 1769480 | tf_op jit(solution)/shard_map/ppermute | solution.py:257

commit v5 on v4

--- a/solution.py
+++ b/solution.py
@@ -36,23 +36,15 @@
     return one(lh, rh) + (one(lh, rl) + one(ll, rh))
 
 
-def join_kernel(w_in, w_in_other, w_out, w_out_other, in_parts, out_parts):
-    size = w_in.shape[1]
-    for k, (v, w) in enumerate(((w_in, w_out), (w_in_other, w_out_other))):
-        at = slice(k * size, (k + 1) * size)
-        in_parts[0, :, at], in_parts[1, :, at] = split(v[...])
-        out_parts[0, at, :], out_parts[1, at, :] = split(w[...])
-
-
 PLAIN, RIGHT_T, LEFT_T = ((1,), (0,)), ((1,), (1,)), ((0,), (0,))
 
 
-def kernel_call(body, out_shapes, args, kept_as=jnp.float32):
-    out = [jax.ShapeDtypeStruct(shape, kept_as) for shape in out_shapes]
+def kernel_call(body, out_shapes, args, scalars=0, far=False):
+    out = [pltpu.HBM(shape, jnp.float32) if far else jax.ShapeDtypeStruct(shape, jnp.float32) for shape in out_shapes]
     return pl.pallas_call(
         body,
         out_shape=out,
-        in_specs=[VMEM] * len(args),
+        in_specs=[SMEM] * scalars + [VMEM] * (len(args) - scalars),
         out_specs=[VMEM] * len(out),
         compiler_params=pltpu.CompilerParams(vmem_limit_bytes=9 * 2**20),
         cost_estimate=pl.CostEstimate(flops=1000, bytes_accessed=1000, transcendentals=0),
@@ -64,32 +56,35 @@
     return gathered[first:last, which * n : (which + 1) * n, :].reshape((last - first) * n, d)
 
 
-def sums_kernel(first, gathered, w_in, w_out, *outs):
-    chips = gathered.shape[0] // 4
-    for which, (weight, dims) in enumerate(((w_in, PLAIN), (w_out, RIGHT_T))):
-        rows = split(token_rows(gathered, first * chips, (first + len(outs)) * chips, which))
-        term = three(rows, (weight[0], weight[1]), dims)
-        block = term.shape[0] // len(outs) // 2
-        for i, out in enumerate(outs):
-            for part in range(2):
-                start = (2 * i + part) * block
-                out[part, which] = term[start : start + block]
-
-
-def halves_kernel(keep, *refs):
-    terms, (kept, given) = refs[:-2], refs[-2:]
-    for out, half in ((kept, keep[0]), (given, 1 - keep[0])):
-        total = terms[0][half]
-        for term in terms[1:]:
-            total = total + term[half]
-        out[...] = total
+def sums_kernel(first, keeps, gathered, w_in, w_in_other, w_out, w_out_other, *outs):
+    count = len(outs) // 2
+    n, d = gathered.shape[1] // 2, gathered.shape[2]
+    half = gathered.shape[0] // 8
+    for which, (weights, dims) in enumerate((((w_in, w_in_other), PLAIN), ((w_out, w_out_other), RIGHT_T))):
+        rows = []
+        for i in range(first, first + count):
+            for part in (1 - keeps[i], keeps[i]):
+                chips = pl.ds((2 * i + part) * half, half)
+                rows.append(gathered[chips, which * n : (which + 1) * n, :].reshape(half * n, d))
+        rows = split(jnp.concatenate(rows, axis=0))
+        for k in range(2):
+            term = three(rows, split(weights[k][...]), dims)
+            for i, out in enumerate(outs):
+                out[which, :, k * d : (k + 1) * d] = term[i * half * n : (i + 1) * half * n]
+
+
+def add_kernel(*refs):
+    total = refs[0][...]
+    for ref in refs[1:-1]:
+        total = total + ref[...]
+    refs[-1][...] = total
 
 
 def hidden_rows(blocks, which):
     return jnp.concatenate([block[part, which] for block in blocks for part in range(2)], axis=0)
 
 
-def back_terms(first, count, gathered, w_in, w_out, blocks):
+def back_terms(first, count, gathered, weights, blocks):
     size = gathered.shape[2]
     quarter = gathered.shape[0] // 4
     begin, end = first * quarter, (first + count) * quarter
@@ -100,29 +95,33 @@
         yield three([v[:, at] for v in act], cotangent, LEFT_T)
         yield three(tokens, [v[:, at] for v in slope], LEFT_T)
     shape = (count * quarter, gathered.shape[1] // 2, size)
-    yield three(act, (w_out[0], w_out[1]), PLAIN).reshape(shape)
-    yield three(slope, (w_in[0], w_in[1]), RIGHT_T).reshape(shape)
-
-
-def early_kernel(gathered, w_in, w_out, *refs):
-    rows, *grads = refs[2:]
+    w_in, w_in_other, w_out, w_out_other = weights
+    for hidden, pair, dims in ((act, (w_out, w_out_other), PLAIN), (slope, (w_in, w_in_other), RIGHT_T)):
+        term = [
+            three([v[:, k * size : (k + 1) * size] for v in hidden], split(pair[k][...]), dims) for k in range(2)
+        ]
+        yield (term[0] + term[1]).reshape(shape)
+
+
+def early_kernel(gathered, *refs):
+    weights, blocks, (rows, *grads) = refs[:4], refs[4:6], refs[6:]
     n = rows.shape[1] // 2
-    for k, term in enumerate(back_terms(2, 2, gathered, w_in, w_out, refs[:2])):
+    for k, term in enumerate(back_terms(2, 2, gathered, weights, blocks)):
         if k < 4:
             grads[k][...] = term
         else:
             rows[:, (k - 4) * n : (k - 3) * n, :] = term
 
 
-def late_kernel(gathered, w_in, w_out, *refs):
-    blocks, (early_rows, *early), refs = refs[:2], refs[2:7], refs[7:]
+def late_kernel(gathered, *refs):
+    weights, blocks, (early_rows, *early), refs = refs[:4], refs[4:6], refs[6:11], refs[11:]
     parts, grads, rows, scratch, done = refs[0], refs[1:5], refs[5], refs[6], refs[7]
     n = rows.shape[1] // 2
     chips = rows.shape[0] // 2
     copies = [pltpu.make_async_copy(scratch.at[k], grads[k], done.at[k]) for k in range(4)]
     copies.append(pltpu.make_async_copy(rows, parts, done.at[4]))
     rows[chips:] = early_rows[...]
-    for k, term in enumerate(back_terms(0, 2, gathered, w_in, w_out, blocks)):
+    for k, term in enumerate(back_terms(0, 2, gathered, weights, blocks)):
         if k < 4:
             scratch[k] = term + early[k][...]
             copies[k].start()
@@ -147,7 +146,7 @@
         return row * self.cols + col
 
     def steps(self, core, col):
-        near = 1 if (col + core) % 2 == 0 else -1
+        near = 1 if col % 2 == 0 else -1
         far = 2 if (col // 2 + core) % 2 == 0 else -2
         return near, -near, far
 
@@ -206,31 +205,34 @@
         weight_in_other = lax.ppermute(weight_in, "row", core_perm)
         weight_out_other = lax.ppermute(weight_out, "row", core_perm)
         gathered = lax.all_to_all(sent, BOTH, 0, 0, tiled=True, axis_index_groups=planes)
-        weights = kernel_call(
-            join_kernel,
-            [(2, d, 2 * h), (2, 2 * h, d)],
-            (weight_in, weight_in_other, weight_out, weight_out_other),
-            kept_as=jnp.bfloat16,
-        )
-        gathered, *weights = lax.optimization_barrier((gathered, *weights))
-
-        away = kernel_call(lambda *refs: sums_kernel(0, *refs), [block] * 3, (gathered, *weights))
-        away = [lax.ppermute(value, BOTH, perm) for value, perm in zip(away, swaps)]
-        own = kernel_call(lambda *refs: sums_kernel(3, *refs), [block], (gathered, *weights))[0]
-        kept, given = pl.pallas_call(
-            halves_kernel,
-            out_shape=[jax.ShapeDtypeStruct(block[1:], jnp.float32)] * 2,
-            in_specs=[SMEM] + [VMEM] * 4,
-            out_specs=[VMEM] * 2,
-            compiler_params=pltpu.CompilerParams(vmem_limit_bytes=9 * 2**20),
-            cost_estimate=pl.CostEstimate(flops=1000, bytes_accessed=1000, transcendentals=0),
-        )(keep.astype(jnp.int32).reshape(1), own, *away)
+        weights = (weight_in, weight_in_other, weight_out, weight_out_other)
+
+        col, core = lax.axis_index("col"), lax.axis_index("row") & 1
+        near = 1 - 2 * (col & 1)
+        far = 2 - 4 * (((col >> 1) + core) & 1)
+        keeps = jnp.stack([((((col + step) & (cols - 1)) >> 2) - core & 3) >> 1 for step in (near, -near, far, 0)])
+        keeps = keeps.astype(jnp.int32)
+
+        def terms(first, count):
+            return kernel_call(
+                lambda *refs: sums_kernel(first, *refs),
+                [block[1:]] * (2 * count),
+                (keeps, gathered, *weights),
+                scalars=1,
+                far=count > 1,
+            )
+
+        away, own = terms(0, 3), terms(3, 1)
+        away_given = [lax.ppermute(value, BOTH, perm) for value, perm in zip(away[0::2], swaps)]
+        away_kept = [lax.ppermute(value, BOTH, perm) for value, perm in zip(away[1::2], swaps)]
+        given = kernel_call(add_kernel, [block[1:]], (own[0], *away_given))[0]
 
         def swap(value, groups, first):
             got = lax.all_gather(value, BOTH, axis=0, axis_index_groups=groups)
             return jnp.where(first == 0, got[1], got[0])
 
-        kept = kept + swap(given, across, keep)
+        got = swap(given, across, keep)
+        kept = kernel_call(add_kernel, [block[1:]], (own[1], *away_kept, got))[0]
         kept = kept + swap(kept, mates, at & 1)
 
         pre, grad = kept[0], kept[1]
@@ -243,7 +245,7 @@
         parts, *grads = pl.pallas_call(
             late_kernel,
             out_shape=[pltpu.HBM(shape, jnp.float32) for shape in [(chips, 2 * n, d)] + square],
-            in_specs=[VMEM] * 10,
+            in_specs=[VMEM] * 12,
             out_specs=[FAR] * 5,
             scratch_shapes=[
                 pltpu.VMEM((chips, 2 * n, d), jnp.float32),

time: 142 us -> 141 us (level)
  waiting for transfers between devices: 27.7 us -> 12.7 us
  blocking collectives: 43 us -> 51.9 us
  starting transfers between devices: 53.4 us -> 58 us
  local copies, waits for them, and re-layouts: 3.11 us -> 1 us
    ppermute x3 -> x6, starting transfers between devices: 15.2 us -> 26.5 us  [local(): lax.ppermute(value, BOTH, perm)]
    ppermute x3 -> x6, waiting for transfers between devices: 11.2 us -> 0.02 us  [local(): lax.ppermute(value, BOTH, perm)]
    all_gather x2, blocking collectives: 29.7 us -> 39.9 us  [swap(): got = lax.all_gather(value, BOTH, axis=0, axis_index_groups=groups)]
    all_to_all x1, starting transfers between devices: 9.82 us -> 4.96 us  [local(): lax.all_to_all(parts, BOTH, 0, 0, tiled=True, axis_index_groups=planes)]
    all_to_all x1, waiting for transfers between devices: 5.09 us -> 2.09 us  [local(): lax.all_to_all(parts, BOTH, 0, 0, tiled=True, axis_index_groups=planes)]
    ppermute x3, waiting for transfers between devices: 5.99 us -> 3.66 us  [local(): blocks = [lax.ppermute(own, BOTH, perm) for perm in swaps] + [own]]
    unnamed x12, local copies, waits for them, and re-layouts: 2.14 us -> 0.03 us
    all_to_all x1, waiting for transfers between devices: 2.94 us -> 4.77 us  [local(): lax.all_to_all(sent, BOTH, 0, 0, tiled=True, axis_index_groups=planes)]
  transfers between devices with their start and end apart: 12 -> 15, of which waited for: 8 -> 7; matrix products, arithmetic and copies ran while one was open for 1% -> 1% of each run, Pallas kernels for 2% -> 3%
where the time goes in v5:
time: 141 us; the launch traced here: 139 us
  starting transfers between devices  58 us (41%)
  blocking collectives  51.9 us (37%)
  waiting for transfers between devices  12.7 us (9%)
  Pallas kernels  11.2 us (8%)
  other arithmetic  2.71 us (2%)
    all_gather x2, blocking collectives, swap(): got = lax.all_gather(value, BOTH, axis=0, axis_index_groups=groups)  39.9 us
    ppermute x6, starting transfers between devices, local(): lax.ppermute(value, BOTH, perm)  26.5 us
    all_gather x1, blocking collectives, local(): own = lax.all_gather(hidden, BOTH, axis=0, axis_index_groups=across)  12 us
    ppermute x3, starting transfers between devices, local(): blocks = [lax.ppermute(own, BOTH, perm) for perm in swaps] + [own]  9.2 us
    all_to_all x1, starting transfers between devices, local(): lax.all_to_all(sent, BOTH, 0, 0, tiled=True, axis_index_groups=planes)  8.73 us
    pallas_call x6, Pallas kernels, kernel_call(): pl.pallas_call(body, out_shape=out, in_specs=[SMEM] * scalars + [VMEM] *...  8.21 us
    all_to_all x1, starting transfers between devices, local(): lax.all_to_all(parts, BOTH, 0, 0, tiled=True, axis_index_groups=planes)  4.96 us
    all_to_all x1, waiting for transfers between devices, local(): lax.all_to_all(sent, BOTH, 0, 0, tiled=True, axis_index_groups=planes)  4.77 us
  transfers between devices with their start and end apart: 15, of which 7 were waited for; matrix products, arithmetic and copies ran while one was open for 1% of the time, Pallas kernels for 3%

profile of v5, /device:TPU:6, one launch (start us, length us, event | category | flops | bytes accessed | tf_op | source)
XLA Modules:
  0.0 138.6 jit_solution(7025356500884659028)
XLA Ops:
  0.6 0.8 pad_maximum_fusion.1
  1.4 1.0 broadcast_in_dim.2
  2.4 8.7 %all-to-all-start = ((f32[16,32,384]{2,1,0:T(8,128)}), f32[16,32,384]{2,1,0:T(8,128)S(1)}, u32[]{:S(2)}, u32[]{:S(2)}) async-start(f32[16,32,384]{2,1,0:T(8,128)} %broadcast_in_dim.2), calls=%async_computation | async-start | bytes 1572864 | tf_op jit(solution)/shard_map/all_to_all | solution.py:207
  11.1 0.0 copy-done
  11.1 1.9 %collective-permute-start = (f32[384,384]{1,0:T(8,128)S(1)}, f32[384,384]{1,0:T(8,128)S(1)}, u32[]{:S(2)}, u32[]{:S(2)}) collective-permute-start(f32[384,384]{1,0:T(8,128)S(1)} %copy-done), channel_id=1, source_target_pairs={{0,16},{16,0},{32,48},{48,32},{64,80},{80,64},{96,112},{112,96},{1... | collective-permute-start | bytes 1769480 | tf_op jit(solution)/shard_map/ppermute | solution.py:205
  13.0 0.0 copy-done.1
  13.1 2.4 %collective-permute-start.1 = (f32[384,384]{1,0:T(8,128)S(1)}, f32[384,384]{1,0:T(8,128)S(1)}, u32[]{:S(2)}, u32[]{:S(2)}) collective-permute-start(f32[384,384]{1,0:T(8,128)S(1)} %copy-done.1), channel_id=1, source_target_pairs={{0,16},{16,0},{32,48},{48,32},{64,80},{80,64},{96,112},{112,96},{1... | collective-permute-start | bytes 1769480 | tf_op jit(solution)/shard_map/ppermute | solution.py:206
  15.5 0.1 pad_add_fusion.refs_0_
  15.6 0.0 collective-permute-done.refs_3_.refs_1_
  15.6 1.5 %collective-permute-done.1.refs_5_.refs_3_ = f32[384,384]{1,0:T(8,128)S(1)} collective-permute-done((f32[384,384]{1,0:T(8,128)S(1)}, f32[384,384]{1,0:T(8,128)S(1)}, u32[]{:S(2)}, u32[]{:S(2)}) %collective-permute-start.1) | collective-permute-done | bytes 589856 | tf_op jit(solution)/shard_map/ppermute | solution.py:206
  17.1 4.8 %all-to-all-done.refs_1_.gathered = f32[16,32,384]{2,1,0:T(8,128)S(1)} async-done(((f32[16,32,384]{2,1,0:T(8,128)}), f32[16,32,384]{2,1,0:T(8,128)S(1)}, u32[]{:S(2)}, u32[]{:S(2)}) %all-to-all-start) | async-done | bytes 786464 | tf_op jit(solution)/shard_map/all_to_all | solution.py:207
  21.8 2.9 %shard_map.76 = (f32[2,32,768]{2,1,0:T(8,128)}, f32[2,32,768]{2,1,0:T(8,128)}, f32[2,32,768]{2,1,0:T(8,128)}, f32[2,32,768]{2,1,0:T(8,128)}, f32[2,32,768]{2,1,0:T(8,128)}, /*index=5*/f32[2,32,768]{2,1,0:T(8,128)}) custom-call(s32[4]{0:T(128)S(1)} %pad_add_fusion.refs_0_, f32[16,32,384]{2,1,0:T(8,128)S(1)} %all-to-all-done.refs_1_.gathered, ...), custom_call_target="tpu_custom_call" | custom-call | flops 1000 | bytes 1000 | tf_op jit(solution)/shard_map/pallas_call | solution.py:44
  24.7 4.4 %collective-permute-start.5 = (f32[2,32,768]{2,1,0:T(8,128)}, f32[2,32,768]{2,1,0:T(8,128)S(1)}, u32[]{:S(2)}, u32[]{:S(2)}) collective-permute-start(f32[2,32,768]{2,1,0:T(8,128)} %get-tuple-element.35), channel_id=1, source_target_pairs={{0,1},{1,0},{2,3},{3,2},{4,5},{5,4},{6,7},{7,6},{8,9},{9,8},{10,11... | collective-permute-start | bytes 589832 | tf_op jit(solution)/shard_map/ppermute | solution.py:226
  29.1 9.6 %collective-permute-start.6 = (f32[2,32,768]{2,1,0:T(8,128)}, f32[2,32,768]{2,1,0:T(8,128)S(1)}, u32[]{:S(2)}, u32[]{:S(2)}) collective-permute-start(f32[2,32,768]{2,1,0:T(8,128)} %get-tuple-element.36), channel_id=1, source_target_pairs={{0,15},{1,2},{2,1},{3,4},{4,3},{5,6},{6,5},{7,8},{8,7},{9,10},{10,... | collective-permute-start | bytes 589832 | tf_op jit(solution)/shard_map/ppermute | solution.py:226
  38.8 1.9 %collective-permute-start.7 = (f32[2,32,768]{2,1,0:T(8,128)}, f32[2,32,768]{2,1,0:T(8,128)}, u32[]{:S(2)}, u32[]{:S(2)}) collective-permute-start(f32[2,32,768]{2,1,0:T(8,128)} %get-tuple-element.37), channel_id=1, source_target_pairs={{0,2},{1,3},{2,0},{3,1},{4,6},{5,7},{6,4},{7,5},{8,10},{9,11},{10,... | collective-permute-start | bytes 589832 | tf_op jit(solution)/shard_map/ppermute | solution.py:226
  40.7 2.5 %collective-permute-start.2 = (f32[2,32,768]{2,1,0:T(8,128)}, f32[2,32,768]{2,1,0:T(8,128)S(1)}, u32[]{:S(2)}, u32[]{:S(2)}) collective-permute-start(f32[2,32,768]{2,1,0:T(8,128)} %get-tuple-element.31), channel_id=1, source_target_pairs={{0,1},{1,0},{2,3},{3,2},{4,5},{5,4},{6,7},{7,6},{8,9},{9,8},{10,11... | collective-permute-start | bytes 589832 | tf_op jit(solution)/shard_map/ppermute | solution.py:227
  43.2 6.1 %collective-permute-start.3 = (f32[2,32,768]{2,1,0:T(8,128)}, f32[2,32,768]{2,1,0:T(8,128)S(1)}, u32[]{:S(2)}, u32[]{:S(2)}) collective-permute-start(f32[2,32,768]{2,1,0:T(8,128)} %get-tuple-element.32), channel_id=1, source_target_pairs={{0,15},{1,2},{2,1},{3,4},{4,3},{5,6},{6,5},{7,8},{8,7},{9,10},{10,... | collective-permute-start | bytes 589832 | tf_op jit(solution)/shard_map/ppermute | solution.py:227
  49.4 1.6 %shard_map.75 = (f32[2,32,768]{2,1,0:T(8,128)S(1)}, f32[2,32,768]{2,1,0:T(8,128)S(1)}) custom-call(s32[4]{0:T(128)S(1)} %pad_add_fusion.refs_0_, f32[16,32,384]{2,1,0:T(8,128)S(1)} %all-to-all-done.refs_1_.gathered, f32[384,384]{1,0:T(8,128)S(1)} %copy-done, f32[384,384]{1,0:T(8,128)S(1)} %collective-permute-done.refs_3_.refs_1_, f32[384,384]{1,0:T(8,128)S(1)} %copy-done.1, ...), custom_call_target="tpu_custom_call" | custom-call | flops 1000 | bytes 1000 | tf_op jit(solution)/shard_map/pallas_call | solution.py:44
  50.9 0.0 collective-permute-done.5.refs_1_
  50.9 1.9 %collective-permute-start.4 = (f32[2,32,768]{2,1,0:T(8,128)S(1)}, f32[2,32,768]{2,1,0:T(8,128)S(1)}, u32[]{:S(2)}, u32[]{:S(2)}) collective-permute-start(f32[2,32,768]{2,1,0:T(8,128)S(1)} %copy-done.5), channel_id=1, source_target_pairs={{0,2},{1,3},{2,0},{3,1},{4,6},{5,7},{6,4},{7,5},{8,10},{9,11},{10,... | collective-permute-start | bytes 589832 | tf_op jit(solution)/shard_map/ppermute | solution.py:227
  52.9 0.0 collective-permute-done.6.refs_2_
  52.9 0.0 collective-permute-done.7.refs_3_
  52.9 1.0 shard_map.77
  53.9 15.5 %all-gather = f32[4,32,768]{2,1,0:T(8,128)S(1)} all-gather(f32[2,32,768]{2,1,0:T(8,128)S(1)} %shard_map.77), channel_id=2, replica_groups={{0,12},{1,13},{2,14},{3,15},{4,8},{5,9},{6,10},{7,11},{20,16},{21,17},{..., dimensions={0}, use_global_device_ids=true | all-gather | bytes 589824 | tf_op jit(solution)/shard_map/all_gather | solution.py:231
  69.4 0.0 collective-permute-done.2.refs_1_
  69.4 0.0 collective-permute-done.3.refs_2_
  69.4 0.0 collective-permute-done.4.refs_3_
  69.5 24.4 %all-gather.1 = f32[4,32,768]{2,1,0:T(8,128)S(1)} all-gather(f32[2,32,768]{2,1,0:T(8,128)S(1)} %shard_map.78), channel_id=3, replica_groups={{0,4},{1,5},{2,6},{3,7},{8,12},{9,13},{10,14},{11,15},{20,24},{21,25},{..., dimensions={0}, use_global_device_ids=true | all-gather | bytes 589824 | tf_op jit(solution)/shard_map/all_gather | solution.py:231
  93.9 0.1 multiply_multiply_fusion.1
  94.0 12.0 %all-gather.2 = f32[4,32,768]{2,1,0:T(8,128)S(1)} all-gather(f32[2,32,768]{2,1,0:T(8,128)S(1)} %pad_maximum_fusion), channel_id=4, replica_groups={{0,12},{1,13},{2,14},{3,15},{4,8},{5,9},{6,10},{7,11},{20,16},{21,17},{..., dimensions={0}, use_global_device_ids=true | all-gather | bytes 589824 | tf_op jit(solution)/shard_map/all_gather | solution.py:240
  106.1 1.9 %collective-permute-start.10 = (f32[2,2,32,768]{3,2,1,0:T(8,128)S(1)}, f32[2,2,32,768]{3,2,1,0:T(8,128)S(1)}, u32[]{:S(2)}, u32[]{:S(2)}) collective-permute-start(f32[2,2,32,768]{3,2,1,0:T(8,128)S(1)} %bitcast.5), channel_id=1, source_target_pairs={{0,2},{1,3},{2,0},{3,1},{4,6},{5,7},{6,4},{7,5},{8,10},{9,11},{10,... | collective-permute-start | bytes 1179656 | tf_op jit(solution)/shard_map/ppermute | solution.py:241
  108.0 1.9 %collective-permute-start.9 = (f32[2,2,32,768]{3,2,1,0:T(8,128)S(1)}, f32[2,2,32,768]{3,2,1,0:T(8,128)S(1)}, u32[]{:S(2)}, u32[]{:S(2)}) collective-permute-start(f32[2,2,32,768]{3,2,1,0:T(8,128)S(1)} %bitcast.6), channel_id=1, source_target_pairs={{0,15},{1,2},{2,1},{3,4},{4,3},{5,6},{6,5},{7,8},{8,7},{9,10},{10,... | collective-permute-start | bytes 1179656 | tf_op jit(solution)/shard_map/ppermute | solution.py:241
  109.9 5.4 %collective-permute-start.8 = (f32[2,2,32,768]{3,2,1,0:T(8,128)S(1)}, f32[2,2,32,768]{3,2,1,0:T(8,128)S(1)}, u32[]{:S(2)}, u32[]{:S(2)}) collective-permute-start(f32[2,2,32,768]{3,2,1,0:T(8,128)S(1)} %bitcast.7), channel_id=1, source_target_pairs={{0,1},{1,0},{2,3},{3,2},{4,5},{5,4},{6,7},{7,6},{8,9},{9,8},{10,11... | collective-permute-start | bytes 1179656 | tf_op jit(solution)/shard_map/ppermute | solution.py:241
  115.3 1.3 collective-permute-done.10.refs_4_
  116.6 2.1 %shard_map.79 = (f32[8,32,384]{2,1,0:T(8,128)S(1)}, f32[384,384]{1,0:T(8,128)S(1)}, f32[384,384]{1,0:T(8,128)S(1)}, f32[384,384]{1,0:T(8,128)S(1)}, f32[384,384]{1,0:T(8,128)S(1)}) custom-call(f32[16,32,384]{2,1,0:T(8,128)S(1)} %all-to-all-done.refs_1_.gathered, f32[384,384]{1,0:T(8,128)S(1)} %copy-done, ...), custom_call_target="tpu_custom_call" | custom-call | flops 1000 | bytes 1000 | tf_op jit(solution)/shard_map/pallas_call | solution.py:44
  118.7 0.2 collective-permute-done.9.refs_5_
  118.8 2.2 %collective-permute-done.8.refs_4_ = f32[2,2,32,768]{3,2,1,0:T(8,128)S(1)} collective-permute-done((f32[2,2,32,768]{3,2,1,0:T(8,128)S(1)}, f32[2,2,32,768]{3,2,1,0:T(8,128)S(1)}, u32[]{:S(2)}, u32[]{:S(2)}) %collective-permute-start.8) | collective-permute-done | bytes 393248 | tf_op jit(solution)/shard_map/ppermute | solution.py:241
  121.0 3.0 %shard_map.80 = (f32[16,32,384]{2,1,0:T(8,128)}, f32[384,384]{1,0:T(8,128)}, f32[384,384]{1,0:T(8,128)}, f32[384,384]{1,0:T(8,128)}, f32[384,384]{1,0:T(8,128)}) custom-call(f32[16,32,384]{2,1,0:T(8,128)S(1)} %all-to-all-done.refs_1_.gathered, f32[384,384]{1,0:T(8,128)S(1)} %copy-done, f32[384,384]{1,0:T(8,128)S(1)} %collective-permute-done.refs_3_.refs_1_, ...), custom_call_target="tpu_custom_call" | custom-call | flops 1000 | bytes 1000 | tf_op jit(solution)/shard_map/pallas_call | solution.py:245
  124.0 0.0 copy-start.4
  124.1 5.0 %all-to-all-start.1 = ((f32[16,32,384]{2,1,0:T(8,128)}), f32[16,32,384]{2,1,0:T(8,128)S(1)}, u32[]{:S(2)}, u32[]{:S(2)}) async-start(f32[16,32,384]{2,1,0:T(8,128)} %get-tuple-element.43), calls=%async_computation.1 | async-start | bytes 1572864 | tf_op jit(solution)/shard_map/all_to_all | solution.py:258
  129.0 1.9 %collective-permute-start.11 = (f32[384,384]{1,0:T(8,128)}, f32[384,384]{1,0:T(8,128)S(1)}, u32[]{:S(2)}, u32[]{:S(2)}) collective-permute-start(f32[384,384]{1,0:T(8,128)} %get-tuple-element.47), channel_id=1, source_target_pairs={{0,16},{16,0},{32,48},{48,32},{64,80},{80,64},{96,112},{112,96},{1... | collective-permute-start | bytes 1769480 | tf_op jit(solution)/shard_map/ppermute | solution.py:260
  131.0 2.4 %collective-permute-start.12 = (f32[384,384]{1,0:T(8,128)S(1)}, f32[384,384]{1,0:T(8,128)S(1)}, u32[]{:S(2)}, u32[]{:S(2)}) collective-permute-start(f32[384,384]{1,0:T(8,128)S(1)} %copy-done.4), channel_id=1, source_target_pairs={{0,16},{16,0},{32,48},{48,32},{64,80},{80,64},{96,112},{112,96},{1... | collective-permute-start | bytes 1769480 | tf_op jit(solution)/shard_map/ppermute | solution.py:259
  133.4 0.0 collective-permute-done.11
  133.4 0.9 add.38
  134.3 0.7 collective-permute-done.12
  135.0 0.9 add.39
  135.9 2.1 %all-to-all-done.1.parts = f32[16,32,384]{2,1,0:T(8,128)S(1)} async-done(((f32[16,32,384]{2,1,0:T(8,128)}), f32[16,32,384]{2,1,0:T(8,128)S(1)}, u32[]{:S(2)}, u32[]{:S(2)}) %all-to-all-start.1) | async-done | bytes 786464 | tf_op jit(solution)/shard_map/all_to_all | solution.py:258
  137.9 0.7 shard_map.81
  (13 shorter events, 0.1 us)
Async XLA Ops:
  2.4 8.7 %copy-start = (f32[384,384]{1,0:T(8,128)S(1)}, f32[384,384]{1,0:T(8,128)}, u32[]{:S(2)}) copy-start(f32[384,384]{1,0:T(8,128)} %refs_0_.1) | copy-start | bytes 1769476
  2.4 10.7 %copy-start.1 = (f32[384,384]{1,0:T(8,128)S(1)}, f32[384,384]{1,0:T(8,128)}, u32[]{:S(2)}) copy-start(f32[384,384]{1,0:T(8,128)} %refs_2_.3) | copy-start | bytes 1769476
  2.4 19.5 %all-to-all-start = ((f32[16,32,384]{2,1,0:T(8,128)}), f32[16,32,384]{2,1,0:T(8,128)S(1)}, u32[]{:S(2)}, u32[]{:S(2)}) async-start(f32[16,32,384]{2,1,0:T(8,128)} %broadcast_in_dim.2), calls=%async_computation | async-start | bytes 1572864 | tf_op jit(solution)/shard_map/all_to_all | solution.py:207
  11.1 4.5 %collective-permute-start = (f32[384,384]{1,0:T(8,128)S(1)}, f32[384,384]{1,0:T(8,128)S(1)}, u32[]{:S(2)}, u32[]{:S(2)}) collective-permute-start(f32[384,384]{1,0:T(8,128)S(1)} %copy-done), channel_id=1, source_target_pairs={{0,16},{16,0},{32,48},{48,32},{64,80},{80,64},{96,112},{112,96},{1... | collective-permute-start | bytes 1769480 | tf_op jit(solution)/shard_map/ppermute | solution.py:205
  13.1 4.0 %collective-permute-start.1 = (f32[384,384]{1,0:T(8,128)S(1)}, f32[384,384]{1,0:T(8,128)S(1)}, u32[]{:S(2)}, u32[]{:S(2)}) collective-permute-start(f32[384,384]{1,0:T(8,128)S(1)} %copy-done.1), channel_id=1, source_target_pairs={{0,16},{16,0},{32,48},{48,32},{64,80},{80,64},{96,112},{112,96},{1... | collective-permute-start | bytes 1769480 | tf_op jit(solution)/shard_map/ppermute | solution.py:206
  24.7 26.2 %collective-permute-start.5 = (f32[2,32,768]{2,1,0:T(8,128)}, f32[2,32,768]{2,1,0:T(8,128)S(1)}, u32[]{:S(2)}, u32[]{:S(2)}) collective-permute-start(f32[2,32,768]{2,1,0:T(8,128)} %get-tuple-element.35), channel_id=1, source_target_pairs={{0,1},{1,0},{2,3},{3,2},{4,5},{5,4},{6,7},{7,6},{8,9},{9,8},{10,11... | collective-permute-start | bytes 589832 | tf_op jit(solution)/shard_map/ppermute | solution.py:226
  29.1 23.7 %collective-permute-start.6 = (f32[2,32,768]{2,1,0:T(8,128)}, f32[2,32,768]{2,1,0:T(8,128)S(1)}, u32[]{:S(2)}, u32[]{:S(2)}) collective-permute-start(f32[2,32,768]{2,1,0:T(8,128)} %get-tuple-element.36), channel_id=1, source_target_pairs={{0,15},{1,2},{2,1},{3,4},{4,3},{5,6},{6,5},{7,8},{8,7},{9,10},{10,... | collective-permute-start | bytes 589832 | tf_op jit(solution)/shard_map/ppermute | solution.py:226
  38.8 14.1 %collective-permute-start.7 = (f32[2,32,768]{2,1,0:T(8,128)}, f32[2,32,768]{2,1,0:T(8,128)}, u32[]{:S(2)}, u32[]{:S(2)}) collective-permute-start(f32[2,32,768]{2,1,0:T(8,128)} %get-tuple-element.37), channel_id=1, source_target_pairs={{0,2},{1,3},{2,0},{3,1},{4,6},{5,7},{6,4},{7,5},{8,10},{9,11},{10,... | collective-permute-start | bytes 589832 | tf_op jit(solution)/shard_map/ppermute | solution.py:226
  40.7 28.7 %collective-permute-start.2 = (f32[2,32,768]{2,1,0:T(8,128)}, f32[2,32,768]{2,1,0:T(8,128)S(1)}, u32[]{:S(2)}, u32[]{:S(2)}) collective-permute-start(f32[2,32,768]{2,1,0:T(8,128)} %get-tuple-element.31), channel_id=1, source_target_pairs={{0,1},{1,0},{2,3},{3,2},{4,5},{5,4},{6,7},{7,6},{8,9},{9,8},{10,11... | collective-permute-start | bytes 589832 | tf_op jit(solution)/shard_map/ppermute | solution.py:227
  43.2 7.7 %copy-start.5 = (f32[2,32,768]{2,1,0:T(8,128)S(1)}, f32[2,32,768]{2,1,0:T(8,128)}, u32[]{:S(2)}) copy-start(f32[2,32,768]{2,1,0:T(8,128)} %get-tuple-element.33) | copy-start | bytes 589828
  43.2 26.2 %collective-permute-start.3 = (f32[2,32,768]{2,1,0:T(8,128)}, f32[2,32,768]{2,1,0:T(8,128)S(1)}, u32[]{:S(2)}, u32[]{:S(2)}) collective-permute-start(f32[2,32,768]{2,1,0:T(8,128)} %get-tuple-element.32), channel_id=1, source_target_pairs={{0,15},{1,2},{2,1},{3,4},{4,3},{5,6},{6,5},{7,8},{8,7},{9,10},{10,... | collective-permute-start | bytes 589832 | tf_op jit(solution)/shard_map/ppermute | solution.py:227
  50.9 18.5 %collective-permute-start.4 = (f32[2,32,768]{2,1,0:T(8,128)S(1)}, f32[2,32,768]{2,1,0:T(8,128)S(1)}, u32[]{:S(2)}, u32[]{:S(2)}) collective-permute-start(f32[2,32,768]{2,1,0:T(8,128)S(1)} %copy-done.5), channel_id=1, source_target_pairs={{0,2},{1,3},{2,0},{3,1},{4,6},{5,7},{6,4},{7,5},{8,10},{9,11},{10,... | collective-permute-start | bytes 589832 | tf_op jit(solution)/shard_map/ppermute | solution.py:227
  106.1 10.6 %collective-permute-start.10 = (f32[2,2,32,768]{3,2,1,0:T(8,128)S(1)}, f32[2,2,32,768]{3,2,1,0:T(8,128)S(1)}, u32[]{:S(2)}, u32[]{:S(2)}) collective-permute-start(f32[2,2,32,768]{3,2,1,0:T(8,128)S(1)} %bitcast.5), channel_id=1, source_target_pairs={{0,2},{1,3},{2,0},{3,1},{4,6},{5,7},{6,4},{7,5},{8,10},{9,11},{10,... | collective-permute-start | bytes 1179656 | tf_op jit(solution)/shard_map/ppermute | solution.py:241
  108.0 10.9 %collective-permute-start.9 = (f32[2,2,32,768]{3,2,1,0:T(8,128)S(1)}, f32[2,2,32,768]{3,2,1,0:T(8,128)S(1)}, u32[]{:S(2)}, u32[]{:S(2)}) collective-permute-start(f32[2,2,32,768]{3,2,1,0:T(8,128)S(1)} %bitcast.6), channel_id=1, source_target_pairs={{0,15},{1,2},{2,1},{3,4},{4,3},{5,6},{6,5},{7,8},{8,7},{9,10},{10,... | collective-permute-start | bytes 1179656 | tf_op jit(solution)/shard_map/ppermute | solution.py:241
  109.9 11.1 %collective-permute-start.8 = (f32[2,2,32,768]{3,2,1,0:T(8,128)S(1)}, f32[2,2,32,768]{3,2,1,0:T(8,128)S(1)}, u32[]{:S(2)}, u32[]{:S(2)}) collective-permute-start(f32[2,2,32,768]{3,2,1,0:T(8,128)S(1)} %bitcast.7), channel_id=1, source_target_pairs={{0,1},{1,0},{2,3},{3,2},{4,5},{5,4},{6,7},{7,6},{8,9},{9,8},{10,11... | collective-permute-start | bytes 1179656 | tf_op jit(solution)/shard_map/ppermute | solution.py:241
  124.0 6.9 %copy-start.4 = (f32[384,384]{1,0:T(8,128)S(1)}, f32[384,384]{1,0:T(8,128)}, u32[]{:S(2)}) copy-start(f32[384,384]{1,0:T(8,128)} %get-tuple-element.49) | copy-start | bytes 1769476
  124.1 9.3 %copy-start.3 = (f32[384,384]{1,0:T(8,128)S(1)}, f32[384,384]{1,0:T(8,128)}, u32[]{:S(2)}) copy-start(f32[384,384]{1,0:T(8,128)} %get-tuple-element.46) | copy-start | bytes 1769476
  124.1 13.9 %all-to-all-start.1 = ((f32[16,32,384]{2,1,0:T(8,128)}), f32[16,32,384]{2,1,0:T(8,128)S(1)}, u32[]{:S(2)}, u32[]{:S(2)}) async-start(f32[16,32,384]{2,1,0:T(8,128)} %get-tuple-element.43), calls=%async_computation.1 | async-start | bytes 1572864 | tf_op jit(solution)/shard_map/all_to_all | solution.py:258
  129.0 4.3 %collective-permute-start.11 = (f32[384,384]{1,0:T(8,128)}, f32[384,384]{1,0:T(8,128)S(1)}, u32[]{:S(2)}, u32[]{:S(2)}) collective-permute-start(f32[384,384]{1,0:T(8,128)} %get-tuple-element.47), channel_id=1, source_target_pairs={{0,16},{16,0},{32,48},{48,32},{64,80},{80,64},{96,112},{112,96},{1... | collective-permute-start | bytes 1769480 | tf_op jit(solution)/shard_map/ppermute | solution.py:260
  131.0 4.0 %collective-permute-start.12 = (f32[384,384]{1,0:T(8,128)S(1)}, f32[384,384]{1,0:T(8,128)S(1)}, u32[]{:S(2)}, u32[]{:S(2)}) collective-permute-start(f32[384,384]{1,0:T(8,128)S(1)} %copy-done.4), channel_id=1, source_target_pairs={{0,16},{16,0},{32,48},{48,32},{64,80},{80,64},{96,112},{112,96},{1... | collective-permute-start | bytes 1769480 | tf_op jit(solution)/shard_map/ppermute | solution.py:259
  133.4 1.6 %copy-start.2 = (f32[384,384]{1,0:T(8,128)S(1)}, f32[384,384]{1,0:T(8,128)}, u32[]{:S(2)}) copy-start(f32[384,384]{1,0:T(8,128)} %get-tuple-element.48) | copy-start | bytes 1769476

commit v6 on v5

--- a/solution.py
+++ b/solution.py
@@ -222,7 +222,8 @@
                 far=count > 1,
             )
 
-        away, own = terms(0, 3), terms(3, 1)
+        every = terms(0, 4)
+        away, own = every[:6], every[6:]
         away_given = [lax.ppermute(value, BOTH, perm) for value, perm in zip(away[0::2], swaps)]
         away_kept = [lax.ppermute(value, BOTH, perm) for value, perm in zip(away[1::2], swaps)]
         given = kernel_call(add_kernel, [block[1:]], (own[0], *away_given))[0]

time: 141 us -> 144 us (1.021)
  the two profiles are of different devices: /device:TPU:6 before, /device:TPU:64 now
where the time goes in v6:
time: 144 us; the launch traced here: 143 us
  starting transfers between devices  68.5 us (48%)
  blocking collectives  40.6 us (28%)
  waiting for transfers between devices  17.4 us (12%)
  Pallas kernels  9.99 us (7%)
  local copies, waits for them, and re-layouts  2.79 us (2%)
  other arithmetic  2.71 us (2%)
    all_gather x2, blocking collectives, swap(): got = lax.all_gather(value, BOTH, axis=0, axis_index_groups=groups)  28.9 us
    ppermute x6, starting transfers between devices, local(): lax.ppermute(value, BOTH, perm)  26.3 us
    ppermute x3, starting transfers between devices, local(): blocks = [lax.ppermute(own, BOTH, perm) for perm in swaps] + [own]  12.7 us
    all_to_all x1, starting transfers between devices, local(): lax.all_to_all(parts, BOTH, 0, 0, tiled=True, axis_index_groups=planes)  12.7 us
    all_gather x1, blocking collectives, local(): own = lax.all_gather(hidden, BOTH, axis=0, axis_index_groups=across)  11.7 us
    all_to_all x1, starting transfers between devices, local(): lax.all_to_all(sent, BOTH, 0, 0, tiled=True, axis_index_groups=planes)  8.22 us
    pallas_call x5, Pallas kernels, kernel_call(): pl.pallas_call(body, out_shape=out, in_specs=[SMEM] * scalars + [VMEM] *...  6.97 us
    all_to_all x1, waiting for transfers between devices, local(): lax.all_to_all(sent, BOTH, 0, 0, tiled=True, axis_index_groups=planes)  6.51 us
  transfers between devices with their start and end apart: 15, of which 5 were waited for; matrix products, arithmetic and copies ran while one was open for 1% of the time, Pallas kernels for 2%

profile of v6, /device:TPU:64, one launch (start us, length us, event | category | flops | bytes accessed | tf_op | source)
XLA Modules:
  0.0 143.0 jit_solution(15259238432811735288)
XLA Ops:
  0.6 0.8 pad_maximum_fusion.1
  1.4 1.0 broadcast_in_dim.2
  2.4 8.2 %all-to-all-start = ((f32[16,32,384]{2,1,0:T(8,128)}), f32[16,32,384]{2,1,0:T(8,128)S(1)}, u32[]{:S(2)}, u32[]{:S(2)}) async-start(f32[16,32,384]{2,1,0:T(8,128)} %broadcast_in_dim.2), calls=%async_computation | async-start | bytes 1572864 | tf_op jit(solution)/shard_map/all_to_all | solution.py:207
  10.6 0.0 copy-done
  10.6 1.9 %collective-permute-start = (f32[384,384]{1,0:T(8,128)S(1)}, f32[384,384]{1,0:T(8,128)S(1)}, u32[]{:S(2)}, u32[]{:S(2)}) collective-permute-start(f32[384,384]{1,0:T(8,128)S(1)} %copy-done), channel_id=1, source_target_pairs={{0,16},{16,0},{32,48},{48,32},{64,80},{80,64},{96,112},{112,96},{1... | collective-permute-start | bytes 1769480 | tf_op jit(solution)/shard_map/ppermute | solution.py:205
  12.5 2.4 %collective-permute-start.1 = (f32[384,384]{1,0:T(8,128)S(1)}, f32[384,384]{1,0:T(8,128)S(1)}, u32[]{:S(2)}, u32[]{:S(2)}) collective-permute-start(f32[384,384]{1,0:T(8,128)S(1)} %copy-done.1), channel_id=1, source_target_pairs={{0,16},{16,0},{32,48},{48,32},{64,80},{80,64},{96,112},{112,96},{1... | collective-permute-start | bytes 1769480 | tf_op jit(solution)/shard_map/ppermute | solution.py:206
  15.0 0.1 pad_add_fusion.refs_0_
  15.1 0.0 collective-permute-done.refs_3_.refs_1_
  15.1 1.5 %collective-permute-done.1.refs_5_.refs_3_ = f32[384,384]{1,0:T(8,128)S(1)} collective-permute-done((f32[384,384]{1,0:T(8,128)S(1)}, f32[384,384]{1,0:T(8,128)S(1)}, u32[]{:S(2)}, u32[]{:S(2)}) %collective-permute-start.1) | collective-permute-done | bytes 589856 | tf_op jit(solution)/shard_map/ppermute | solution.py:206
  16.6 6.5 %all-to-all-done.refs_1_.gathered = f32[16,32,384]{2,1,0:T(8,128)S(1)} async-done(((f32[16,32,384]{2,1,0:T(8,128)}), f32[16,32,384]{2,1,0:T(8,128)S(1)}, u32[]{:S(2)}, u32[]{:S(2)}) %all-to-all-start) | async-done | bytes 786464 | tf_op jit(solution)/shard_map/all_to_all | solution.py:207
  23.1 3.2 %shard_map.75 = (f32[2,32,768]{2,1,0:T(8,128)}, f32[2,32,768]{2,1,0:T(8,128)}, f32[2,32,768]{2,1,0:T(8,128)}, f32[2,32,768]{2,1,0:T(8,128)}, f32[2,32,768]{2,1,0...) custom-call(s32[4]{0:T(128)S(1)} %pad_add_fusion.refs_0_, ...), custom_call_target="tpu_custom_call" | custom-call | flops 1000 | bytes 1000 | tf_op jit(solution)/shard_map/pallas_call | solution.py:44
  26.3 3.2 %collective-permute-start.5 = (f32[2,32,768]{2,1,0:T(8,128)}, f32[2,32,768]{2,1,0:T(8,128)S(1)}, u32[]{:S(2)}, u32[]{:S(2)}) collective-permute-start(f32[2,32,768]{2,1,0:T(8,128)} %get-tuple-element.35), channel_id=1, source_target_pairs={{0,1},{1,0},{2,3},{3,2},{4,5},{5,4},{6,7},{7,6},{8,9},{9,8},{10,11... | collective-permute-start | bytes 589832 | tf_op jit(solution)/shard_map/ppermute | solution.py:227
  29.5 1.9 %collective-permute-start.6 = (f32[2,32,768]{2,1,0:T(8,128)}, f32[2,32,768]{2,1,0:T(8,128)S(1)}, u32[]{:S(2)}, u32[]{:S(2)}) collective-permute-start(f32[2,32,768]{2,1,0:T(8,128)} %get-tuple-element.36), channel_id=1, source_target_pairs={{0,15},{1,2},{2,1},{3,4},{4,3},{5,6},{6,5},{7,8},{8,7},{9,10},{10,... | collective-permute-start | bytes 589832 | tf_op jit(solution)/shard_map/ppermute | solution.py:227
  31.4 10.8 %collective-permute-start.7 = (f32[2,32,768]{2,1,0:T(8,128)}, f32[2,32,768]{2,1,0:T(8,128)}, u32[]{:S(2)}, u32[]{:S(2)}) collective-permute-start(f32[2,32,768]{2,1,0:T(8,128)} %get-tuple-element.37), channel_id=1, source_target_pairs={{0,2},{1,3},{2,0},{3,1},{4,6},{5,7},{6,4},{7,5},{8,10},{9,11},{10,... | collective-permute-start | bytes 589832 | tf_op jit(solution)/shard_map/ppermute | solution.py:227
  42.2 1.9 %collective-permute-start.2 = (f32[2,32,768]{2,1,0:T(8,128)}, f32[2,32,768]{2,1,0:T(8,128)S(1)}, u32[]{:S(2)}, u32[]{:S(2)}) collective-permute-start(f32[2,32,768]{2,1,0:T(8,128)} %get-tuple-element.31), channel_id=1, source_target_pairs={{0,1},{1,0},{2,3},{3,2},{4,5},{5,4},{6,7},{7,6},{8,9},{9,8},{10,11... | collective-permute-start | bytes 589832 | tf_op jit(solution)/shard_map/ppermute | solution.py:228
  44.1 2.5 %collective-permute-start.3 = (f32[2,32,768]{2,1,0:T(8,128)}, f32[2,32,768]{2,1,0:T(8,128)S(1)}, u32[]{:S(2)}, u32[]{:S(2)}) collective-permute-start(f32[2,32,768]{2,1,0:T(8,128)} %get-tuple-element.32), channel_id=1, source_target_pairs={{0,15},{1,2},{2,1},{3,4},{4,3},{5,6},{6,5},{7,8},{8,7},{9,10},{10,... | collective-permute-start | bytes 589832 | tf_op jit(solution)/shard_map/ppermute | solution.py:228
  46.6 0.0 collective-permute-done.5.refs_1_
  46.6 6.0 %collective-permute-start.4 = (f32[2,32,768]{2,1,0:T(8,128)}, f32[2,32,768]{2,1,0:T(8,128)S(1)}, u32[]{:S(2)}, u32[]{:S(2)}) collective-permute-start(f32[2,32,768]{2,1,0:T(8,128)} %get-tuple-element.33), channel_id=1, source_target_pairs={{0,2},{1,3},{2,0},{3,1},{4,6},{5,7},{6,4},{7,5},{8,10},{9,11},{10,... | collective-permute-start | bytes 589832 | tf_op jit(solution)/shard_map/ppermute | solution.py:228
  52.6 0.0 collective-permute-done.6.refs_2_
  52.7 0.0 collective-permute-done.7.refs_3_
  52.7 0.9 copy-done.3
  53.6 1.0 shard_map.76
  54.6 15.4 %all-gather = f32[4,32,768]{2,1,0:T(8,128)S(1)} all-gather(f32[2,32,768]{2,1,0:T(8,128)S(1)} %shard_map.76), channel_id=2, replica_groups={{0,12},{1,13},{2,14},{3,15},{4,8},{5,9},{6,10},{7,11},{20,16},{21,17},{..., dimensions={0}, use_global_device_ids=true | all-gather | bytes 589824 | tf_op jit(solution)/shard_map/all_gather | solution.py:232
  69.9 0.0 collective-permute-done.2.refs_1_
  70.0 0.0 collective-permute-done.3.refs_2_
  70.0 0.0 collective-permute-done.4.refs_3_
  70.0 0.9 copy-done.2
  70.9 13.5 %all-gather.1 = f32[4,32,768]{2,1,0:T(8,128)S(1)} all-gather(f32[2,32,768]{2,1,0:T(8,128)S(1)} %shard_map.77), channel_id=3, replica_groups={{0,4},{1,5},{2,6},{3,7},{8,12},{9,13},{10,14},{11,15},{20,24},{21,25},{..., dimensions={0}, use_global_device_ids=true | all-gather | bytes 589824 | tf_op jit(solution)/shard_map/all_gather | solution.py:232
  84.4 0.1 multiply_multiply_fusion.1
  84.5 11.7 %all-gather.2 = f32[4,32,768]{2,1,0:T(8,128)S(1)} all-gather(f32[2,32,768]{2,1,0:T(8,128)S(1)} %pad_maximum_fusion), channel_id=4, replica_groups={{0,12},{1,13},{2,14},{3,15},{4,8},{5,9},{6,10},{7,11},{20,16},{21,17},{..., dimensions={0}, use_global_device_ids=true | all-gather | bytes 589824 | tf_op jit(solution)/shard_map/all_gather | solution.py:241
  96.3 7.3 %collective-permute-start.10 = (f32[2,2,32,768]{3,2,1,0:T(8,128)S(1)}, f32[2,2,32,768]{3,2,1,0:T(8,128)S(1)}, u32[]{:S(2)}, u32[]{:S(2)}) collective-permute-start(f32[2,2,32,768]{3,2,1,0:T(8,128)S(1)} %bitcast.5), channel_id=1, source_target_pairs={{0,2},{1,3},{2,0},{3,1},{4,6},{5,7},{6,4},{7,5},{8,10},{9,11},{10,... | collective-permute-start | bytes 1179656 | tf_op jit(solution)/shard_map/ppermute | solution.py:242
  103.5 1.9 %collective-permute-start.9 = (f32[2,2,32,768]{3,2,1,0:T(8,128)S(1)}, f32[2,2,32,768]{3,2,1,0:T(8,128)S(1)}, u32[]{:S(2)}, u32[]{:S(2)}) collective-permute-start(f32[2,2,32,768]{3,2,1,0:T(8,128)S(1)} %bitcast.6), channel_id=1, source_target_pairs={{0,15},{1,2},{2,1},{3,4},{4,3},{5,6},{6,5},{7,8},{8,7},{9,10},{10,... | collective-permute-start | bytes 1179656 | tf_op jit(solution)/shard_map/ppermute | solution.py:242
  105.5 3.6 %collective-permute-start.8 = (f32[2,2,32,768]{3,2,1,0:T(8,128)S(1)}, f32[2,2,32,768]{3,2,1,0:T(8,128)S(1)}, u32[]{:S(2)}, u32[]{:S(2)}) collective-permute-start(f32[2,2,32,768]{3,2,1,0:T(8,128)S(1)} %bitcast.7), channel_id=1, source_target_pairs={{0,1},{1,0},{2,3},{3,2},{4,5},{5,4},{6,7},{7,6},{8,9},{9,8},{10,11... | collective-permute-start | bytes 1179656 | tf_op jit(solution)/shard_map/ppermute | solution.py:242
  109.0 5.8 %collective-permute-done.10.refs_4_ = f32[2,2,32,768]{3,2,1,0:T(8,128)S(1)} collective-permute-done((f32[2,2,32,768]{3,2,1,0:T(8,128)S(1)}, f32[2,2,32,768]{3,2,1,0:T(8,128)S(1)}, u32[]{:S(2)}, u32[]{:S(2)}) %collective-permute-start.10) | collective-permute-done | bytes 393248 | tf_op jit(solution)/shard_map/ppermute | solution.py:242
  114.9 2.1 %shard_map.78 = (f32[8,32,384]{2,1,0:T(8,128)S(1)}, f32[384,384]{1,0:T(8,128)S(1)}, f32[384,384]{1,0:T(8,128)S(1)}, f32[384,384]{1,0:T(8,128)S(1)}, f32[384,384]{1,0:T(8,128)S(1)}) custom-call(f32[16,32,384]{2,1,0:T(8,128)S(1)} %all-to-all-done.refs_1_.gathered, f32[384,384]{1,0:T(8,128)S(1)} %copy-done, ...), custom_call_target="tpu_custom_call" | custom-call | flops 1000 | bytes 1000 | tf_op jit(solution)/shard_map/pallas_call | solution.py:44
  116.9 0.0 collective-permute-done.9.refs_5_
  117.0 0.0 collective-permute-done.8.refs_4_
  117.0 3.0 %shard_map.79 = (f32[16,32,384]{2,1,0:T(8,128)}, f32[384,384]{1,0:T(8,128)}, f32[384,384]{1,0:T(8,128)}, f32[384,384]{1,0:T(8,128)}, f32[384,384]{1,0:T(8,128)}) custom-call(f32[16,32,384]{2,1,0:T(8,128)S(1)} %all-to-all-done.refs_1_.gathered, f32[384,384]{1,0:T(8,128)S(1)} %copy-done, f32[384,384]{1,0:T(8,128)S(1)} %collective-permute-done.refs_3_.refs_1_, ...), custom_call_target="tpu_custom_call" | custom-call | flops 1000 | bytes 1000 | tf_op jit(solution)/shard_map/pallas_call | solution.py:246
  120.0 0.0 copy-start.6
  120.0 12.7 %all-to-all-start.1 = ((f32[16,32,384]{2,1,0:T(8,128)}), f32[16,32,384]{2,1,0:T(8,128)S(1)}, u32[]{:S(2)}, u32[]{:S(2)}) async-start(f32[16,32,384]{2,1,0:T(8,128)} %get-tuple-element.43), calls=%async_computation.1 | async-start | bytes 1572864 | tf_op jit(solution)/shard_map/all_to_all | solution.py:259
  132.7 1.9 %collective-permute-start.11 = (f32[384,384]{1,0:T(8,128)S(1)}, f32[384,384]{1,0:T(8,128)S(1)}, u32[]{:S(2)}, u32[]{:S(2)}) collective-permute-start(f32[384,384]{1,0:T(8,128)S(1)} %copy-done.6), channel_id=1, source_target_pairs={{0,16},{16,0},{32,48},{48,32},{64,80},{80,64},{96,112},{112,96},{1... | collective-permute-start | bytes 1769480 | tf_op jit(solution)/shard_map/ppermute | solution.py:261
  134.6 2.4 %collective-permute-start.12 = (f32[384,384]{1,0:T(8,128)}, f32[384,384]{1,0:T(8,128)S(1)}, u32[]{:S(2)}, u32[]{:S(2)}) collective-permute-start(f32[384,384]{1,0:T(8,128)} %get-tuple-element.49), channel_id=1, source_target_pairs={{0,16},{16,0},{32,48},{48,32},{64,80},{80,64},{96,112},{112,96},{1... | collective-permute-start | bytes 1769480 | tf_op jit(solution)/shard_map/ppermute | solution.py:260
  137.0 0.0 collective-permute-done.11
  137.1 0.9 add.38
  137.9 0.9 collective-permute-done.12
  138.8 0.9 add.39
  139.7 2.7 %all-to-all-done.1.parts = f32[16,32,384]{2,1,0:T(8,128)S(1)} async-done(((f32[16,32,384]{2,1,0:T(8,128)}), f32[16,32,384]{2,1,0:T(8,128)S(1)}, u32[]{:S(2)}, u32[]{:S(2)}) %all-to-all-start.1) | async-done | bytes 786464 | tf_op jit(solution)/shard_map/all_to_all | solution.py:259
  142.4 0.7 shard_map.80
  (14 shorter events, 0.1 us)
Async XLA Ops:
  2.4 8.2 %copy-start = (f32[384,384]{1,0:T(8,128)S(1)}, f32[384,384]{1,0:T(8,128)}, u32[]{:S(2)}) copy-start(f32[384,384]{1,0:T(8,128)} %refs_0_.1) | copy-start | bytes 1769476
  2.4 10.2 %copy-start.1 = (f32[384,384]{1,0:T(8,128)S(1)}, f32[384,384]{1,0:T(8,128)}, u32[]{:S(2)}) copy-start(f32[384,384]{1,0:T(8,128)} %refs_2_.2) | copy-start | bytes 1769476
  2.4 20.7 %all-to-all-start = ((f32[16,32,384]{2,1,0:T(8,128)}), f32[16,32,384]{2,1,0:T(8,128)S(1)}, u32[]{:S(2)}, u32[]{:S(2)}) async-start(f32[16,32,384]{2,1,0:T(8,128)} %broadcast_in_dim.2), calls=%async_computation | async-start | bytes 1572864 | tf_op jit(solution)/shard_map/all_to_all | solution.py:207
  10.6 4.5 %collective-permute-start = (f32[384,384]{1,0:T(8,128)S(1)}, f32[384,384]{1,0:T(8,128)S(1)}, u32[]{:S(2)}, u32[]{:S(2)}) collective-permute-start(f32[384,384]{1,0:T(8,128)S(1)} %copy-done), channel_id=1, source_target_pairs={{0,16},{16,0},{32,48},{48,32},{64,80},{80,64},{96,112},{112,96},{1... | collective-permute-start | bytes 1769480 | tf_op jit(solution)/shard_map/ppermute | solution.py:205
  12.5 4.0 %collective-permute-start.1 = (f32[384,384]{1,0:T(8,128)S(1)}, f32[384,384]{1,0:T(8,128)S(1)}, u32[]{:S(2)}, u32[]{:S(2)}) collective-permute-start(f32[384,384]{1,0:T(8,128)S(1)} %copy-done.1), channel_id=1, source_target_pairs={{0,16},{16,0},{32,48},{48,32},{64,80},{80,64},{96,112},{112,96},{1... | collective-permute-start | bytes 1769480 | tf_op jit(solution)/shard_map/ppermute | solution.py:206
  26.3 20.3 %collective-permute-start.5 = (f32[2,32,768]{2,1,0:T(8,128)}, f32[2,32,768]{2,1,0:T(8,128)S(1)}, u32[]{:S(2)}, u32[]{:S(2)}) collective-permute-start(f32[2,32,768]{2,1,0:T(8,128)} %get-tuple-element.35), channel_id=1, source_target_pairs={{0,1},{1,0},{2,3},{3,2},{4,5},{5,4},{6,7},{7,6},{8,9},{9,8},{10,11... | collective-permute-start | bytes 589832 | tf_op jit(solution)/shard_map/ppermute | solution.py:227
  29.5 23.2 %collective-permute-start.6 = (f32[2,32,768]{2,1,0:T(8,128)}, f32[2,32,768]{2,1,0:T(8,128)S(1)}, u32[]{:S(2)}, u32[]{:S(2)}) collective-permute-start(f32[2,32,768]{2,1,0:T(8,128)} %get-tuple-element.36), channel_id=1, source_target_pairs={{0,15},{1,2},{2,1},{3,4},{4,3},{5,6},{6,5},{7,8},{8,7},{9,10},{10,... | collective-permute-start | bytes 589832 | tf_op jit(solution)/shard_map/ppermute | solution.py:227
  31.4 21.2 %collective-permute-start.7 = (f32[2,32,768]{2,1,0:T(8,128)}, f32[2,32,768]{2,1,0:T(8,128)}, u32[]{:S(2)}, u32[]{:S(2)}) collective-permute-start(f32[2,32,768]{2,1,0:T(8,128)} %get-tuple-element.37), channel_id=1, source_target_pairs={{0,2},{1,3},{2,0},{3,1},{4,6},{5,7},{6,4},{7,5},{8,10},{9,11},{10,... | collective-permute-start | bytes 589832 | tf_op jit(solution)/shard_map/ppermute | solution.py:227
  42.2 27.7 %collective-permute-start.2 = (f32[2,32,768]{2,1,0:T(8,128)}, f32[2,32,768]{2,1,0:T(8,128)S(1)}, u32[]{:S(2)}, u32[]{:S(2)}) collective-permute-start(f32[2,32,768]{2,1,0:T(8,128)} %get-tuple-element.31), channel_id=1, source_target_pairs={{0,1},{1,0},{2,3},{3,2},{4,5},{5,4},{6,7},{7,6},{8,9},{9,8},{10,11... | collective-permute-start | bytes 589832 | tf_op jit(solution)/shard_map/ppermute | solution.py:228
  44.1 25.8 %collective-permute-start.3 = (f32[2,32,768]{2,1,0:T(8,128)}, f32[2,32,768]{2,1,0:T(8,128)S(1)}, u32[]{:S(2)}, u32[]{:S(2)}) collective-permute-start(f32[2,32,768]{2,1,0:T(8,128)} %get-tuple-element.32), channel_id=1, source_target_pairs={{0,15},{1,2},{2,1},{3,4},{4,3},{5,6},{6,5},{7,8},{8,7},{9,10},{10,... | collective-permute-start | bytes 589832 | tf_op jit(solution)/shard_map/ppermute | solution.py:228
  46.6 23.3 %collective-permute-start.4 = (f32[2,32,768]{2,1,0:T(8,128)}, f32[2,32,768]{2,1,0:T(8,128)S(1)}, u32[]{:S(2)}, u32[]{:S(2)}) collective-permute-start(f32[2,32,768]{2,1,0:T(8,128)} %get-tuple-element.33), channel_id=1, source_target_pairs={{0,2},{1,3},{2,0},{3,1},{4,6},{5,7},{6,4},{7,5},{8,10},{9,11},{10,... | collective-permute-start | bytes 589832 | tf_op jit(solution)/shard_map/ppermute | solution.py:228
  52.7 0.9 copy-start.3
  69.9 0.9 copy-start.2
  96.3 18.6 %collective-permute-start.10 = (f32[2,2,32,768]{3,2,1,0:T(8,128)S(1)}, f32[2,2,32,768]{3,2,1,0:T(8,128)S(1)}, u32[]{:S(2)}, u32[]{:S(2)}) collective-permute-start(f32[2,2,32,768]{3,2,1,0:T(8,128)S(1)} %bitcast.5), channel_id=1, source_target_pairs={{0,2},{1,3},{2,0},{3,1},{4,6},{5,7},{6,4},{7,5},{8,10},{9,11},{10,... | collective-permute-start | bytes 1179656 | tf_op jit(solution)/shard_map/ppermute | solution.py:242
  103.5 13.4 %collective-permute-start.9 = (f32[2,2,32,768]{3,2,1,0:T(8,128)S(1)}, f32[2,2,32,768]{3,2,1,0:T(8,128)S(1)}, u32[]{:S(2)}, u32[]{:S(2)}) collective-permute-start(f32[2,2,32,768]{3,2,1,0:T(8,128)S(1)} %bitcast.6), channel_id=1, source_target_pairs={{0,15},{1,2},{2,1},{3,4},{4,3},{5,6},{6,5},{7,8},{8,7},{9,10},{10,... | collective-permute-start | bytes 1179656 | tf_op jit(solution)/shard_map/ppermute | solution.py:242
  105.5 11.5 %collective-permute-start.8 = (f32[2,2,32,768]{3,2,1,0:T(8,128)S(1)}, f32[2,2,32,768]{3,2,1,0:T(8,128)S(1)}, u32[]{:S(2)}, u32[]{:S(2)}) collective-permute-start(f32[2,2,32,768]{3,2,1,0:T(8,128)S(1)} %bitcast.7), channel_id=1, source_target_pairs={{0,1},{1,0},{2,3},{3,2},{4,5},{5,4},{6,7},{7,6},{8,9},{9,8},{10,11... | collective-permute-start | bytes 1179656 | tf_op jit(solution)/shard_map/ppermute | solution.py:242
  120.0 12.7 %copy-start.6 = (f32[384,384]{1,0:T(8,128)S(1)}, f32[384,384]{1,0:T(8,128)}, u32[]{:S(2)}) copy-start(f32[384,384]{1,0:T(8,128)} %get-tuple-element.47) | copy-start | bytes 1769476
  120.0 17.0 %copy-start.5 = (f32[384,384]{1,0:T(8,128)S(1)}, f32[384,384]{1,0:T(8,128)}, u32[]{:S(2)}) copy-start(f32[384,384]{1,0:T(8,128)} %get-tuple-element.46) | copy-start | bytes 1769476
  120.0 22.4 %all-to-all-start.1 = ((f32[16,32,384]{2,1,0:T(8,128)}), f32[16,32,384]{2,1,0:T(8,128)S(1)}, u32[]{:S(2)}, u32[]{:S(2)}) async-start(f32[16,32,384]{2,1,0:T(8,128)} %get-tuple-element.43), calls=%async_computation.1 | async-start | bytes 1572864 | tf_op jit(solution)/shard_map/all_to_all | solution.py:259
  132.7 4.3 %collective-permute-start.11 = (f32[384,384]{1,0:T(8,128)S(1)}, f32[384,384]{1,0:T(8,128)S(1)}, u32[]{:S(2)}, u32[]{:S(2)}) collective-permute-start(f32[384,384]{1,0:T(8,128)S(1)} %copy-done.6), channel_id=1, source_target_pairs={{0,16},{16,0},{32,48},{48,32},{64,80},{80,64},{96,112},{112,96},{1... | collective-permute-start | bytes 1769480 | tf_op jit(solution)/shard_map/ppermute | solution.py:261
  134.6 4.2 %collective-permute-start.12 = (f32[384,384]{1,0:T(8,128)}, f32[384,384]{1,0:T(8,128)S(1)}, u32[]{:S(2)}, u32[]{:S(2)}) collective-permute-start(f32[384,384]{1,0:T(8,128)} %get-tuple-element.49), channel_id=1, source_target_pairs={{0,16},{16,0},{32,48},{48,32},{64,80},{80,64},{96,112},{112,96},{1... | collective-permute-start | bytes 1769480 | tf_op jit(solution)/shard_map/ppermute | solution.py:260
  137.0 1.8 %copy-start.4 = (f32[384,384]{1,0:T(8,128)S(1)}, f32[384,384]{1,0:T(8,128)}, u32[]{:S(2)}) copy-start(f32[384,384]{1,0:T(8,128)} %get-tuple-element.48) | copy-start | bytes 1769476
